TPU v7x, 32 devices: a whole 2x2x4 slice. The times are simulated.
32 devices in a mesh: rows: 4 (over y, x), cols: 8 (over z, core).
Axes of the slice: x: 2, y: 2, z: 4, core: 2. Of those that a mesh axis runs over, the one named last changes fastest.
Arguments:
- forget_grad: bfloat16 [4096, 4096], P('rows', 'cols'), may hold values from -6 to 6
- left_basis: bfloat16 [4096, 4096], P('rows', 'cols'), may hold values from -0.09375 to 0.09375
- right_basis: bfloat16 [4096, 4096], P('rows', 'cols'), may hold values from -0.09375 to 0.09375
- first_moment: float32 [4096, 4096], P('rows', 'cols'), may hold values from -6 to 6
- second_moment: float32 [4096, 4096], P('rows', 'cols'), may hold values from 0.05 to 2
Outputs:
- step_dir: bfloat16 [4096, 4096], P('rows', 'cols')
- new_first: float32 [4096, 4096], P('rows', 'cols')
- new_second: float32 [4096, 4096], P('rows', 'cols')
All inputs are finite; a program needn't handle non-finite values.
Results may differ from a plain program's by a relative error of at most 0.019.
Values may be sent and summed in bfloat16 or wider, within the bound.
No kernel may reach another device: no remote copies, remote signals or barrier semaphores. Data moves between devices by JAX's collectives and lax.ppermute only.
A program may use at most 64 MiB of HBM per device.

v0:
```python
import jax
import jax.numpy as jnp
from jax import lax
from jax.sharding import PartitionSpec as P

beta_first = 0.9
beta_second = 0.95
corr_first = 1.0 - 0.9**10
corr_second = 1.0 - 0.95**10
epsilon = 1e-08


def local(forget_grad, left_basis, right_basis, first_moment, second_moment):
    negated = -forget_grad
    right_cols = lax.all_gather(right_basis, "rows", axis=0, tiled=True)
    basis_part = right_cols
    half_rotated = jnp.dot(
        lax.all_gather(negated, "cols", axis=1, tiled=True),
        basis_part,
        preferred_element_type=jnp.float32,
    ).astype(jnp.bfloat16)
    half_rows = lax.all_gather(half_rotated, "cols", axis=1, tiled=True)
    rotated = lax.psum_scatter(
        lax.dot_general(
            half_rows, left_basis, (((0,), (0,)), ((), ())), preferred_element_type=jnp.float32
        ).astype(jnp.bfloat16),
        "rows",
        scatter_dimension=0,
        tiled=True,
    ).astype(jnp.float32)
    new_first = beta_first * first_moment + (1.0 - beta_first) * rotated
    new_second = beta_second * second_moment + (1.0 - beta_second) * rotated * rotated
    normalized = (new_first / corr_first / (jnp.sqrt(new_second / corr_second) + epsilon)).astype(
        jnp.bfloat16
    )
    right_rows = lax.all_gather(right_basis, "cols", axis=1, tiled=True)
    basis_part = right_rows
    back_half = jnp.dot(
        basis_part,
        lax.all_gather(normalized, "rows", axis=0, tiled=True),
        preferred_element_type=jnp.float32,
    ).astype(jnp.bfloat16)
    back_cols = lax.all_gather(back_half, "rows", axis=0, tiled=True)
    step_trans = lax.psum_scatter(
        lax.dot_general(
            back_cols, left_basis, (((1,), (1,)), ((), ())), preferred_element_type=jnp.float32
        ).astype(jnp.bfloat16),
        "cols",
        scatter_dimension=0,
        tiled=True,
    ).astype(jnp.float32)
    step_dir = step_trans.T.astype(jnp.bfloat16)
    return (step_dir, new_first, new_second)


def solution(mesh):
    return jax.shard_map(
        local,
        mesh=mesh,
        in_specs=(
            P("rows", "cols"),
            P("rows", "cols"),
            P("rows", "cols"),
            P("rows", "cols"),
            P("rows", "cols"),
        ),
        out_specs=(P("rows", "cols"), P("rows", "cols"), P("rows", "cols")),
        check_vma=False,
    )
```

profile of v0, /device:TPU:0, one launch (start us, length us, event | category | flops | bytes accessed | tf_op | source)
XLA Modules:
  0.0 609.8 jit_solution(16516503778416540090)
XLA Ops:
  7.2 0.0 copy-start
  7.2 0.0 all-gather.9.cloned.1.call-start
  7.2 0.7 all-gather.9.cloned.1.call-update
  7.9 0.0 all-gather.7.cloned.1.call-start
  8.0 2.4 neg.3
  10.3 0.0 all-gather.7.cloned.1.call-update
  10.4 0.0 all-gather.11.cloned.1.call-start
  10.4 54.9 %all-gather.9.cloned.1.call-done = bf16[4096,512]{1,0:T(8,128)(2,1)} async-done(((bf16[1024,512]{1,0:T(8,128)(2,1)}), bf16[4096,512]{1,0:T(8,128)(2,1)}) %all-gather.9.cloned.1.call-update) | async-done | bytes 4194320 | tf_op jit(solution)/shard_map/all_gather | solution.py:15
  65.3 84.3 %all-gather.7.cloned.1.call-done = bf16[1024,4096]{1,0:T(8,128)(2,1)} async-done(((bf16[1024,512]{1,0:T(8,128)(2,1)}), bf16[1024,4096]{1,0:T(8,128)(2,1)}) %all-gather.7.cloned.1.call-update) | async-done | bytes 8388624 | tf_op jit(solution)/shard_map/all_gather | solution.py:18
  149.6 10.0 %convolution_convert_fusion.3 = bf16[1024,512]{1,0:T(8,128)(2,1)} fusion(bf16[1024,4096]{1,0:T(8,128)(2,1)} %all-gather.7.cloned.1.call-done, bf16[4096,512]{1,0:T(8,128)(2,1)} %all-gather.9.cloned.1.call-done), kind=kOutput, calls=%fused_computation.8 | convolution fusion | flops 4295491584 | bytes 13631488 | tf_op jit(solution)/shard_map/dot_general | solution.py:17
  159.6 0.0 all-gather.11.cloned.1.call-update
  159.6 0.0 reduce-scatter.3.cloned.1.call-start
  159.7 80.7 %all-gather.11.cloned.1.call-done = bf16[1024,4096]{1,0:T(8,128)(2,1)} async-done(((bf16[1024,512]{1,0:T(8,128)(2,1)}), bf16[1024,4096]{1,0:T(8,128)(2,1)}) %all-gather.11.cloned.1.call-update) | async-done | bytes 8388624 | tf_op jit(solution)/shard_map/all_gather | solution.py:22
  240.4 0.0 copy-done
  240.4 9.7 %convolution_convert_fusion.1 = bf16[4096,512]{1,0:T(8,128)(2,1)} fusion(bf16[1024,4096]{1,0:T(8,128)(2,1)} %all-gather.11.cloned.1.call-done, bf16[1024,512]{1,0:T(8,128)(2,1)S(1)} %copy-done), kind=kOutput, calls=%fused_computation.1 | convolution fusion | flops 4297064448 | bytes 13631488 | tf_op jit(solution)/shard_map/dot_general | solution.py:24
  250.1 0.0 copy-start.1
  250.1 0.0 reduce-scatter.3.cloned.1.call-update
  250.1 0.0 all-gather.15.cloned.1.call-start
  250.2 0.5 all-gather.15.cloned.1.call-update
  250.7 0.0 all-gather.13.cloned.1.call-start
  250.7 50.7 %reduce-scatter.3.cloned.1.call-done = bf16[1024,512]{1,0:T(8,128)(2,1)} async-done(((bf16[4096,512]{1,0:T(8,128)(2,1)}), bf16[1024,512]{1,0:T(8,128)(2,1)}) %reduce-scatter.3.cloned.1.call-update) | async-done | bytes 1048592 | tf_op jit(solution)/shard_map/reduce_scatter | solution.py:23
  301.5 0.0 copy-done.1
  301.5 5.3 divide_convert_fusion
  306.8 0.0 all-gather.13.cloned.1.call-update
  306.8 0.2 all-gather.17.cloned.1.call-start
  307.0 78.1 %all-gather.15.cloned.1.call-done = bf16[1024,4096]{1,0:T(8,128)(2,1)} async-done(((bf16[1024,512]{1,0:T(8,128)(2,1)}), bf16[1024,4096]{1,0:T(8,128)(2,1)}) %all-gather.15.cloned.1.call-update) | async-done | bytes 8388624 | tf_op jit(solution)/shard_map/all_gather | solution.py:36
  385.1 53.7 %all-gather.13.cloned.1.call-done = bf16[4096,512]{1,0:T(8,128)(2,1)} async-done(((bf16[1024,512]{1,0:T(8,128)(2,1)}), bf16[4096,512]{1,0:T(8,128)(2,1)}) %all-gather.13.cloned.1.call-update) | async-done | bytes 4194320 | tf_op jit(solution)/shard_map/all_gather | solution.py:40
  438.8 10.2 %fusion.2 = bf16[1024,512]{0,1:T(8,128)(2,1)} fusion(bf16[4096,512]{1,0:T(8,128)(2,1)} %all-gather.13.cloned.1.call-done, bf16[1024,4096]{1,0:T(8,128)(2,1)} %all-gather.15.cloned.1.call-done), kind=kOutput, calls=%fused_computation.9 | convolution fusion | flops 4295491584 | bytes 13631488 | tf_op jit(solution)/shard_map/dot_general | solution.py:38
  449.0 0.0 all-gather.17.cloned.1.call-update
  449.0 0.0 reduce-scatter.5.cloned.1.call-start
  449.0 52.8 %all-gather.17.cloned.1.call-done = bf16[4096,512]{0,1:T(8,128)(2,1)} async-done(((bf16[1024,512]{0,1:T(8,128)(2,1)}), bf16[4096,512]{0,1:T(8,128)(2,1)}) %all-gather.17.cloned.1.call-update) | async-done | bytes 4194320 | tf_op jit(solution)/shard_map/all_gather | solution.py:43
  501.9 9.1 %convolution_convert_fusion = bf16[4096,1024]{1,0:T(8,128)(2,1)} fusion(bf16[4096,512]{0,1:T(8,128)(2,1)} %all-gather.17.cloned.1.call-done, bf16[1024,512]{1,0:T(8,128)(2,1)S(1)} %copy-done), kind=kOutput, calls=%fused_computation | convolution fusion | flops 4299161600 | bytes 13631488 | tf_op jit(solution)/shard_map/dot_general | solution.py:45
  510.9 0.0 reduce-scatter.5.cloned.1.call-update
  511.0 89.8 %reduce-scatter.5.cloned.1.call-done = bf16[512,1024]{1,0:T(8,128)(2,1)} async-done(((bf16[4096,1024]{1,0:T(8,128)(2,1)}), bf16[512,1024]{1,0:T(8,128)(2,1)}) %reduce-scatter.5.cloned.1.call-update) | async-done | bytes 1048592 | tf_op jit(solution)/shard_map/reduce_scatter | solution.py:44
  600.7 2.3 copy.8
Async XLA Ops:
  7.2 233.2 %copy-start = (bf16[1024,512]{1,0:T(8,128)(2,1)S(1)}, bf16[1024,512]{1,0:T(8,128)(2,1)}, u32[]{:S(2)}) copy-start(bf16[1024,512]{1,0:T(8,128)(2,1)} %param.6) | copy-start | bytes 3145732
  7.2 58.1 %all-gather.9.cloned.1.call-start = ((), (), s32[]{:S(2)}) async-start(), calls=%async_computation.3 | async-start | bytes 5242880 | tf_op jit(solution)/shard_map/all_gather | solution.py:15
  7.9 141.7 %all-gather.7.cloned.1.call-start = ((), (), s32[]{:S(2)}) async-start(), calls=%async_computation.2 | async-start | bytes 9437184 | tf_op jit(solution)/shard_map/all_gather | solution.py:18
  10.4 230.0 %all-gather.11.cloned.1.call-start = ((), (), s32[]{:S(2)}) async-start(), calls=%async_computation.4 | async-start | bytes 9437184 | tf_op jit(solution)/shard_map/all_gather | solution.py:22
  159.6 141.9 %reduce-scatter.3.cloned.1.call-start = ((), (), s32[]{:S(2)}) async-start(), calls=%async_computation.5 | async-start | bytes 5242880 | tf_op jit(solution)/shard_map/reduce_scatter | solution.py:23
  250.1 51.4 %copy-start.1 = (f32[1024,512]{1,0:T(8,128)S(1)}, f32[1024,512]{1,0:T(8,128)}, u32[]{:S(2)}) copy-start(f32[1024,512]{1,0:T(8,128)} %param.8) | copy-start | bytes 6291460
  250.1 135.0 %all-gather.15.cloned.1.call-start = ((), (), s32[]{:S(2)}) async-start(), calls=%async_computation.7 | async-start | bytes 9437184 | tf_op jit(solution)/shard_map/all_gather | solution.py:36
  250.7 188.1 %all-gather.13.cloned.1.call-start = ((), (), s32[]{:S(2)}) async-start(), calls=%async_computation.6 | async-start | bytes 5242880 | tf_op jit(solution)/shard_map/all_gather | solution.py:40
  306.8 195.1 %all-gather.17.cloned.1.call-start = ((), (), s32[]{:S(2)}) async-start(), calls=%async_computation.8 | async-start | bytes 5242880 | tf_op jit(solution)/shard_map/all_gather | solution.py:43
  449.0 151.7 %reduce-scatter.5.cloned.1.call-start = ((), (), s32[]{:S(2)}) async-start(), calls=%async_computation.9 | async-start | bytes 9437184 | tf_op jit(solution)/shard_map/reduce_scatter | solution.py:44
Sparse Core Ops, SparseCore 0:
  9.9 55.3 all-gather.8
  67.5 82.0 all-gather.6
  159.7 80.5 all-gather.10
  250.2 51.2 reduce-scatter.2
  303.0 82.0 all-gather.14
  387.5 51.2 all-gather.12
  449.1 52.6 all-gather.16
  511.1 89.5 reduce-scatter.4
where the time goes:
time: 610 us
  waiting for transfers between devices  546 us (90%)
  matrix products  39 us (6%)
  between operations  14.1 us (2%)
  other arithmetic  7.66 us (1%)
    reduce_scatter x1, waiting for transfers between devices, local(): lax.psum_scatter(lax.dot_general(back_cols, left_basis, (((1,), (1,)), ((...  89.8 us
    all_gather x1, waiting for transfers between devices, local(): lax.all_gather(negated, 'cols', axis=1, tiled=True)  84.3 us
    all_gather x1, waiting for transfers between devices, local(): half_rows = lax.all_gather(half_rotated, 'cols', axis=1, tiled=True)  80.7 us
    all_gather x1, waiting for transfers between devices, local(): right_rows = lax.all_gather(right_basis, 'cols', axis=1, tiled=True)  78.1 us
    all_gather x1, waiting for transfers between devices, local(): right_cols = lax.all_gather(right_basis, 'rows', axis=0, tiled=True)  54.9 us
    all_gather x1, waiting for transfers between devices, local(): lax.all_gather(normalized, 'rows', axis=0, tiled=True)  53.7 us
    all_gather x1, waiting for transfers between devices, local(): back_cols = lax.all_gather(back_half, 'rows', axis=0, tiled=True)  52.8 us
    reduce_scatter x1, waiting for transfers between devices, local(): lax.psum_scatter(lax.dot_general(half_rows, left_basis, (((0,), (0,)), ((...  50.7 us
  transfers between devices with their start and end apart: 8, of which 8 were waited for; matrix products, arithmetic and copies ran while one was open for 1% of the time, Pallas kernels for 0%

commit v1 on v0

v1 whole, which is shorter than its diff:
```python
import jax
import jax.numpy as jnp
from jax import lax
from jax.sharding import PartitionSpec as P

beta_first = 0.9
beta_second = 0.95
corr_first = 1.0 - 0.9**10
corr_second = 1.0 - 0.95**10
epsilon = 1e-08

bf16 = jnp.bfloat16
f32 = jnp.float32


def bits_of(count, reverse):
    bits = list(range(count.bit_length() - 1))
    return bits[::-1] if reverse else bits


def swap(block, count, bit):
    return lax.ppermute(block, "rows", [(i, i ^ (1 << bit)) for i in range(count)])


def my_bit(bit):
    return (lax.axis_index("rows") >> bit) & 1


def scatter_sum(parts, reverse):
    count = parts.shape[0]
    held = list(range(count.bit_length() - 1))[::-1]
    parts = parts.reshape((2,) * len(held) + parts.shape[1:])
    for bit in bits_of(count, reverse):
        axis = held.index(bit)
        mine = my_bit(bit)
        got = swap(lax.dynamic_index_in_dim(parts, 1 - mine, axis, False), count, bit)
        kept = lax.dynamic_index_in_dim(parts, mine, axis, False)
        held.remove(bit)
        total = kept.astype(f32) + got.astype(f32)
        parts = total.astype(bf16) if held else total
    return parts


def gather(block, count, reverse):
    rest = block.shape
    held = []
    for bit in bits_of(count, reverse):
        got = swap(block, count, bit)
        mine = my_bit(bit)
        axis = sum(other > bit for other in held)
        block = jnp.where(mine == 0, jnp.stack([block, got], axis), jnp.stack([got, block], axis))
        held.append(bit)
    return block.reshape((count,) + rest)


def make_local(rows, cols):
    def local(forget_grad, left_basis, right_basis, first_moment, second_moment):
        width = right_basis.shape[1]
        depth = right_basis.shape[0]
        per = cols // rows
        sub = width // rows

        grad_rows = lax.all_gather(forget_grad, "cols", axis=1, tiled=True)

        dealt = lax.all_to_all(right_basis.reshape(per, rows, sub, width), "rows", 1, 0)
        dealt = dealt.reshape(depth, width)
        cuts = [0, width * 3 // 4, width]
        spans = list(zip(cuts[:-1], cuts[1:]))
        right_rows = [
            lax.all_gather(dealt[:, lo:hi], "cols", axis=1, tiled=True) for lo, hi in spans
        ]
        left_rows = lax.all_gather(left_basis, "cols", axis=1, tiled=True)

        half = lax.dot_general(
            grad_rows, left_basis, (((0,), (0,)), ((), ())), preferred_element_type=f32
        ).astype(bf16)
        half = half.reshape(cols, rows, sub, width).swapaxes(0, 1)
        cut = cols // 2
        half = jnp.concatenate(
            [scatter_sum(half[:, :cut], False), scatter_sum(half[:, cut:], True)], 0
        ).astype(bf16).reshape(depth, width)

        first = first_moment.reshape(per, width, width)
        second = second_moment.reshape(per, width, width)
        back = None
        rotated = []
        cut = per // 2
        for (lo, hi), basis in zip(spans, right_rows):
            parts = lax.dot_general(
                basis, half, (((0,), (0,)), ((), ())), preferred_element_type=f32
            ).astype(bf16)
            parts = parts.reshape(rows, per, hi - lo, width)
            normals = []
            pair = []
            for reverse, own in ((False, slice(0, cut)), (True, slice(cut, per))):
                turned = -scatter_sum(parts[:, own], reverse)
                pair.append(turned)
                new_first = beta_first * first[own, lo:hi] + (1.0 - beta_first) * turned
                new_second = beta_second * second[own, lo:hi] + (1.0 - beta_second) * turned * turned
                normal = new_first / corr_first / (jnp.sqrt(new_second / corr_second) + epsilon)
                normals.append(gather(normal.astype(bf16), rows, reverse))
            rotated.append(jnp.concatenate(pair, 0))
            normals = jnp.concatenate(normals, 1).reshape(cols * (hi - lo), width)
            term = jnp.dot(basis, normals, preferred_element_type=f32)
            back = term if back is None else back + term
        rotated = jnp.concatenate(rotated, 1).reshape(depth, width)
        new_first = beta_first * first_moment + (1.0 - beta_first) * rotated
        new_second = beta_second * second_moment + (1.0 - beta_second) * rotated * rotated

        back = back.astype(bf16).reshape(cols, sub, width)
        back = lax.all_to_all(back, "cols", 0, 1).reshape(sub, cols * width)
        cut = sub // 2
        back = jnp.concatenate([gather(back[:cut], rows, False), gather(back[cut:], rows, True)], 1)
        back = back.reshape(width, cols * width)
        step_dir = lax.dot_general(
            left_rows, back, (((1,), (1,)), ((), ())), preferred_element_type=f32
        ).astype(bf16)
        return (step_dir, new_first, new_second)

    return local


def solution(mesh):
    spec = P("rows", "cols")
    return jax.shard_map(
        make_local(mesh.shape["rows"], mesh.shape["cols"]),
        mesh=mesh,
        in_specs=(spec,) * 5,
        out_specs=(spec,) * 3,
        check_vma=False,
    )
```

time: 610 us -> 403 us (0.66)
  waiting for transfers between devices: 546 us -> 192 us
  local copies, waits for them, and re-layouts: 2.29 us -> 59.1 us
  blocking collectives: 0 us -> 48.1 us
  starting transfers between devices: 0.5 us -> 26.6 us
  other arithmetic: 7.66 us -> 27.5 us
    all_gather x6 -> x4, waiting for transfers between devices: 404 us -> 92.2 us  [the longest x1 64.1 us: local(): grad_rows = lax.all_gather(forget_grad, 'cols', axis=1, tiled=True)]
    reduce_scatter x2 -> x0, waiting for transfers between devices: 140 us -> none  [the longest x1 89.8 us: local(): lax.psum_scatter(lax.dot_general(back_cols, left_basis, (((1,), (1,)), ((...]
    ppermute x0 -> x24, waiting for transfers between devices: none -> 99 us  [swap(): lax.ppermute(block, 'rows', [(i, i ^ 1 << bit) for i in range(count)])]
    all_to_all x0 -> x2, blocking collectives: none -> 48.1 us  [the longest x1 29 us: local(): back = lax.all_to_all(back, 'cols', 0, 1).reshape(sub, cols * width)]
    ppermute x0 -> x24, starting transfers between devices: none -> 26.4 us  [swap(): lax.ppermute(block, 'rows', [(i, i ^ 1 << bit) for i in range(count)])]
    unnamed x5 -> x47, local copies, waits for them, and re-layouts: 2.29 us -> 26 us
    slice x0 -> x8, local copies, waits for them, and re-layouts: none -> 11.1 us  [the longest x2 8.39 us: local(): turned = -scatter_sum(parts[:, own], reverse)]
    reshape x0 -> x2, local copies, waits for them, and re-layouts: none -> 7.94 us  [local(): parts = parts.reshape(rows, per, hi - lo, width)]
  transfers between devices with their start and end apart: 8 -> 28, of which waited for: 8 -> 17; matrix products, arithmetic and copies ran while one was open for 1% -> 26% of each run, Pallas kernels for 0% -> 0%
where the time goes in v1:
time: 403 us; the launch traced here: 401 us
  waiting for transfers between devices  192 us (48%)
  local copies, waits for them, and re-layouts  59.1 us (15%)
  blocking collectives  48.1 us (12%)
  matrix products  33.9 us (8%)
  other arithmetic  27.5 us (7%)
  starting transfers between devices  26.6 us (7%)
  between operations  14.3 us (4%)
    ppermute x24, waiting for transfers between devices, swap(): lax.ppermute(block, 'rows', [(i, i ^ 1 << bit) for i in range(count)])  99 us
    all_gather x1, waiting for transfers between devices, local(): grad_rows = lax.all_gather(forget_grad, 'cols', axis=1, tiled=True)  64.1 us
    all_to_all x1, blocking collectives, local(): back = lax.all_to_all(back, 'cols', 0, 1).reshape(sub, cols * width)  29 us
    all_gather x2, waiting for transfers between devices, local(): lax.all_gather(dealt[:, lo:hi], 'cols', axis=1, tiled=True)  28.1 us
    ppermute x24, starting transfers between devices, swap(): lax.ppermute(block, 'rows', [(i, i ^ 1 << bit) for i in range(count)])  26.4 us
    unnamed x47, local copies, waits for them, and re-layouts  26 us
    all_to_all x1, blocking collectives, local(): lax.all_to_all(right_basis.reshape(per, rows, sub, width), 'rows', 1, 0)  19.1 us
    dot_general x2, matrix products, local(): lax.dot_general(basis, half, (((0,), (0,)), ((), ())), preferred_element_...  10.6 us
  transfers between devices with their start and end apart: 28, of which 17 were waited for; matrix products, arithmetic and copies ran while one was open for 26% of the time, Pallas kernels for 0%

profile of v1, /device:TPU:0, one launch (start us, length us, event | category | flops | bytes accessed | tf_op | source)
XLA Modules:
  0.0 401.4 jit_solution(17008855031719364063)
XLA Ops:
  9.3 19.1 %all_to_all.30 = bf16[1,2,4,128,512]{4,3,1,0,2:T(8,128)(2,1)S(1)} all-to-all(bf16[1,2,4,128,512]{4,3,1,0,2:T(8,128)(2,1)S(1)} %copy.52), channel_id=1, replica_groups=mesh['rows'=4,'cols'=8] {'rows'}, dimensions={2} | all-to-all | bytes 2097152 | tf_op jit(solution)/shard_map/all_to_all | solution.py:65
  30.3 64.1 %all-gather.5.cloned.1.call-done = bf16[1024,4096]{1,0:T(8,128)(2,1)} async-done(((bf16[1024,512]{1,0:T(8,128)(2,1)}), bf16[1024,4096]{1,0:T(8,128)(2,1)}) %all-gather.5.cloned.1.call-update) | async-done | bytes 8388624 | tf_op jit(solution)/shard_map/all_gather | solution.py:63
  94.4 8.4 %convolution_convert_fusion = bf16[4096,512]{1,0:T(8,128)(2,1)S(1)} fusion(bf16[1024,4096]{1,0:T(8,128)(2,1)} %all-gather.5.cloned.1.call-done, bf16[1024,512]{1,0:T(8,128)(2,1)S(1)} %copy-done.17), kind=kOutput, calls=%fused_computation | convolution fusion | flops 4297064448 | bytes 13631488 | tf_op jit(solution)/shard_map/dot_general | solution.py:74
  105.5 1.5 collective-permute-start.2
  108.2 1.5 collective-permute-start
  109.7 21.4 %collective-permute-done.2 = bf16[2,4,128,512]{3,2,0,1:T(8,128)(2,1)} collective-permute-done((bf16[2,4,128,512]{3,2,0,1:T(8,128)(2,1)}, bf16[2,4,128,512]{3,2,0,1:T(8,128)(2,1)}, u32[]{:S(2)}, u32[]{:S(2)}) %collective-permute-start.2) | collective-permute-done | bytes 1048608 | tf_op jit(solution)/shard_map/ppermute | solution.py:22
  131.1 1.5 fusion.2
  135.0 1.6 fusion.3
  136.6 1.6 collective-permute-start.1
  138.3 8.7 %collective-permute-done.3 = bf16[4,128,512]{2,1,0:T(8,128)(2,1)S(1)} collective-permute-done((bf16[4,128,512]{2,1,0:T(8,128)(2,1)}, bf16[4,128,512]{2,1,0:T(8,128)(2,1)S(1)}, u32[]{:S(2)}, u32[]{:S(2)}) %collective-permute-start.3) | collective-permute-done | bytes 524320 | tf_op jit(solution)/shard_map/ppermute | solution.py:22
  148.2 1.5 collective-permute-done.1
  150.0 2.9 fusion.7
  153.7 2.3 fusion.57
  156.0 2.4 copy.76
  161.0 1.5 collective-permute-start.16
  162.6 28.1 %all-gather.7.cloned.1.call-done = bf16[1024,3072]{1,0:T(8,128)(2,1)} async-done(((bf16[1024,384]{1,0:T(8,128)(2,1)}), bf16[1024,3072]{1,0:T(8,128)(2,1)}) %all-gather.7.cloned.1.call-update) | async-done | bytes 6291472 | tf_op jit(solution)/shard_map/all_gather | solution.py:70
  190.6 7.7 %fusion = bf16[3072,512]{0,1:T(8,128)(2,1)} fusion(bf16[1024,512]{1,0:T(8,128)(2,1)S(1)} %bitcast.209, bf16[1024,3072]{1,0:T(8,128)(2,1)} %all-gather.7.cloned.1.call-done), kind=kOutput, calls=%fused_computation.3 | convolution fusion | flops 3222798336 | bytes 10485760 | tf_op jit(solution)/shard_map/dot_general | solution.py:89
  198.3 7.2 %reshape.1014 = bf16[4,2,384,512]{2,1,0,3:T(2,128)(2,1)S(1)} reshape(bf16[3072,512]{0,1:T(8,128)(2,1)} %fusion) | data formatting | bytes 6291456 | tf_op jit(solution)/shard_map/reshape | solution.py:92
  205.5 6.1 %fusion.55 = (bf16[4,1,384,512]{2,1,0,3:T(2,128)(2,1)}, bf16[4,1,384,512]{2,1,0,3:T(2,128)(2,1)}) fusion(bf16[4,2,384,512]{2,1,0,3:T(2,128)(2,1)S(1)} %reshape.1014), kind=kLoop, calls=%fused_computation.120 | loop fusion | bytes 6291456 | tf_op jit(solution)/shard_map/slice | solution.py:96
  211.6 8.3 %copy.74 = bf16[4,1,384,512]{3,2,0,1:T(8,128)(2,1)} copy(bf16[4,1,384,512]{2,1,0,3:T(2,128)(2,1)} %get-tuple-element.29) | data formatting | bytes 3145728
  219.9 2.1 dynamic-slice_bitcast_fusion.2
  222.0 1.5 collective-permute-start.4
  223.5 6.1 %copy.75 = bf16[4,1,384,512]{3,2,0,1:T(8,128)(2,1)} copy(bf16[4,1,384,512]{2,1,0,3:T(2,128)(2,1)S(1)} %copy-done) | data formatting | bytes 3145728
  231.0 1.5 collective-permute-start.8
  236.0 6.6 %collective-permute-done.4 = bf16[2,1,384,512]{3,2,0,1:T(8,128)(2,1)} collective-permute-done((bf16[2,1,384,512]{3,2,0,1:T(8,128)(2,1)}, bf16[2,1,384,512]{3,2,0,1:T(8,128)(2,1)}, u32[]{:S(2)}, u32[]{:S(2)}) %collective-permute-start.4) | collective-permute-done | bytes 786464 | tf_op jit(solution)/shard_map/ppermute | solution.py:22
  244.8 1.5 collective-permute-start.5
  246.3 5.1 %collective-permute-done.8 = bf16[2,1,384,512]{3,2,1,0:T(8,128)(2,1)S(1)} collective-permute-done((bf16[2,1,384,512]{3,2,1,0:T(8,128)(2,1)S(1)}, bf16[2,1,384,512]{3,2,1,0:T(8,128)(2,1)S(1)}, u32[]{:S(2)}, u32[]{:S(2)}) %collective-permute-start.8) | collective-permute-done | bytes 786464 | tf_op jit(solution)/shard_map/ppermute | solution.py:22
  254.3 2.1 fusion.49
  256.4 1.5 collective-permute-start.18
  259.0 5.5 %collective-permute-done.18 = bf16[1,128,512]{2,1,0:T(8,128)(2,1)S(1)} collective-permute-done((bf16[1,128,512]{2,1,0:T(8,128)(2,1)S(1)}, bf16[1,128,512]{2,1,0:T(8,128)(2,1)S(1)}, u32[]{:S(2)}, u32[]{:S(2)}) %collective-permute-start.18) | collective-permute-done | bytes 131104 | tf_op jit(solution)/shard_map/ppermute | solution.py:22
  266.7 1.5 collective-permute-start.15
  268.3 4.1 %fusion.29 = (bf16[1,384,512]{2,1,0:T(8,128)(2,1)S(1)}, f32[1,384,512]{2,1,0:T(8,128)}, bf16[1,384,512]{2,1,0:T(8,128)(2,1)S(1)}, f32[1,384,512]{2,1,0:T(8,128)}) fusion(f32[2,512,512]{2,1,0:T(8,128)S(1)} %bitcast.186, f32[2,512,512]{2,1,0:T(8,128)} %bitcast.188, bf16[1,384,512]{2,1,0:T(8,128)(2,1)} %collective-permute-done.5, ...), kind=kLoop, calls=%fused_computation.72 | loop fusion | flops 6291456 | bytes 7077896 | tf_op jit(solution)/shard_map/convert_element_type | solution.py:101
  275.2 6.5 %collective-permute-done.10 = bf16[1,384,512]{2,1,0:T(8,128)(2,1)S(1)} collective-permute-done((bf16[1,384,512]{2,1,0:T(8,128)(2,1)S(1)}, bf16[1,384,512]{2,1,0:T(8,128)(2,1)S(1)}, u32[]{:S(2)}, u32[]{:S(2)}) %collective-permute-start.10) | collective-permute-done | bytes 393248 | tf_op jit(solution)/shard_map/ppermute | solution.py:22
  281.9 1.6 collective-permute-start.11
  283.8 1.5 collective-permute-start.7
  287.0 12.9 %collective-permute-done.11 = bf16[2,1,384,512]{3,2,1,0:T(8,128)(2,1)S(1)} collective-permute-done((bf16[2,1,384,512]{3,2,1,0:T(8,128)(2,1)S(1)}, bf16[2,1,384,512]{3,2,1,0:T(8,128)(2,1)S(1)}, u32[]{:S(2)}, u32[]{:S(2)}) %collective-permute-start.11) | collective-permute-done | bytes 786464 | tf_op jit(solution)/shard_map/ppermute | solution.py:22
  300.3 1.5 collective-permute-done.7
  304.7 4.4 %fusion.9 = bf16[1024,512]{0,1:T(8,128)(2,1)} fusion(f32[512,1024]{1,0:T(8,128)S(1)} %fusion.58, bf16[3072,512]{1,0:T(8,128)(2,1)S(1)} %bitcast.214, bf16[1024,3072]{1,0:T(8,128)(2,1)S(1)} %bitcast.242), kind=kOutput, calls=%fused_computation.27 | convolution fusion | flops 3222274048 | bytes 12582912 | tf_op jit(solution)/shard_map/dot_general | solution.py:104
  309.2 1.5 copy.72
  310.7 29.0 %all_to_all.31 = bf16[8,128,1,512]{3,1,2,0:T(8,128)(2,1)S(1)} all-to-all(bf16[8,128,1,512]{3,1,2,0:T(8,128)(2,1)S(1)} %bitcast.207), channel_id=1, replica_groups=mesh['rows'=4,'cols'=8] {'cols'}, dimensions={0} | all-to-all | bytes 2097152 | tf_op jit(solution)/shard_map/all_to_all | solution.py:111
  340.6 1.7 collective-permute-start.22
  344.1 2.8 fusion.1
  349.4 4.7 %collective-permute-done.22 = bf16[64,4096]{1,0:T(8,128)(2,1)S(1)} collective-permute-done((bf16[64,4096]{1,0:T(8,128)(2,1)}, bf16[64,4096]{1,0:T(8,128)(2,1)S(1)}, u32[]{:S(2)}, u32[]{:S(2)}) %collective-permute-start.22) | collective-permute-done | bytes 524320 | tf_op jit(solution)/shard_map/ppermute | solution.py:22
  354.7 3.0 collective-permute-done.20
  360.8 18.3 %collective-permute-done.23 = bf16[2,64,4096]{2,1,0:T(8,128)(2,1)S(1)} collective-permute-done((bf16[2,64,4096]{2,1,0:T(8,128)(2,1)S(1)}, bf16[2,64,4096]{2,1,0:T(8,128)(2,1)S(1)}, u32[]{:S(2)}, u32[]{:S(2)}) %collective-permute-start.23) | collective-permute-done | bytes 1048608 | tf_op jit(solution)/shard_map/ppermute | solution.py:22
  379.4 2.0 collective-permute-done.21
  381.8 2.6 pad_maximum_fusion
  384.4 9.2 %fusion.8 = bf16[1024,512]{0,1:T(8,128)(2,1)S(1)} fusion(bf16[512,4096]{1,0:T(8,128)(2,1)} %bitcast.202, bf16[1024,4096]{1,0:T(8,128)(2,1)} %all-gather.11.cloned.1.call-done), kind=kOutput, calls=%fused_computation.26 | convolution fusion | flops 4295491584 | bytes 13631488 | tf_op jit(solution)/shard_map/dot_general | solution.py:115
  (135 shorter events, 47.1 us)
Async XLA Ops:
  7.2 87.2 %all-gather.5.cloned.1.call-start = ((), (), s32[]{:S(2)}) async-start(), calls=%async_computation.2 | async-start | bytes 9437184 | tf_op jit(solution)/shard_map/all_gather | solution.py:63
  7.9 142.0 %all-gather.9.cloned.1.call-start = ((), (), s32[]{:S(2)}) async-start(), calls=%async_computation.4 | async-start | bytes 2359296 | tf_op jit(solution)/shard_map/all_gather | solution.py:70
  28.4 66.0 %copy-start.17 = (bf16[1024,512]{1,0:T(8,128)(2,1)S(1)}, bf16[1024,512]{1,0:T(8,128)(2,1)}, u32[]{:S(2)}) copy-start(bf16[1024,512]{1,0:T(8,128)(2,1)} %param.6) | copy-start | bytes 3145732
  29.2 161.5 %all-gather.7.cloned.1.call-start = ((), (), s32[]{:S(2)}) async-start(), calls=%async_computation.3 | async-start | bytes 7077888 | tf_op jit(solution)/shard_map/all_gather | solution.py:70
  30.2 354.2 %all-gather.11.cloned.1.call-start = ((), (), s32[]{:S(2)}) async-start(), calls=%async_computation.5 | async-start | bytes 9437184 | tf_op jit(solution)/shard_map/all_gather | solution.py:72
  103.1 1.3 copy-start.3
  105.5 25.6 %collective-permute-start.2 = (bf16[2,4,128,512]{3,2,0,1:T(8,128)(2,1)}, bf16[2,4,128,512]{3,2,0,1:T(8,128)(2,1)}, u32[]{:S(2)}, u32[]{:S(2)}) collective-permute-start(bf16[2,4,128,512]{3,2,0,1:T(8,128)(2,1)} %dynamic-slice_bitcast_fusion), channel_id=1, source_target_pairs={{0,16},{8,24},{16,0},{24,8},{1,17},{9,25},{17,1},{25,9},{2,18},{10... | collective-permute-start | bytes 3145736 | tf_op jit(solution)/shard_map/ppermute | solution.py:22
  107.2 24.0 %copy-start.4 = (bf16[4,4,128,512]{3,2,0,1:T(8,128)(2,1)S(1)}, bf16[4,4,128,512]{3,2,0,1:T(8,128)(2,1)}, u32[]{:S(2)}) copy-start(bf16[4,4,128,512]{3,2,0,1:T(8,128)(2,1)} %copy-done.3) | copy-start | bytes 6291460
  108.2 26.8 %collective-permute-start = (bf16[2,4,128,512]{3,2,1,0:T(8,128)(2,1)}, bf16[2,4,128,512]{3,2,1,0:T(8,128)(2,1)}, u32[]{:S(2)}, u32[]{:S(2)}) collective-permute-start(bf16[2,4,128,512]{3,2,1,0:T(8,128)(2,1)} %bitcast.184), channel_id=1, source_target_pairs={{0,8},{8,0},{16,24},{24,16},{1,9},{9,1},{17,25},{25,17},{2,10},{10... | collective-permute-start | bytes 3145736 | tf_op jit(solution)/shard_map/ppermute | solution.py:22
  132.6 3.9 copy-start.7
  133.5 13.5 %collective-permute-start.3 = (bf16[4,128,512]{2,1,0:T(8,128)(2,1)}, bf16[4,128,512]{2,1,0:T(8,128)(2,1)S(1)}, u32[]{:S(2)}, u32[]{:S(2)}) collective-permute-start(bf16[4,128,512]{2,1,0:T(8,128)(2,1)} %dynamic-slice_bitcast_fusion.3), channel_id=1, source_target_pairs={{0,8},{8,0},{16,24},{24,16},{1,9},{9,1},{17,25},{25,17},{2,10},{10... | collective-permute-start | bytes 1572872 | tf_op jit(solution)/shard_map/ppermute | solution.py:22
  136.6 13.0 %collective-permute-start.1 = (bf16[4,128,512]{2,1,0:T(8,128)(2,1)S(1)}, bf16[4,128,512]{2,1,0:T(8,128)(2,1)S(1)}, u32[]{:S(2)}, u32[]{:S(2)}) collective-permute-start(bf16[4,128,512]{2,1,0:T(8,128)(2,1)S(1)} %dynamic-slice_bitcast_fusion.4), channel_id=1, source_target_pairs={{0,16},{8,24},{16,0},{24,8},{1,17},{9,25},{17,1},{25,9},{2,18},{10... | collective-permute-start | bytes 1572872 | tf_op jit(solution)/shard_map/ppermute | solution.py:22
  158.3 1.3 copy-start.13
  159.1 73.4 %collective-permute-start.12 = (bf16[2,1,128,512]{3,2,1,0:T(8,128)(2,1)}, bf16[2,1,128,512]{3,2,1,0:T(8,128)(2,1)}, u32[]{:S(2)}, u32[]{:S(2)}) collective-permute-start(bf16[2,1,128,512]{3,2,1,0:T(8,128)(2,1)} %dynamic-slice_bitcast_fusion.8), channel_id=1, source_target_pairs={{0,8},{8,0},{16,24},{24,16},{1,9},{9,1},{17,25},{25,17},{2,10},{10... | collective-permute-start | bytes 786440 | tf_op jit(solution)/shard_map/ppermute | solution.py:22
  161.0 29.7 %copy-start.11 = (bf16[4,1,128,512]{3,2,0,1:T(8,128)(2,1)}, bf16[4,1,128,512]{3,2,0,1:T(8,128)(2,1)S(1)}, u32[]{:S(2)}) copy-start(bf16[4,1,128,512]{3,2,0,1:T(8,128)(2,1)S(1)} %copy.78) | copy-start | bytes 1572868
  161.0 73.2 %collective-permute-start.16 = (bf16[2,1,128,512]{3,2,1,0:T(8,128)(2,1)S(1)}, bf16[2,1,128,512]{3,2,1,0:T(8,128)(2,1)}, u32[]{:S(2)}, u32[]{:S(2)}) collective-permute-start(bf16[2,1,128,512]{3,2,1,0:T(8,128)(2,1)S(1)} %dynamic-slice_bitcast_fusion.7), channel_id=1, source_target_pairs={{0,16},{8,24},{16,0},{24,8},{1,17},{9,25},{17,1},{25,9},{2,18},{10... | collective-permute-start | bytes 786440 | tf_op jit(solution)/shard_map/ppermute | solution.py:22
  211.6 11.9 %copy-start = (bf16[4,1,384,512]{2,1,0,3:T(2,128)(2,1)S(1)}, bf16[4,1,384,512]{2,1,0,3:T(2,128)(2,1)}, u32[]{:S(2)}) copy-start(bf16[4,1,384,512]{2,1,0,3:T(2,128)(2,1)} %get-tuple-element.30) | copy-start | bytes 4718596
  222.0 20.7 %collective-permute-start.4 = (bf16[2,1,384,512]{3,2,0,1:T(8,128)(2,1)}, bf16[2,1,384,512]{3,2,0,1:T(8,128)(2,1)}, u32[]{:S(2)}, u32[]{:S(2)}) collective-permute-start(bf16[2,1,384,512]{3,2,0,1:T(8,128)(2,1)} %dynamic-slice_bitcast_fusion.2), channel_id=1, source_target_pairs={{0,8},{8,0},{16,24},{24,16},{1,9},{9,1},{17,25},{25,17},{2,10},{10... | collective-permute-start | bytes 2359304 | tf_op jit(solution)/shard_map/ppermute | solution.py:22
  229.6 4.6 %copy-start.12 = (bf16[4,1,128,512]{3,2,0,1:T(8,128)(2,1)S(1)}, bf16[4,1,128,512]{3,2,0,1:T(8,128)(2,1)}, u32[]{:S(2)}) copy-start(bf16[4,1,128,512]{3,2,0,1:T(8,128)(2,1)} %copy-done.11) | copy-start | bytes 1572868
  229.6 13.1 %copy-start.6 = (bf16[4,1,384,512]{3,2,0,1:T(8,128)(2,1)S(1)}, bf16[4,1,384,512]{3,2,0,1:T(8,128)(2,1)}, u32[]{:S(2)}) copy-start(bf16[4,1,384,512]{3,2,0,1:T(8,128)(2,1)} %copy.74) | copy-start | bytes 4718596
  231.0 20.5 %collective-permute-start.8 = (bf16[2,1,384,512]{3,2,1,0:T(8,128)(2,1)S(1)}, bf16[2,1,384,512]{3,2,1,0:T(8,128)(2,1)S(1)}, u32[]{:S(2)}, u32[]{:S(2)}) collective-permute-start(bf16[2,1,384,512]{3,2,1,0:T(8,128)(2,1)S(1)} %dynamic-slice_bitcast_fusion.1), channel_id=1, source_target_pairs={{0,16},{8,24},{16,0},{24,8},{1,17},{9,25},{17,1},{25,9},{2,18},{10... | collective-permute-start | bytes 2359304 | tf_op jit(solution)/shard_map/ppermute | solution.py:22
  233.6 20.6 %collective-permute-start.13 = (bf16[1,128,512]{2,1,0:T(8,128)(2,1)S(1)}, bf16[1,128,512]{2,1,0:T(8,128)(2,1)S(1)}, u32[]{:S(2)}, u32[]{:S(2)}) collective-permute-start(bf16[1,128,512]{2,1,0:T(8,128)(2,1)S(1)} %dynamic-slice_bitcast_fusion.10), channel_id=1, source_target_pairs={{0,16},{8,24},{16,0},{24,8},{1,17},{9,25},{17,1},{25,9},{2,18},{10... | collective-permute-start | bytes 393224 | tf_op jit(solution)/shard_map/ppermute | solution.py:22
  234.3 17.2 %copy-start.5 = (bf16[4,1,384,512]{3,2,0,1:T(8,128)(2,1)S(1)}, bf16[4,1,384,512]{3,2,0,1:T(8,128)(2,1)}, u32[]{:S(2)}) copy-start(bf16[4,1,384,512]{3,2,0,1:T(8,128)(2,1)} %copy.75) | copy-start | bytes 4718596
  235.4 18.8 %collective-permute-start.17 = (bf16[1,128,512]{2,1,0:T(8,128)(2,1)S(1)}, bf16[1,128,512]{2,1,0:T(8,128)(2,1)S(1)}, u32[]{:S(2)}, u32[]{:S(2)}) collective-permute-start(bf16[1,128,512]{2,1,0:T(8,128)(2,1)S(1)} %dynamic-slice_bitcast_fusion.9), channel_id=1, source_target_pairs={{0,8},{8,0},{16,24},{24,16},{1,9},{9,1},{17,25},{25,17},{2,10},{10... | collective-permute-start | bytes 393224 | tf_op jit(solution)/shard_map/ppermute | solution.py:22
  244.0 10.2 %copy-start.1 = (f32[1024,512]{1,0:T(8,128)S(1)}, f32[1024,512]{1,0:T(8,128)}, u32[]{:S(2)}) copy-start(f32[1024,512]{1,0:T(8,128)} %param.9) | copy-start | bytes 6291460
  244.8 23.5 %collective-permute-start.5 = (bf16[1,384,512]{2,1,0:T(8,128)(2,1)}, bf16[1,384,512]{2,1,0:T(8,128)(2,1)}, u32[]{:S(2)}, u32[]{:S(2)}) collective-permute-start(bf16[1,384,512]{2,1,0:T(8,128)(2,1)} %dynamic-slice_bitcast_fusion.6), channel_id=1, source_target_pairs={{0,16},{8,24},{16,0},{24,8},{1,17},{9,25},{17,1},{25,9},{2,18},{10... | collective-permute-start | bytes 1179656 | tf_op jit(solution)/shard_map/ppermute | solution.py:22
  251.7 0.9 copy-start.10
  253.3 15.0 %collective-permute-start.9 = (bf16[1,384,512]{2,1,0:T(8,128)(2,1)}, bf16[1,384,512]{2,1,0:T(8,128)(2,1)}, u32[]{:S(2)}, u32[]{:S(2)}) collective-permute-start(bf16[1,384,512]{2,1,0:T(8,128)(2,1)} %dynamic-slice_bitcast_fusion.5), channel_id=1, source_target_pairs={{0,8},{8,0},{16,24},{24,16},{1,9},{9,1},{17,25},{25,17},{2,10},{10... | collective-permute-start | bytes 1179656 | tf_op jit(solution)/shard_map/ppermute | solution.py:22
  256.4 8.1 %collective-permute-start.18 = (bf16[1,128,512]{2,1,0:T(8,128)(2,1)S(1)}, bf16[1,128,512]{2,1,0:T(8,128)(2,1)S(1)}, u32[]{:S(2)}, u32[]{:S(2)}) collective-permute-start(bf16[1,128,512]{2,1,0:T(8,128)(2,1)S(1)} %get-tuple-element.25), channel_id=1, source_target_pairs={{0,16},{8,24},{16,0},{24,8},{1,17},{9,25},{17,1},{25,9},{2,18},{10... | collective-permute-start | bytes 393224 | tf_op jit(solution)/shard_map/ppermute | solution.py:22
  257.9 7.8 %collective-permute-start.14 = (bf16[1,128,512]{2,1,0:T(8,128)(2,1)S(1)}, bf16[1,128,512]{2,1,0:T(8,128)(2,1)}, u32[]{:S(2)}, u32[]{:S(2)}) collective-permute-start(bf16[1,128,512]{2,1,0:T(8,128)(2,1)S(1)} %get-tuple-element.19), channel_id=1, source_target_pairs={{0,8},{8,0},{16,24},{24,16},{1,9},{9,1},{17,25},{25,17},{2,10},{10... | collective-permute-start | bytes 393224 | tf_op jit(solution)/shard_map/ppermute | solution.py:22
  264.5 9.4 %collective-permute-start.19 = (bf16[2,1,128,512]{3,2,1,0:T(8,128)(2,1)S(1)}, bf16[2,1,128,512]{3,2,1,0:T(8,128)(2,1)S(1)}, u32[]{:S(2)}, u32[]{:S(2)}) collective-permute-start(bf16[2,1,128,512]{3,2,1,0:T(8,128)(2,1)S(1)} %maximum_select_fusion.17), channel_id=1, source_target_pairs={{0,8},{8,0},{16,24},{24,16},{1,9},{9,1},{17,25},{25,17},{2,10},{10... | collective-permute-start | bytes 786440 | tf_op jit(solution)/shard_map/ppermute | solution.py:22
  266.7 8.4 %collective-permute-start.15 = (bf16[2,1,128,512]{3,2,1,0:T(8,128)(2,1)S(1)}, bf16[2,1,128,512]{3,2,1,0:T(8,128)(2,1)S(1)}, u32[]{:S(2)}, u32[]{:S(2)}) collective-permute-start(bf16[2,1,128,512]{3,2,1,0:T(8,128)(2,1)S(1)} %maximum_select_fusion.15), channel_id=1, source_target_pairs={{0,16},{8,24},{16,0},{24,8},{1,17},{9,25},{17,1},{25,9},{2,18},{10... | collective-permute-start | bytes 786440 | tf_op jit(solution)/shard_map/ppermute | solution.py:22
  272.4 9.4 %collective-permute-start.10 = (bf16[1,384,512]{2,1,0:T(8,128)(2,1)S(1)}, bf16[1,384,512]{2,1,0:T(8,128)(2,1)S(1)}, u32[]{:S(2)}, u32[]{:S(2)}) collective-permute-start(bf16[1,384,512]{2,1,0:T(8,128)(2,1)S(1)} %get-tuple-element.23), channel_id=1, source_target_pairs={{0,16},{8,24},{16,0},{24,8},{1,17},{9,25},{17,1},{25,9},{2,18},{10... | collective-permute-start | bytes 1179656 | tf_op jit(solution)/shard_map/ppermute | solution.py:22
  274.1 9.6 %collective-permute-start.6 = (bf16[1,384,512]{2,1,0:T(8,128)(2,1)S(1)}, bf16[1,384,512]{2,1,0:T(8,128)(2,1)S(1)}, u32[]{:S(2)}, u32[]{:S(2)}) collective-permute-start(bf16[1,384,512]{2,1,0:T(8,128)(2,1)S(1)} %get-tuple-element.15), channel_id=1, source_target_pairs={{0,8},{8,0},{16,24},{24,16},{1,9},{9,1},{17,25},{25,17},{2,10},{10... | collective-permute-start | bytes 1179656 | tf_op jit(solution)/shard_map/ppermute | solution.py:22
  281.9 18.0 %collective-permute-start.11 = (bf16[2,1,384,512]{3,2,1,0:T(8,128)(2,1)S(1)}, bf16[2,1,384,512]{3,2,1,0:T(8,128)(2,1)S(1)}, u32[]{:S(2)}, u32[]{:S(2)}) collective-permute-start(bf16[2,1,384,512]{3,2,1,0:T(8,128)(2,1)S(1)} %maximum_select_fusion.11), channel_id=1, source_target_pairs={{0,8},{8,0},{16,24},{24,16},{1,9},{9,1},{17,25},{25,17},{2,10},{10... | collective-permute-start | bytes 2359304 | tf_op jit(solution)/shard_map/ppermute | solution.py:22
  283.6 1.8 copy-start.15
  283.8 18.0 %collective-permute-start.7 = (bf16[2,1,384,512]{3,2,1,0:T(8,128)(2,1)S(1)}, bf16[2,1,384,512]{3,2,1,0:T(8,128)(2,1)S(1)}, u32[]{:S(2)}, u32[]{:S(2)}) collective-permute-start(bf16[2,1,384,512]{3,2,1,0:T(8,128)(2,1)S(1)} %maximum_select_fusion.9), channel_id=1, source_target_pairs={{0,16},{8,24},{16,0},{24,8},{1,17},{9,25},{17,1},{25,9},{2,18},{10... | collective-permute-start | bytes 2359304 | tf_op jit(solution)/shard_map/ppermute | solution.py:22
  301.8 2.2 slice-start
  302.1 2.7 slice-start.1
  339.7 2.7 copy-start.8
  339.7 2.7 copy-start.9
  339.7 2.7 copy-start.16
  340.6 13.5 %collective-permute-start.22 = (bf16[64,4096]{1,0:T(8,128)(2,1)}, bf16[64,4096]{1,0:T(8,128)(2,1)S(1)}, u32[]{:S(2)}, u32[]{:S(2)}) collective-permute-start(bf16[64,4096]{1,0:T(8,128)(2,1)} %bitcast.119), channel_id=1, source_target_pairs={{0,16},{8,24},{16,0},{24,8},{1,17},{9,25},{17,1},{25,9},{2,18},{10... | collective-permute-start | bytes 1572872 | tf_op jit(solution)/shard_map/ppermute | solution.py:22
  342.3 1.8 copy-start.2
  343.4 14.3 %collective-permute-start.20 = (bf16[64,4096]{1,0:T(8,128)(2,1)}, bf16[64,4096]{1,0:T(8,128)(2,1)}, u32[]{:S(2)}, u32[]{:S(2)}) collective-permute-start(bf16[64,4096]{1,0:T(8,128)(2,1)} %bitcast.111), channel_id=1, source_target_pairs={{0,8},{8,0},{16,24},{24,16},{1,9},{9,1},{17,25},{25,17},{2,10},{10... | collective-permute-start | bytes 1572872 | tf_op jit(solution)/shard_map/ppermute | solution.py:22
  348.8 5.3 %copy-start.14 = (bf16[1,64,4096]{2,1,0:T(8,128)(2,1)S(1)}, bf16[1,64,4096]{2,1,0:T(8,128)(2,1)}, u32[]{:S(2)}) copy-start(bf16[1,64,4096]{2,1,0:T(8,128)(2,1)} %stack.263) | copy-start | bytes 1572868
  354.3 24.8 %collective-permute-start.23 = (bf16[2,64,4096]{2,1,0:T(8,128)(2,1)S(1)}, bf16[2,64,4096]{2,1,0:T(8,128)(2,1)S(1)}, u32[]{:S(2)}, u32[]{:S(2)}) collective-permute-start(bf16[2,64,4096]{2,1,0:T(8,128)(2,1)S(1)} %maximum_select_fusion.7), channel_id=1, source_target_pairs={{0,8},{8,0},{16,24},{24,16},{1,9},{9,1},{17,25},{25,17},{2,10},{10... | collective-permute-start | bytes 3145736 | tf_op jit(solution)/shard_map/ppermute | solution.py:22
  359.1 22.4 %collective-permute-start.21 = (bf16[2,64,4096]{2,1,0:T(8,128)(2,1)S(1)}, bf16[2,64,4096]{2,1,0:T(8,128)(2,1)S(1)}, u32[]{:S(2)}, u32[]{:S(2)}) collective-permute-start(bf16[2,64,4096]{2,1,0:T(8,128)(2,1)S(1)} %maximum_select_fusion.5), channel_id=1, source_target_pairs={{0,16},{8,24},{16,0},{24,8},{1,17},{9,25},{17,1},{25,9},{2,18},{10... | collective-permute-start | bytes 3145736 | tf_op jit(solution)/shard_map/ppermute | solution.py:22
Sparse Core Ops, SparseCore 0:
  9.6 84.7 all-gather.4
  96.0 29.3 all-gather.8
  127.0 63.5 all-gather.6
  192.1 80.6 all-gather.10

commit v2 on v0

v2 whole, which is shorter than its diff:
```python
import jax
import jax.numpy as jnp
from jax import lax
from jax.experimental.layout import Layout, with_layout_constraint
from jax.sharding import PartitionSpec as P

beta_first = 0.9
beta_second = 0.95
corr_first = 1.0 - 0.9**10
corr_second = 1.0 - 0.95**10
epsilon = 1e-08

bf16 = jnp.bfloat16
f32 = jnp.float32
chunks = 2


def rows_first(value):
    return with_layout_constraint(value, Layout(major_to_minor=tuple(range(value.ndim))))


def swap(block, count, mask):
    return lax.ppermute(block, "rows", [(i, i ^ mask) for i in range(count)])


def partners(count):
    return sorted(range(1, count), key=lambda mask: -mask.bit_count())


def scatter_sum(parts, axis):
    count = parts.shape[axis]
    me = lax.axis_index("rows")
    got = [
        swap(lax.dynamic_index_in_dim(parts, me ^ mask, axis, False), count, mask)
        for mask in partners(count)
    ]
    total = lax.dynamic_index_in_dim(parts, me, axis, False).astype(f32)
    for term in got:
        total = total + term.astype(f32)
    return total


def gather(block, count):
    me = lax.axis_index("rows")
    got = [(mask, swap(block, count, mask)) for mask in partners(count)]
    whole = lax.dynamic_update_index_in_dim(
        jnp.zeros((count,) + block.shape, block.dtype), block, me, 0
    )
    for mask, term in got:
        whole = lax.dynamic_update_index_in_dim(whole, term, me ^ mask, 0)
    return whole


def deal(parts):
    count = parts.shape[1]
    me = lax.axis_index("rows")
    own = lax.dynamic_index_in_dim(parts, me, 1, False)
    whole = lax.dynamic_update_index_in_dim(jnp.zeros((count,) + own.shape, own.dtype), own, me, 0)
    got = [
        (mask, swap(lax.dynamic_index_in_dim(parts, me ^ mask, 1, False), count, mask))
        for mask in partners(count)
    ]
    for mask, term in got:
        whole = lax.dynamic_update_index_in_dim(whole, term, me ^ mask, 0)
    return whole


def rotate_left(grad, left, later, rows, cols):
    depth, width = grad.shape
    sub = width // rows
    half = cols // 4
    index = lax.axis_index("cols")
    core, odd, pair = index & 1, (index >> 1) & 1, index >> 2
    left_other = lax.ppermute(left, "cols", [(i, i ^ 2) for i in range(cols)])
    moved = []
    for step in range(half):
        route = []
        for chip in range(half):
            for odd_chip in range(2):
                source, target = odd_chip * half + chip, 2 * ((chip + step) % half) + odd_chip
                route += [(2 * source + c, 2 * target + c) for c in range(2)]
        if moved:
            grad, moved[-1], left_other, later = lax.optimization_barrier(
                (grad, moved[-1], left_other, later)
            )
        moved.append(lax.ppermute(grad, "cols", route))
    moved[-1], later, left = lax.optimization_barrier((moved[-1], later, left))
    left_pair = jnp.concatenate([left_other, left], 1)
    whole = jnp.zeros((2, half, 2, sub, width), bf16)
    for step, block in enumerate(moved):
        other = lax.ppermute(block, "cols", [(i, i ^ 1) for i in range(cols)])
        both = jnp.where(core == 0, jnp.stack([block, other]), jnp.stack([other, block]))
        parts = lax.dot_general(
            both, left_pair, (((1,), (0,)), ((), ())), preferred_element_type=f32
        ).astype(bf16)
        parts = scatter_sum(parts.reshape(2, rows, sub, 2 * width), 1).astype(bf16)
        got = lax.ppermute(parts[..., :width], "cols", [(i, i ^ 2) for i in range(cols)])
        chip = lax.rem(pair + half - step, half)
        for half_index, value in ((odd, parts[..., width:]), (1 - odd, got)):
            whole = lax.dynamic_update_slice(
                whole, value[None, None], (half_index, chip, 0, 0, 0)
            )
    return whole.reshape(depth, width), later, left


def make_local(rows, cols):
    def local(forget_grad, left_basis, right_basis, first_moment, second_moment):
        depth, width = right_basis.shape
        per = cols // rows
        sub = width // rows
        mid = width // 2
        spans = (slice(0, mid), slice(mid, width))

        dealt = deal(right_basis.reshape(per, rows, sub, width)).reshape(depth, width)
        half, dealt, left = rotate_left(forget_grad, left_basis, dealt, rows, cols)
        basis = [lax.all_gather(dealt[:, span], "cols", axis=1, tiled=True) for span in spans]
        left_rows = lax.all_gather(left, "cols", axis=1, tiled=True)

        first = first_moment.reshape(per, 2, mid, width)
        second = second_moment.reshape(per, 2, mid, width)

        def turn(c, span):
            parts = lax.dot_general(
                basis[c], half[:, span], (((0,), (0,)), ((), ())), preferred_element_type=f32
            ).astype(bf16)
            return -scatter_sum(rows_first(parts).reshape(rows, per, mid, -1), 0)

        def normalize(c, span, value):
            new_first = beta_first * first[:, c, :, span] + (1.0 - beta_first) * value
            new_second = beta_second * second[:, c, :, span] + (1.0 - beta_second) * value * value
            normal = new_first / corr_first / (jnp.sqrt(new_second / corr_second) + epsilon)
            return gather(normal.astype(bf16), rows).reshape(cols * mid, -1)

        value = turn(0, slice(0, width))
        back = jnp.dot(basis[0], normalize(0, slice(0, width), value), preferred_element_type=f32)
        values = [turn(1, span) for span in spans]
        rotated = jnp.stack([value, jnp.concatenate(values, 2)], 1).reshape(depth, width)

        step_dir = None
        left_rows = left_rows.reshape(depth, cols, 2, mid)
        for c, span in enumerate(spans):
            normals = normalize(1, span, values[c])
            term = jnp.dot(basis[1], normals, preferred_element_type=f32) + back[:, span]
            term = rows_first(term.astype(bf16)).reshape(cols, sub, mid)
            term = lax.all_to_all(term, "cols", 0, 1).reshape(sub, cols * mid)
            term = lax.dot_general(
                left_rows[:, :, c].reshape(depth, cols * mid),
                gather(term, rows).reshape(width, cols * mid),
                (((1,), (1,)), ((), ())),
                preferred_element_type=f32,
            )
            step_dir = term if step_dir is None else step_dir + term
        step_dir = step_dir.astype(bf16)

        new_first = beta_first * first_moment + (1.0 - beta_first) * rotated
        new_second = beta_second * second_moment + (1.0 - beta_second) * rotated * rotated
        return (step_dir, new_first, new_second)

    return local


def solution(mesh):
    spec = P("rows", "cols")
    return jax.shard_map(
        make_local(mesh.shape["rows"], mesh.shape["cols"]),
        mesh=mesh,
        in_specs=(spec,) * 5,
        out_specs=(spec,) * 3,
        check_vma=False,
    )
```

time: 610 us -> 358 us (0.59)
  waiting for transfers between devices: 546 us -> 190 us
  starting transfers between devices: 0.5 us -> 68.4 us
  local copies, waits for them, and re-layouts: 2.29 us -> 35 us
  other arithmetic: 7.66 us -> 16.5 us
  matrix products: 39 us -> 32.5 us
    all_gather x6 -> x3, waiting for transfers between devices: 404 us -> 8.87 us  [the longest x2 8.85 us: local(): lax.all_gather(dealt[:, span], 'cols', axis=1, tiled=True)]
    ppermute x0 -> x40, waiting for transfers between devices: none -> 162 us  [the longest x33 111 us: swap(): return lax.ppermute(block, 'rows', [(i, i ^ mask) for i in range(count)])]
    reduce_scatter x2 -> x0, waiting for transfers between devices: 140 us -> none  [the longest x1 89.8 us: local(): lax.psum_scatter(lax.dot_general(back_cols, left_basis, (((1,), (1,)), ((...]
    ppermute x0 -> x40, starting transfers between devices: none -> 60.8 us  [the longest x33 43.2 us: swap(): return lax.ppermute(block, 'rows', [(i, i ^ mask) for i in range(count)])]
    all_to_all x0 -> x2, waiting for transfers between devices: none -> 19 us  [local(): term = lax.all_to_all(term, 'cols', 0, 1).reshape(sub, cols * mid)]
    dynamic_update_slice x0 -> x25, local copies, waits for them, and re-layouts: none -> 9.6 us  [the longest x15 8.37 us: gather(): whole = lax.dynamic_update_index_in_dim(whole, term, me ^ mask, 0)]
    all_to_all x0 -> x2, starting transfers between devices: none -> 7.45 us  [local(): term = lax.all_to_all(term, 'cols', 0, 1).reshape(sub, cols * mid)]
    dot_general x4 -> x10, matrix products: 39 us -> 32.5 us  [the longest x3 9.7 us: turn(): lax.dot_general(basis[c], half[:, span], (((0,), (0,)), ((), ())), prefer...]
  transfers between devices with their start and end apart: 8 -> 45, of which waited for: 8 -> 25; matrix products, arithmetic and copies ran while one was open for 1% -> 19% of each run, Pallas kernels for 0% -> 0%
where the time goes in v2:
time: 358 us; the launch traced here: 357 us
  waiting for transfers between devices  190 us (53%)
  starting transfers between devices  68.4 us (19%)
  local copies, waits for them, and re-layouts  35 us (10%)
  matrix products  32.5 us (9%)
  other arithmetic  16.5 us (5%)
  between operations  14.4 us (4%)
    ppermute x33, waiting for transfers between devices, swap(): return lax.ppermute(block, 'rows', [(i, i ^ mask) for i in range(count)])  111 us
    ppermute x33, starting transfers between devices, swap(): return lax.ppermute(block, 'rows', [(i, i ^ mask) for i in range(count)])  43.2 us
    ppermute x2, waiting for transfers between devices, rotate_left(): moved.append(lax.ppermute(grad, 'cols', route))  22.2 us
    all_to_all x2, waiting for transfers between devices, local(): term = lax.all_to_all(term, 'cols', 0, 1).reshape(sub, cols * mid)  19 us
    ppermute x2, waiting for transfers between devices, rotate_left(): lax.ppermute(parts[..., :width], 'cols', [(i, i ^ 2) for i in range(cols)])  16.7 us
    ppermute x2, starting transfers between devices, rotate_left(): moved.append(lax.ppermute(grad, 'cols', route))  12.7 us
    dot_general x3, matrix products, turn(): lax.dot_general(basis[c], half[:, span], (((0,), (0,)), ((), ())), prefer...  9.7 us
    dot_general x2, matrix products, rotate_left(): lax.dot_general(both, left_pair, (((1,), (0,)), ((), ())), preferred_elem...  9.41 us
  transfers between devices with their start and end apart: 45, of which 25 were waited for; matrix products, arithmetic and copies ran while one was open for 19% of the time, Pallas kernels for 0%

profile of v2, /device:TPU:0, one launch (start us, length us, event | category | flops | bytes accessed | tf_op | source)
XLA Modules:
  0.0 357.0 jit_solution(1411760959099288773)
XLA Ops:
  7.2 9.4 %collective-permute-start = (bf16[1024,512]{1,0:T(8,128)(2,1)}, bf16[1024,512]{1,0:T(8,128)(2,1)}, u32[]{:S(2)}, u32[]{:S(2)}) collective-permute-start(bf16[1024,512]{1,0:T(8,128)(2,1)} %param.5), channel_id=1, source_target_pairs={{0,0},{1,1},{4,2},{5,3},{2,4},{3,5},{6,6},{7,7},{8,8},{9,9},{12,10... | collective-permute-start | bytes 3145736 | tf_op jit(solution)/shard_map/ppermute | solution.py:86
  17.8 4.0 %collective-permute-start.2 = (bf16[2,128,512]{2,1,0:T(8,128)(2,1)S(1)}, bf16[2,128,512]{2,1,0:T(8,128)(2,1)S(1)}, u32[]{:S(2)}, u32[]{:S(2)}) collective-permute-start(bf16[2,128,512]{2,1,0:T(8,128)(2,1)S(1)} %get-tuple-element.48), channel_id=1, source_target_pairs={{0,24},{8,16},{16,8},{24,0},{1,25},{9,17},{17,9},{25,1},{2,26},{10... | collective-permute-start | bytes 786440 | tf_op jit(solution)/shard_map/ppermute | solution.py:23
  23.5 5.5 %collective-permute-done.2 = bf16[2,128,512]{2,1,0:T(8,128)(2,1)S(1)} collective-permute-done((bf16[2,128,512]{2,1,0:T(8,128)(2,1)S(1)}, bf16[2,128,512]{2,1,0:T(8,128)(2,1)S(1)}, u32[]{:S(2)}, u32[]{:S(2)}) %collective-permute-start.2) | collective-permute-done | bytes 262176 | tf_op jit(solution)/shard_map/ppermute | solution.py:23
  29.0 5.0 %collective-permute-done.3 = bf16[2,128,512]{2,1,0:T(8,128)(2,1)S(1)} collective-permute-done((bf16[2,128,512]{2,1,0:T(8,128)(2,1)S(1)}, bf16[2,128,512]{2,1,0:T(8,128)(2,1)S(1)}, u32[]{:S(2)}, u32[]{:S(2)}) %collective-permute-start.3) | collective-permute-done | bytes 262176 | tf_op jit(solution)/shard_map/ppermute | solution.py:23
  34.1 8.4 %collective-permute-done.1 = bf16[1024,512]{1,0:T(8,128)(2,1)} collective-permute-done((bf16[1024,512]{1,0:T(8,128)(2,1)}, bf16[1024,512]{1,0:T(8,128)(2,1)}, u32[]{:S(2)}, u32[]{:S(2)}) %collective-permute-start.1) | collective-permute-done | bytes 1048608 | tf_op jit(solution)/shard_map/ppermute | solution.py:74
  42.5 3.3 collective-permute-start.5
  45.7 22.2 %collective-permute-done.5 = bf16[1024,512]{1,0:T(8,128)(2,1)S(1)} collective-permute-done((bf16[1024,512]{1,0:T(8,128)(2,1)}, bf16[1024,512]{1,0:T(8,128)(2,1)S(1)}, u32[]{:S(2)}, u32[]{:S(2)}) %collective-permute-start.5) | collective-permute-done | bytes 1048608 | tf_op jit(solution)/shard_map/ppermute | solution.py:86
  71.8 3.1 collective-permute-done.6
  74.9 5.1 %fusion.17 = bf16[2,512,1024]{2,1,0:T(8,128)(2,1)S(1)} fusion(bf16[1,1024,512]{2,1,0:T(8,128)(2,1)} %bitcast.14, bf16[1,1024,512]{2,1,0:T(8,128)(2,1)} %bitcast.13, pred[]{:T(512)S(6)} %eq.4, bf16[1024,512]{1,0:T(8,128)(2,1)S(1)} %copy-done.12, bf16[1024,512]{1,0:T(8,128)(2,1)} %collective-permute-done.1), kind=kOutput, calls=%fused_computation.27 | convolution fusion | flops 2155872256 | bytes 6291457 | tf_op jit(solution)/shard_map/dot_general | solution.py:93
  81.2 2.4 collective-permute-start.7
  85.6 4.3 %fusion.16 = bf16[2,512,1024]{2,1,0:T(8,128)(2,1)S(1)} fusion(bf16[1,1024,512]{2,1,0:T(8,128)(2,1)} %bitcast.348, bf16[1,1024,512]{2,1,0:T(8,128)(2,1)S(1)} %bitcast.347, pred[]{:T(512)S(6)} %eq.4, bf16[1024,512]{1,0:T(8,128)(2,1)S(1)} %copy-done.12, bf16[1024,512]{1,0:T(8,128)(2,1)} %collective-permute-done.1), kind=kOutput, calls=%fused_computation.26 | convolution fusion | flops 2155872256 | bytes 6291457 | tf_op jit(solution)/shard_map/dot_general | solution.py:93
  91.2 2.4 collective-permute-start.12
  94.1 2.8 collective-permute-done.7
  99.1 9.1 %collective-permute-done.8 = bf16[2,128,1024]{2,1,0:T(8,128)(2,1)} collective-permute-done((bf16[2,128,1024]{2,1,0:T(8,128)(2,1)}, bf16[2,128,1024]{2,1,0:T(8,128)(2,1)}, u32[]{:S(2)}, u32[]{:S(2)}) %collective-permute-start.8) | collective-permute-done | bytes 524320 | tf_op jit(solution)/shard_map/ppermute | solution.py:23
  108.3 1.9 fusion.39
  110.2 2.2 collective-permute-start.10
  112.5 7.0 %collective-permute-done.12 = bf16[2,128,1024]{2,1,0:T(8,128)(2,1)} collective-permute-done((bf16[2,128,1024]{2,1,0:T(8,128)(2,1)}, bf16[2,128,1024]{2,1,0:T(8,128)(2,1)}, u32[]{:S(2)}, u32[]{:S(2)}) %collective-permute-start.12) | collective-permute-done | bytes 524320 | tf_op jit(solution)/shard_map/ppermute | solution.py:23
  119.5 10.4 %collective-permute-done.13 = bf16[2,128,1024]{2,1,0:T(8,128)(2,1)} collective-permute-done((bf16[2,128,1024]{2,1,0:T(8,128)(2,1)}, bf16[2,128,1024]{2,1,0:T(8,128)(2,1)}, u32[]{:S(2)}, u32[]{:S(2)}) %collective-permute-start.13) | collective-permute-done | bytes 524320 | tf_op jit(solution)/shard_map/ppermute | solution.py:23
  129.9 1.7 fusion.36
  131.7 2.2 collective-permute-start.15
  134.0 16.7 %collective-permute-done.15 = bf16[2,128,512]{2,1,0:T(8,128)(2,1)S(1)} collective-permute-done((bf16[2,128,512]{2,1,0:T(8,128)(2,1)S(1)}, bf16[2,128,512]{2,1,0:T(8,128)(2,1)S(1)}, u32[]{:S(2)}, u32[]{:S(2)}) %collective-permute-start.15) | collective-permute-done | bytes 262176 | tf_op jit(solution)/shard_map/ppermute | solution.py:97
  150.7 3.7 %convolution_convert_fusion.2 = bf16[2048,256]{1,0:T(8,128)(2,1)S(1)} fusion(bf16[1024,2048]{1,0:T(8,128)(2,1)} %all-gather.6.cloned.1.call-done, bf16[1024,512]{1,0:T(8,128)(2,1)S(1)} %bitcast.338), kind=kOutput, calls=%fused_computation.3 | convolution fusion | flops 1074266112 | bytes 5767168 | tf_op jit(solution)/shard_map/dot_general | solution.py:123
  155.4 2.3 collective-permute-start.16
  162.1 2.3 collective-permute-start.31
  164.4 8.8 %all-gather.8.cloned.1.call-done = bf16[1024,2048]{1,0:T(8,128)(2,1)} async-done(((bf16[1024,256]{1,0:T(8,128)(2,1)}), bf16[1024,2048]{1,0:T(8,128)(2,1)}) %all-gather.8.cloned.1.call-update) | async-done | bytes 4194320 | tf_op jit(solution)/shard_map/all_gather | solution.py:116
  173.3 4.6 %convolution_convert_fusion = bf16[2048,512]{1,0:T(8,128)(2,1)S(1)} fusion(bf16[1024,2048]{1,0:T(8,128)(2,1)} %all-gather.8.cloned.1.call-done, bf16[1024,512]{1,0:T(8,128)(2,1)S(1)} %bitcast.340), kind=kOutput, calls=%fused_computation.1 | convolution fusion | flops 2148532224 | bytes 7340032 | tf_op jit(solution)/shard_map/dot_general | solution.py:123
  178.3 2.5 collective-permute-start.22
  184.9 2.5 bitcast_dynamic-update-slice_fusion.14
  187.4 22.9 %collective-permute-done.32 = bf16[2,256,256]{2,1,0:T(8,128)(2,1)S(1)} collective-permute-done((bf16[2,256,256]{2,1,0:T(8,128)(2,1)S(1)}, bf16[2,256,256]{2,1,0:T(8,128)(2,1)S(1)}, u32[]{:S(2)}, u32[]{:S(2)}) %collective-permute-start.32) | collective-permute-done | bytes 262176 | tf_op jit(solution)/shard_map/ppermute | solution.py:23
  212.3 2.4 bitcast_dynamic-update-slice_fusion.10
  221.1 4.0 %collective-permute-done.20 = bf16[2,256,256]{2,1,0:T(8,128)(2,1)S(1)} collective-permute-done((bf16[2,256,256]{2,1,0:T(8,128)(2,1)S(1)}, bf16[2,256,256]{2,1,0:T(8,128)(2,1)S(1)}, u32[]{:S(2)}, u32[]{:S(2)}) %collective-permute-start.20) | collective-permute-done | bytes 262176 | tf_op jit(solution)/shard_map/ppermute | solution.py:23
  225.1 2.4 collective-permute-start.25
  227.5 2.1 collective-permute-done.21
  232.7 15.8 %collective-permute-done.25 = bf16[2,256,512]{2,1,0:T(8,128)(2,1)S(1)} collective-permute-done((bf16[2,256,512]{2,1,0:T(8,128)(2,1)S(1)}, bf16[2,256,512]{2,1,0:T(8,128)(2,1)S(1)}, u32[]{:S(2)}, u32[]{:S(2)}) %collective-permute-start.25) | collective-permute-done | bytes 524320 | tf_op jit(solution)/shard_map/ppermute | solution.py:23
  248.6 8.8 %collective-permute-done.26 = bf16[2,256,512]{2,1,0:T(8,128)(2,1)S(1)} collective-permute-done((bf16[2,256,512]{2,1,0:T(8,128)(2,1)S(1)}, bf16[2,256,512]{2,1,0:T(8,128)(2,1)S(1)}, u32[]{:S(2)}, u32[]{:S(2)}) %collective-permute-start.26) | collective-permute-done | bytes 524320 | tf_op jit(solution)/shard_map/ppermute | solution.py:23
  258.3 2.3 fusion.85
  263.0 3.7 %all-to-all-start = ((bf16[8,128,1,256]{1,3,2,0:T(8,128)(2,1)}), bf16[8,128,1,256]{1,3,2,0:T(8,128)(2,1)S(1)}, u32[]{:S(2)}, u32[]{:S(2)}) async-start(bf16[8,128,1,256]{1,3,2,0:T(8,128)(2,1)} %copy.55), calls=%async_computation | async-start | bytes 1048576 | tf_op jit(solution)/shard_map/all_to_all | solution.py:145
  267.5 1.7 bitcast_dynamic-update-slice_fusion.7
  269.1 4.0 %fusion.19 = bf16[1024,256]{1,0:T(8,128)(2,1)S(1)} fusion(bf16[1024,2048]{1,0:T(8,128)(2,1)} %all-gather.6.cloned.1.call-done, bf16[2048,256]{1,0:T(8,128)(2,1)} %bitcast.337, f32[1024,512]{1,0:T(8,128)} %copy-done.24), kind=kOutput, calls=%fused_computation.32 | convolution fusion | flops 1074266112 | bytes 6815744 | tf_op jit(solution)/shard_map/dot_general | solution.py:143
  274.2 7.9 %all-to-all-done = bf16[8,128,1,256]{1,3,2,0:T(8,128)(2,1)S(1)} async-done(((bf16[8,128,1,256]{1,3,2,0:T(8,128)(2,1)}), bf16[8,128,1,256]{1,3,2,0:T(8,128)(2,1)S(1)}, u32[]{:S(2)}, u32[]{:S(2)}) %all-to-all-start) | async-done | bytes 524320 | tf_op jit(solution)/shard_map/all_to_all | solution.py:145
  282.1 3.7 %all-to-all-start.1 = ((bf16[8,128,1,256]{1,3,2,0:T(8,128)(2,1)}), bf16[8,128,1,256]{1,3,2,0:T(8,128)(2,1)S(1)}, u32[]{:S(2)}, u32[]{:S(2)}) async-start(bf16[8,128,1,256]{1,3,2,0:T(8,128)(2,1)} %copy.62), calls=%async_computation.1 | async-start | bytes 1048576 | tf_op jit(solution)/shard_map/all_to_all | solution.py:145
  289.8 11.1 %all-to-all-done.1 = bf16[8,128,1,256]{1,3,2,0:T(8,128)(2,1)S(1)} async-done(((bf16[8,128,1,256]{1,3,2,0:T(8,128)(2,1)}), bf16[8,128,1,256]{1,3,2,0:T(8,128)(2,1)S(1)}, u32[]{:S(2)}, u32[]{:S(2)}) %all-to-all-start.1) | async-done | bytes 524320 | tf_op jit(solution)/shard_map/all_to_all | solution.py:145
  303.4 5.1 %fusion = (f32[1024,512]{1,0:T(8,128)}, f32[1024,512]{1,0:T(8,128)}) fusion(f32[2,2,256,512]{3,2,1,0:T(8,128)S(1)} %copy.67, f32[1024,512]{1,0:T(8,128)} %param.9, f32[1024,512]{1,0:T(8,128)} %param.8), kind=kLoop, calls=%fused_computation.4 | loop fusion | flops 3670016 | bytes 10485760 | tf_op jit(solution)/shard_map/add | solution.py:156
  319.9 8.6 %collective-permute-done.29 = bf16[128,2048]{0,1:T(8,128)(2,1)} collective-permute-done((bf16[128,2048]{0,1:T(8,128)(2,1)S(1)}, bf16[128,2048]{0,1:T(8,128)(2,1)}, u32[]{:S(2)}, u32[]{:S(2)}) %collective-permute-start.29) | collective-permute-done | bytes 524320 | tf_op jit(solution)/shard_map/ppermute | solution.py:23
  332.7 5.8 %collective-permute-done.38 = bf16[128,2048]{1,0:T(8,128)(2,1)} collective-permute-done((bf16[128,2048]{1,0:T(8,128)(2,1)}, bf16[128,2048]{1,0:T(8,128)(2,1)}, u32[]{:S(2)}, u32[]{:S(2)}) %collective-permute-start.38) | collective-permute-done | bytes 524320 | tf_op jit(solution)/shard_map/ppermute | solution.py:23
  340.7 4.0 %fusion.83 = (bf16[1024,8,1,256]{0,3,2,1:T(8,128)(2,1)S(1)}, bf16[1024,8,1,256]{0,3,2,1:T(8,128)(2,1)S(1)}) fusion(bf16[1024,8,2,256]{0,3,2,1:T(8,128)(2,1)} %bitcast.308), kind=kLoop, calls=%fused_computation.151 | loop fusion | bytes 16777216 | tf_op jit(solution)/shard_map/slice | solution.py:147
  344.7 2.4 fusion.86
  347.1 3.4 add_convert_fusion
  (166 shorter events, 64.8 us)
Async XLA Ops:
  7.2 143.5 %all-gather.6.cloned.1.call-start = ((), (), s32[]{:S(2)}) async-start(), calls=%async_computation.3 | async-start | bytes 4718592 | tf_op jit(solution)/shard_map/all_gather | solution.py:116
  7.2 26.8 %collective-permute-start = (bf16[1024,512]{1,0:T(8,128)(2,1)}, bf16[1024,512]{1,0:T(8,128)(2,1)}, u32[]{:S(2)}, u32[]{:S(2)}) collective-permute-start(bf16[1024,512]{1,0:T(8,128)(2,1)} %param.5), channel_id=1, source_target_pairs={{0,0},{1,1},{4,2},{5,3},{2,4},{3,5},{6,6},{7,7},{8,8},{9,9},{12,10... | collective-permute-start | bytes 3145736 | tf_op jit(solution)/shard_map/ppermute | solution.py:86
  16.6 25.8 %collective-permute-start.1 = (bf16[1024,512]{1,0:T(8,128)(2,1)}, bf16[1024,512]{1,0:T(8,128)(2,1)}, u32[]{:S(2)}, u32[]{:S(2)}) collective-permute-start(bf16[1024,512]{1,0:T(8,128)(2,1)} %param.6), channel_id=1, source_target_pairs={{0,2},{1,3},{2,0},{3,1},{4,6},{5,7},{6,4},{7,5},{8,10},{9,11},{10,... | collective-permute-start | bytes 3145736 | tf_op jit(solution)/shard_map/ppermute | solution.py:74
  17.8 11.1 %collective-permute-start.2 = (bf16[2,128,512]{2,1,0:T(8,128)(2,1)S(1)}, bf16[2,128,512]{2,1,0:T(8,128)(2,1)S(1)}, u32[]{:S(2)}, u32[]{:S(2)}) collective-permute-start(bf16[2,128,512]{2,1,0:T(8,128)(2,1)S(1)} %get-tuple-element.48), channel_id=1, source_target_pairs={{0,24},{8,16},{16,8},{24,0},{1,25},{9,17},{17,9},{25,1},{2,26},{10... | collective-permute-start | bytes 786440 | tf_op jit(solution)/shard_map/ppermute | solution.py:23
  21.8 12.2 %collective-permute-start.3 = (bf16[2,128,512]{2,1,0:T(8,128)(2,1)S(1)}, bf16[2,128,512]{2,1,0:T(8,128)(2,1)S(1)}, u32[]{:S(2)}, u32[]{:S(2)}) collective-permute-start(bf16[2,128,512]{2,1,0:T(8,128)(2,1)S(1)} %get-tuple-element.47), channel_id=1, source_target_pairs={{0,8},{8,0},{16,24},{24,16},{1,9},{9,1},{17,25},{25,17},{2,10},{10... | collective-permute-start | bytes 786440 | tf_op jit(solution)/shard_map/ppermute | solution.py:23
  22.3 11.7 %collective-permute-start.4 = (bf16[2,128,512]{2,1,0:T(8,128)(2,1)S(1)}, bf16[2,128,512]{2,1,0:T(8,128)(2,1)S(1)}, u32[]{:S(2)}, u32[]{:S(2)}) collective-permute-start(bf16[2,128,512]{2,1,0:T(8,128)(2,1)S(1)} %get-tuple-element.46), channel_id=1, source_target_pairs={{0,16},{8,24},{16,0},{24,8},{1,17},{9,25},{17,1},{25,9},{2,18},{10... | collective-permute-start | bytes 786440 | tf_op jit(solution)/shard_map/ppermute | solution.py:23
  29.0 40.9 %copy-start.12 = (bf16[1024,512]{1,0:T(8,128)(2,1)S(1)}, bf16[1024,512]{1,0:T(8,128)(2,1)}, u32[]{:S(2)}) copy-start(bf16[1024,512]{1,0:T(8,128)(2,1)} %param.6) | copy-start | bytes 3145732
  42.5 25.4 %collective-permute-start.5 = (bf16[1024,512]{1,0:T(8,128)(2,1)}, bf16[1024,512]{1,0:T(8,128)(2,1)S(1)}, u32[]{:S(2)}, u32[]{:S(2)}) collective-permute-start(bf16[1024,512]{1,0:T(8,128)(2,1)} %param.5), channel_id=1, source_target_pairs={{0,4},{1,5},{4,6},{5,7},{2,0},{3,1},{6,2},{7,3},{8,12},{9,13},{12,... | collective-permute-start | bytes 3145736 | tf_op jit(solution)/shard_map/ppermute | solution.py:86
  69.1 104.2 %all-gather.8.cloned.1.call-start = ((), (), s32[]{:S(2)}) async-start(), calls=%async_computation.4 | async-start | bytes 4718592 | tf_op jit(solution)/shard_map/all_gather | solution.py:116
  69.8 270.9 %all-gather.4.cloned.1.call-start = ((), (), s32[]{:S(2)}) async-start(), calls=%async_computation.2 | async-start | bytes 9437184 | tf_op jit(solution)/shard_map/all_gather | solution.py:117
  71.2 3.7 %collective-permute-start.6 = (bf16[1024,512]{1,0:T(8,128)(2,1)}, bf16[1024,512]{1,0:T(8,128)(2,1)}, u32[]{:S(2)}, u32[]{:S(2)}) collective-permute-start(bf16[1024,512]{1,0:T(8,128)(2,1)} %collective-permute-done), channel_id=1, source_target_pairs={{0,1},{1,0},{2,3},{3,2},{4,5},{5,4},{6,7},{7,6},{8,9},{9,8},{10,11... | collective-permute-start | bytes 3145736 | tf_op jit(solution)/shard_map/ppermute | solution.py:91
  71.3 13.4 %collective-permute-start.11 = (bf16[1024,512]{1,0:T(8,128)(2,1)S(1)}, bf16[1024,512]{1,0:T(8,128)(2,1)S(1)}, u32[]{:S(2)}, u32[]{:S(2)}) collective-permute-start(bf16[1024,512]{1,0:T(8,128)(2,1)S(1)} %collective-permute-done.5), channel_id=1, source_target_pairs={{0,1},{1,0},{2,3},{3,2},{4,5},{5,4},{6,7},{7,6},{8,9},{9,8},{10,11... | collective-permute-start | bytes 3145736 | tf_op jit(solution)/shard_map/ppermute | solution.py:91
  81.2 15.7 %collective-permute-start.7 = (bf16[2,128,1024]{2,1,0:T(8,128)(2,1)S(1)}, bf16[2,128,1024]{2,1,0:T(8,128)(2,1)S(1)}, u32[]{:S(2)}, u32[]{:S(2)}) collective-permute-start(bf16[2,128,1024]{2,1,0:T(8,128)(2,1)S(1)} %get-tuple-element.35), channel_id=1, source_target_pairs={{0,24},{8,16},{16,8},{24,0},{1,25},{9,17},{17,9},{25,1},{2,26},{10... | collective-permute-start | bytes 1572872 | tf_op jit(solution)/shard_map/ppermute | solution.py:23
  83.6 24.7 %collective-permute-start.8 = (bf16[2,128,1024]{2,1,0:T(8,128)(2,1)}, bf16[2,128,1024]{2,1,0:T(8,128)(2,1)}, u32[]{:S(2)}, u32[]{:S(2)}) collective-permute-start(bf16[2,128,1024]{2,1,0:T(8,128)(2,1)} %get-tuple-element.37), channel_id=1, source_target_pairs={{0,8},{8,0},{16,24},{24,16},{1,9},{9,1},{17,25},{25,17},{2,10},{10... | collective-permute-start | bytes 1572872 | tf_op jit(solution)/shard_map/ppermute | solution.py:23
  84.1 24.2 %collective-permute-start.9 = (bf16[2,128,1024]{2,1,0:T(8,128)(2,1)}, bf16[2,128,1024]{2,1,0:T(8,128)(2,1)}, u32[]{:S(2)}, u32[]{:S(2)}) collective-permute-start(bf16[2,128,1024]{2,1,0:T(8,128)(2,1)} %get-tuple-element.36), channel_id=1, source_target_pairs={{0,16},{8,24},{16,0},{24,8},{1,17},{9,25},{17,1},{25,9},{2,18},{10... | collective-permute-start | bytes 1572872 | tf_op jit(solution)/shard_map/ppermute | solution.py:23
  91.2 28.3 %collective-permute-start.12 = (bf16[2,128,1024]{2,1,0:T(8,128)(2,1)}, bf16[2,128,1024]{2,1,0:T(8,128)(2,1)}, u32[]{:S(2)}, u32[]{:S(2)}) collective-permute-start(bf16[2,128,1024]{2,1,0:T(8,128)(2,1)} %get-tuple-element.32), channel_id=1, source_target_pairs={{0,24},{8,16},{16,8},{24,0},{1,25},{9,17},{17,9},{25,1},{2,26},{10... | collective-permute-start | bytes 1572872 | tf_op jit(solution)/shard_map/ppermute | solution.py:23
  93.5 36.4 %collective-permute-start.13 = (bf16[2,128,1024]{2,1,0:T(8,128)(2,1)}, bf16[2,128,1024]{2,1,0:T(8,128)(2,1)}, u32[]{:S(2)}, u32[]{:S(2)}) collective-permute-start(bf16[2,128,1024]{2,1,0:T(8,128)(2,1)} %get-tuple-element.34), channel_id=1, source_target_pairs={{0,8},{8,0},{16,24},{24,16},{1,9},{9,1},{17,25},{25,17},{2,10},{10... | collective-permute-start | bytes 1572872 | tf_op jit(solution)/shard_map/ppermute | solution.py:23
  97.7 32.3 %collective-permute-start.14 = (bf16[2,128,1024]{2,1,0:T(8,128)(2,1)}, bf16[2,128,1024]{2,1,0:T(8,128)(2,1)}, u32[]{:S(2)}, u32[]{:S(2)}) collective-permute-start(bf16[2,128,1024]{2,1,0:T(8,128)(2,1)} %get-tuple-element.33), channel_id=1, source_target_pairs={{0,16},{8,24},{16,0},{24,8},{1,17},{9,25},{17,1},{25,9},{2,18},{10... | collective-permute-start | bytes 1572872 | tf_op jit(solution)/shard_map/ppermute | solution.py:23
  110.2 23.7 %collective-permute-start.10 = (bf16[2,128,512]{2,1,0:T(8,128)(2,1)S(1)}, bf16[2,128,512]{2,1,0:T(8,128)(2,1)S(1)}, u32[]{:S(2)}, u32[]{:S(2)}) collective-permute-start(bf16[2,128,512]{2,1,0:T(8,128)(2,1)S(1)} %slice.75), channel_id=1, source_target_pairs={{0,2},{1,3},{2,0},{3,1},{4,6},{5,7},{6,4},{7,5},{8,10},{9,11},{10,... | collective-permute-start | bytes 786440 | tf_op jit(solution)/shard_map/ppermute | solution.py:97
  131.7 19.0 %collective-permute-start.15 = (bf16[2,128,512]{2,1,0:T(8,128)(2,1)S(1)}, bf16[2,128,512]{2,1,0:T(8,128)(2,1)S(1)}, u32[]{:S(2)}, u32[]{:S(2)}) collective-permute-start(bf16[2,128,512]{2,1,0:T(8,128)(2,1)S(1)} %slice.77), channel_id=1, source_target_pairs={{0,2},{1,3},{2,0},{3,1},{4,6},{5,7},{6,4},{7,5},{8,10},{9,11},{10,... | collective-permute-start | bytes 786440 | tf_op jit(solution)/shard_map/ppermute | solution.py:97
  155.4 25.4 %collective-permute-start.16 = (bf16[2,256,256]{2,1,0:T(8,128)(2,1)}, bf16[2,256,256]{2,1,0:T(8,128)(2,1)}, u32[]{:S(2)}, u32[]{:S(2)}) collective-permute-start(bf16[2,256,256]{2,1,0:T(8,128)(2,1)} %get-tuple-element.38), channel_id=1, source_target_pairs={{0,24},{8,16},{16,8},{24,0},{1,25},{9,17},{17,9},{25,1},{2,26},{10... | collective-permute-start | bytes 786440 | tf_op jit(solution)/shard_map/ppermute | solution.py:23
  157.7 23.6 %collective-permute-start.17 = (bf16[2,256,256]{2,1,0:T(8,128)(2,1)}, bf16[2,256,256]{2,1,0:T(8,128)(2,1)}, u32[]{:S(2)}, u32[]{:S(2)}) collective-permute-start(bf16[2,256,256]{2,1,0:T(8,128)(2,1)} %get-tuple-element.40), channel_id=1, source_target_pairs={{0,8},{8,0},{16,24},{24,16},{1,9},{9,1},{17,25},{25,17},{2,10},{10... | collective-permute-start | bytes 786440 | tf_op jit(solution)/shard_map/ppermute | solution.py:23
  158.2 23.6 %collective-permute-start.18 = (bf16[2,256,256]{2,1,0:T(8,128)(2,1)}, bf16[2,256,256]{2,1,0:T(8,128)(2,1)}, u32[]{:S(2)}, u32[]{:S(2)}) collective-permute-start(bf16[2,256,256]{2,1,0:T(8,128)(2,1)} %get-tuple-element.39), channel_id=1, source_target_pairs={{0,16},{8,24},{16,0},{24,8},{1,17},{9,25},{17,1},{25,9},{2,18},{10... | collective-permute-start | bytes 786440 | tf_op jit(solution)/shard_map/ppermute | solution.py:23
  162.1 21.2 %collective-permute-start.31 = (bf16[2,256,256]{2,1,0:T(8,128)(2,1)}, bf16[2,256,256]{2,1,0:T(8,128)(2,1)}, u32[]{:S(2)}, u32[]{:S(2)}) collective-permute-start(bf16[2,256,256]{2,1,0:T(8,128)(2,1)} %get-tuple-element.43), channel_id=1, source_target_pairs={{0,24},{8,16},{16,8},{24,0},{1,25},{9,17},{17,9},{25,1},{2,26},{10... | collective-permute-start | bytes 786440 | tf_op jit(solution)/shard_map/ppermute | solution.py:23
  178.3 36.5 %collective-permute-start.22 = (bf16[2,256,512]{2,1,0:T(8,128)(2,1)S(1)}, bf16[2,256,512]{2,1,0:T(8,128)(2,1)S(1)}, u32[]{:S(2)}, u32[]{:S(2)}) collective-permute-start(bf16[2,256,512]{2,1,0:T(8,128)(2,1)S(1)} %get-tuple-element.29), channel_id=1, source_target_pairs={{0,24},{8,16},{16,8},{24,0},{1,25},{9,17},{17,9},{25,1},{2,26},{10... | collective-permute-start | bytes 1572872 | tf_op jit(solution)/shard_map/ppermute | solution.py:23
  180.7 35.5 %collective-permute-start.23 = (bf16[2,256,512]{2,1,0:T(8,128)(2,1)S(1)}, bf16[2,256,512]{2,1,0:T(8,128)(2,1)S(1)}, u32[]{:S(2)}, u32[]{:S(2)}) collective-permute-start(bf16[2,256,512]{2,1,0:T(8,128)(2,1)S(1)} %get-tuple-element.31), channel_id=1, source_target_pairs={{0,8},{8,0},{16,24},{24,16},{1,9},{9,1},{17,25},{25,17},{2,10},{10... | collective-permute-start | bytes 1572872 | tf_op jit(solution)/shard_map/ppermute | solution.py:23
  181.3 36.4 %collective-permute-start.24 = (bf16[2,256,512]{2,1,0:T(8,128)(2,1)S(1)}, bf16[2,256,512]{2,1,0:T(8,128)(2,1)S(1)}, u32[]{:S(2)}, u32[]{:S(2)}) collective-permute-start(bf16[2,256,512]{2,1,0:T(8,128)(2,1)S(1)} %get-tuple-element.30), channel_id=1, source_target_pairs={{0,16},{8,24},{16,0},{24,8},{1,17},{9,25},{17,1},{25,9},{2,18},{10... | collective-permute-start | bytes 1572872 | tf_op jit(solution)/shard_map/ppermute | solution.py:23
  181.8 28.4 %collective-permute-start.32 = (bf16[2,256,256]{2,1,0:T(8,128)(2,1)S(1)}, bf16[2,256,256]{2,1,0:T(8,128)(2,1)S(1)}, u32[]{:S(2)}, u32[]{:S(2)}) collective-permute-start(bf16[2,256,256]{2,1,0:T(8,128)(2,1)S(1)} %copy-done.17), channel_id=1, source_target_pairs={{0,8},{8,0},{16,24},{24,16},{1,9},{9,1},{17,25},{25,17},{2,10},{10... | collective-permute-start | bytes 786440 | tf_op jit(solution)/shard_map/ppermute | solution.py:23
  183.3 28.4 %collective-permute-start.33 = (bf16[2,256,256]{2,1,0:T(8,128)(2,1)S(1)}, bf16[2,256,256]{2,1,0:T(8,128)(2,1)S(1)}, u32[]{:S(2)}, u32[]{:S(2)}) collective-permute-start(bf16[2,256,256]{2,1,0:T(8,128)(2,1)S(1)} %get-tuple-element.44), channel_id=1, source_target_pairs={{0,16},{8,24},{16,0},{24,8},{1,17},{9,25},{17,1},{25,9},{2,18},{10... | collective-permute-start | bytes 786440 | tf_op jit(solution)/shard_map/ppermute | solution.py:23
  210.3 10.1 %collective-permute-start.19 = (bf16[2,256,256]{2,1,0:T(8,128)(2,1)S(1)}, bf16[2,256,256]{2,1,0:T(8,128)(2,1)S(1)}, u32[]{:S(2)}, u32[]{:S(2)}) collective-permute-start(bf16[2,256,256]{2,1,0:T(8,128)(2,1)S(1)} %get-tuple-element.18), channel_id=1, source_target_pairs={{0,24},{8,16},{16,8},{24,0},{1,25},{9,17},{17,9},{25,1},{2,26},{10... | collective-permute-start | bytes 786440 | tf_op jit(solution)/shard_map/ppermute | solution.py:23
  211.7 13.3 %collective-permute-start.20 = (bf16[2,256,256]{2,1,0:T(8,128)(2,1)S(1)}, bf16[2,256,256]{2,1,0:T(8,128)(2,1)S(1)}, u32[]{:S(2)}, u32[]{:S(2)}) collective-permute-start(bf16[2,256,256]{2,1,0:T(8,128)(2,1)S(1)} %get-tuple-element.18), channel_id=1, source_target_pairs={{0,8},{8,0},{16,24},{24,16},{1,9},{9,1},{17,25},{25,17},{2,10},{10... | collective-permute-start | bytes 786440 | tf_op jit(solution)/shard_map/ppermute | solution.py:23
  214.7 14.9 %collective-permute-start.21 = (bf16[2,256,256]{2,1,0:T(8,128)(2,1)S(1)}, bf16[2,256,256]{2,1,0:T(8,128)(2,1)S(1)}, u32[]{:S(2)}, u32[]{:S(2)}) collective-permute-start(bf16[2,256,256]{2,1,0:T(8,128)(2,1)S(1)} %get-tuple-element.18), channel_id=1, source_target_pairs={{0,16},{8,24},{16,0},{24,8},{1,17},{9,25},{17,1},{25,9},{2,18},{10... | collective-permute-start | bytes 786440 | tf_op jit(solution)/shard_map/ppermute | solution.py:23
  216.3 15.4 %collective-permute-start.34 = (bf16[2,256,256]{2,1,0:T(8,128)(2,1)}, bf16[2,256,256]{2,1,0:T(8,128)(2,1)S(1)}, u32[]{:S(2)}, u32[]{:S(2)}) collective-permute-start(bf16[2,256,256]{2,1,0:T(8,128)(2,1)} %get-tuple-element.23), channel_id=1, source_target_pairs={{0,24},{8,16},{16,8},{24,0},{1,25},{9,17},{17,9},{25,1},{2,26},{10... | collective-permute-start | bytes 786440 | tf_op jit(solution)/shard_map/ppermute | solution.py:23
  217.7 49.0 %collective-permute-start.35 = (bf16[2,256,256]{2,1,0:T(8,128)(2,1)}, bf16[2,256,256]{2,1,0:T(8,128)(2,1)S(1)}, u32[]{:S(2)}, u32[]{:S(2)}) collective-permute-start(bf16[2,256,256]{2,1,0:T(8,128)(2,1)} %get-tuple-element.23), channel_id=1, source_target_pairs={{0,8},{8,0},{16,24},{24,16},{1,9},{9,1},{17,25},{25,17},{2,10},{10... | collective-permute-start | bytes 786440 | tf_op jit(solution)/shard_map/ppermute | solution.py:23
  220.4 47.1 %collective-permute-start.36 = (bf16[2,256,256]{2,1,0:T(8,128)(2,1)}, bf16[2,256,256]{2,1,0:T(8,128)(2,1)}, u32[]{:S(2)}, u32[]{:S(2)}) collective-permute-start(bf16[2,256,256]{2,1,0:T(8,128)(2,1)} %get-tuple-element.23), channel_id=1, source_target_pairs={{0,16},{8,24},{16,0},{24,8},{1,17},{9,25},{17,1},{25,9},{2,18},{10... | collective-permute-start | bytes 786440 | tf_op jit(solution)/shard_map/ppermute | solution.py:23
  225.1 23.5 %collective-permute-start.25 = (bf16[2,256,512]{2,1,0:T(8,128)(2,1)S(1)}, bf16[2,256,512]{2,1,0:T(8,128)(2,1)S(1)}, u32[]{:S(2)}, u32[]{:S(2)}) collective-permute-start(bf16[2,256,512]{2,1,0:T(8,128)(2,1)S(1)} %get-tuple-element.21), channel_id=1, source_target_pairs={{0,24},{8,16},{16,8},{24,0},{1,25},{9,17},{17,9},{25,1},{2,26},{10... | collective-permute-start | bytes 1572872 | tf_op jit(solution)/shard_map/ppermute | solution.py:23
  227.5 30.8 %copy-start.20 = (bf16[1024,2048]{1,0:T(8,128)(2,1)S(1)}, bf16[1024,2048]{1,0:T(8,128)(2,1)}, u32[]{:S(2)}) copy-start(bf16[1024,2048]{1,0:T(8,128)(2,1)} %all-gather.8.cloned.1.call-done) | copy-start | bytes 12582916
  229.6 27.8 %collective-permute-start.26 = (bf16[2,256,512]{2,1,0:T(8,128)(2,1)S(1)}, bf16[2,256,512]{2,1,0:T(8,128)(2,1)S(1)}, u32[]{:S(2)}, u32[]{:S(2)}) collective-permute-start(bf16[2,256,512]{2,1,0:T(8,128)(2,1)S(1)} %get-tuple-element.21), channel_id=1, source_target_pairs={{0,8},{8,0},{16,24},{24,16},{1,9},{9,1},{17,25},{25,17},{2,10},{10... | collective-permute-start | bytes 1572872 | tf_op jit(solution)/shard_map/ppermute | solution.py:23
  231.7 26.6 %collective-permute-start.27 = (bf16[2,256,512]{2,1,0:T(8,128)(2,1)S(1)}, bf16[2,256,512]{2,1,0:T(8,128)(2,1)S(1)}, u32[]{:S(2)}, u32[]{:S(2)}) collective-permute-start(bf16[2,256,512]{2,1,0:T(8,128)(2,1)S(1)} %get-tuple-element.21), channel_id=1, source_target_pairs={{0,16},{8,24},{16,0},{24,8},{1,17},{9,25},{17,1},{25,9},{2,18},{10... | collective-permute-start | bytes 1572872 | tf_op jit(solution)/shard_map/ppermute | solution.py:23
  232.7 27.9 %copy-start.13 = (bf16[4,2,256,256]{3,2,1,0:T(8,128)(2,1)}, bf16[4,2,256,256]{3,2,1,0:T(8,128)(2,1)S(1)}, u32[]{:S(2)}) copy-start(bf16[4,2,256,256]{3,2,1,0:T(8,128)(2,1)S(1)} %bitcast_dynamic-update-slice_fusion.9) | copy-start | bytes 3145732
  263.0 19.1 %all-to-all-start = ((bf16[8,128,1,256]{1,3,2,0:T(8,128)(2,1)}), bf16[8,128,1,256]{1,3,2,0:T(8,128)(2,1)S(1)}, u32[]{:S(2)}, u32[]{:S(2)}) async-start(bf16[8,128,1,256]{1,3,2,0:T(8,128)(2,1)} %copy.55), calls=%async_computation | async-start | bytes 1048576 | tf_op jit(solution)/shard_map/all_to_all | solution.py:145
  282.1 18.8 %all-to-all-start.1 = ((bf16[8,128,1,256]{1,3,2,0:T(8,128)(2,1)}), bf16[8,128,1,256]{1,3,2,0:T(8,128)(2,1)S(1)}, u32[]{:S(2)}, u32[]{:S(2)}) async-start(bf16[8,128,1,256]{1,3,2,0:T(8,128)(2,1)} %copy.62), calls=%async_computation.1 | async-start | bytes 1048576 | tf_op jit(solution)/shard_map/all_to_all | solution.py:145
  288.1 26.6 %collective-permute-start.28 = (bf16[128,2048]{0,1:T(8,128)(2,1)S(1)}, bf16[128,2048]{0,1:T(8,128)(2,1)}, u32[]{:S(2)}, u32[]{:S(2)}) collective-permute-start(bf16[128,2048]{0,1:T(8,128)(2,1)S(1)} %bitcast.330), channel_id=1, source_target_pairs={{0,24},{8,16},{16,8},{24,0},{1,25},{9,17},{17,9},{25,1},{2,26},{10... | collective-permute-start | bytes 1572872 | tf_op jit(solution)/shard_map/ppermute | solution.py:23
  301.9 16.1 %collective-permute-start.37 = (bf16[128,2048]{1,0:T(8,128)(2,1)}, bf16[128,2048]{1,0:T(8,128)(2,1)}, u32[]{:S(2)}, u32[]{:S(2)}) collective-permute-start(bf16[128,2048]{1,0:T(8,128)(2,1)} %copy.64), channel_id=1, source_target_pairs={{0,24},{8,16},{16,8},{24,0},{1,25},{9,17},{17,9},{25,1},{2,26},{10... | collective-permute-start | bytes 1572872 | tf_op jit(solution)/shard_map/ppermute | solution.py:23
  308.5 20.0 %collective-permute-start.29 = (bf16[128,2048]{0,1:T(8,128)(2,1)S(1)}, bf16[128,2048]{0,1:T(8,128)(2,1)}, u32[]{:S(2)}, u32[]{:S(2)}) collective-permute-start(bf16[128,2048]{0,1:T(8,128)(2,1)S(1)} %bitcast.331), channel_id=1, source_target_pairs={{0,8},{8,0},{16,24},{24,16},{1,9},{9,1},{17,25},{25,17},{2,10},{10... | collective-permute-start | bytes 1572872 | tf_op jit(solution)/shard_map/ppermute | solution.py:23
  309.2 20.6 %collective-permute-start.30 = (bf16[128,2048]{0,1:T(8,128)(2,1)S(1)}, bf16[128,2048]{0,1:T(8,128)(2,1)}, u32[]{:S(2)}, u32[]{:S(2)}) collective-permute-start(bf16[128,2048]{0,1:T(8,128)(2,1)S(1)} %bitcast.332), channel_id=1, source_target_pairs={{0,16},{8,24},{16,0},{24,8},{1,17},{9,25},{17,1},{25,9},{2,18},{10... | collective-permute-start | bytes 1572872 | tf_op jit(solution)/shard_map/ppermute | solution.py:23
  310.4 28.0 %collective-permute-start.38 = (bf16[128,2048]{1,0:T(8,128)(2,1)}, bf16[128,2048]{1,0:T(8,128)(2,1)}, u32[]{:S(2)}, u32[]{:S(2)}) collective-permute-start(bf16[128,2048]{1,0:T(8,128)(2,1)} %copy.64), channel_id=1, source_target_pairs={{0,8},{8,0},{16,24},{24,16},{1,9},{9,1},{17,25},{25,17},{2,10},{10... | collective-permute-start | bytes 1572872 | tf_op jit(solution)/shard_map/ppermute | solution.py:23
  314.8 24.8 %collective-permute-start.39 = (bf16[128,2048]{1,0:T(8,128)(2,1)}, bf16[128,2048]{1,0:T(8,128)(2,1)}, u32[]{:S(2)}, u32[]{:S(2)}) collective-permute-start(bf16[128,2048]{1,0:T(8,128)(2,1)} %copy.64), channel_id=1, source_target_pairs={{0,16},{8,24},{16,0},{24,8},{1,17},{9,25},{17,1},{25,9},{2,18},{10... | collective-permute-start | bytes 1572872 | tf_op jit(solution)/shard_map/ppermute | solution.py:23
  (22 other events, 79.2 us)
Sparse Core Ops, SparseCore 0:
  69.2 48.8 all-gather.5
  119.6 53.5 all-gather.7
  175.4 80.4 all-gather.3

commit v3 on v2

--- a/solution.py
+++ b/solution.py
@@ -37,12 +37,14 @@
     total = lax.dynamic_index_in_dim(parts, me, axis, False).astype(f32)
     for term in got:
         total = total + term.astype(f32)
-    return total
+    return total, got[0]
 
 
-def gather(block, count):
+def gather(block, count, before=None):
     me = lax.axis_index("rows")
     got = [(mask, swap(block, count, mask)) for mask in partners(count)]
+    if before is not None:
+        block, _ = lax.optimization_barrier((block, before))
     whole = lax.dynamic_update_index_in_dim(
         jnp.zeros((count,) + block.shape, block.dtype), block, me, 0
     )
@@ -65,42 +67,52 @@
     return whole
 
 
+def product(blocks, left):
+    return lax.dot_general(
+        blocks, left, (((1,), (0,)), ((), ())), preferred_element_type=f32
+    ).astype(bf16)
+
+
 def rotate_left(grad, left, later, rows, cols):
     depth, width = grad.shape
     sub = width // rows
     half = cols // 4
     index = lax.axis_index("cols")
     core, odd, pair = index & 1, (index >> 1) & 1, index >> 2
-    left_other = lax.ppermute(left, "cols", [(i, i ^ 2) for i in range(cols)])
-    moved = []
-    for step in range(half):
+    left_pair = jnp.concatenate(
+        [lax.ppermute(left, "cols", [(i, i ^ 2) for i in range(cols)]), left], 1
+    )
+    def along(step, value):
         route = []
         for chip in range(half):
             for odd_chip in range(2):
                 source, target = odd_chip * half + chip, 2 * ((chip + step) % half) + odd_chip
                 route += [(2 * source + c, 2 * target + c) for c in range(2)]
-        if moved:
-            grad, moved[-1], left_other, later = lax.optimization_barrier(
-                (grad, moved[-1], left_other, later)
-            )
-        moved.append(lax.ppermute(grad, "cols", route))
-    moved[-1], later, left = lax.optimization_barrier((moved[-1], later, left))
-    left_pair = jnp.concatenate([left_other, left], 1)
+        return lax.ppermute(value, "cols", route)
+
     whole = jnp.zeros((2, half, 2, sub, width), bf16)
-    for step, block in enumerate(moved):
+    block = along(0, grad)
+    for step in range(half):
+        if step < half - 1:
+            grad, block, left_pair, later = lax.optimization_barrier((grad, block, left_pair, later))
+            ahead = along(step + 1, grad)
         other = lax.ppermute(block, "cols", [(i, i ^ 1) for i in range(cols)])
         both = jnp.where(core == 0, jnp.stack([block, other]), jnp.stack([other, block]))
-        parts = lax.dot_general(
-            both, left_pair, (((1,), (0,)), ((), ())), preferred_element_type=f32
-        ).astype(bf16)
-        parts = scatter_sum(parts.reshape(2, rows, sub, 2 * width), 1).astype(bf16)
-        got = lax.ppermute(parts[..., :width], "cols", [(i, i ^ 2) for i in range(cols)])
+        parts = product(both, left_pair).reshape(2, rows, sub, 2 * width)
+        mark = parts
+        sums, got = scatter_sum(parts, 1)
+        sums = sums.astype(bf16)
+        if step == half - 2:
+            later, _, _ = lax.optimization_barrier((later, ahead, got))
+        if step < half - 1:
+            block, _ = lax.optimization_barrier((ahead, sums))
+        got = lax.ppermute(sums[..., :width], "cols", [(i, i ^ 2) for i in range(cols)])
         chip = lax.rem(pair + half - step, half)
-        for half_index, value in ((odd, parts[..., width:]), (1 - odd, got)):
+        for half_index, value in ((odd, sums[..., width:]), (1 - odd, got)):
             whole = lax.dynamic_update_slice(
                 whole, value[None, None], (half_index, chip, 0, 0, 0)
             )
-    return whole.reshape(depth, width), later, left
+    return whole.reshape(depth, width), later, mark
 
 
 def make_local(rows, cols):
@@ -112,8 +124,9 @@
         spans = (slice(0, mid), slice(mid, width))
 
         dealt = deal(right_basis.reshape(per, rows, sub, width)).reshape(depth, width)
-        half, dealt, left = rotate_left(forget_grad, left_basis, dealt, rows, cols)
-        basis = [lax.all_gather(dealt[:, span], "cols", axis=1, tiled=True) for span in spans]
+        half, dealt, mark = rotate_left(forget_grad, left_basis, dealt, rows, cols)
+        late, left, _ = lax.optimization_barrier((dealt[:, mid:], left_basis, mark))
+        basis = [lax.all_gather(x, "cols", axis=1, tiled=True) for x in (dealt[:, :mid], late)]
         left_rows = lax.all_gather(left, "cols", axis=1, tiled=True)
 
         first = first_moment.reshape(per, 2, mid, width)
@@ -123,7 +136,7 @@
             parts = lax.dot_general(
                 basis[c], half[:, span], (((0,), (0,)), ((), ())), preferred_element_type=f32
             ).astype(bf16)
-            return -scatter_sum(rows_first(parts).reshape(rows, per, mid, -1), 0)
+            return -scatter_sum(rows_first(parts).reshape(rows, per, mid, -1), 0)[0]
 
         def normalize(c, span, value):
             new_first = beta_first * first[:, c, :, span] + (1.0 - beta_first) * value
@@ -138,18 +151,19 @@
 
         step_dir = None
         left_rows = left_rows.reshape(depth, cols, 2, mid)
+        term = back
         for c, span in enumerate(spans):
-            normals = normalize(1, span, values[c])
+            normals, _ = lax.optimization_barrier((normalize(1, span, values[c]), term))
             term = jnp.dot(basis[1], normals, preferred_element_type=f32) + back[:, span]
             term = rows_first(term.astype(bf16)).reshape(cols, sub, mid)
-            term = lax.all_to_all(term, "cols", 0, 1).reshape(sub, cols * mid)
-            term = lax.dot_general(
+            full = lax.all_to_all(term, "cols", 0, 1).reshape(sub, cols * mid)
+            full = lax.dot_general(
                 left_rows[:, :, c].reshape(depth, cols * mid),
-                gather(term, rows).reshape(width, cols * mid),
+                gather(full, rows, step_dir).reshape(width, cols * mid),
                 (((1,), (1,)), ((), ())),
                 preferred_element_type=f32,
             )
-            step_dir = term if step_dir is None else step_dir + term
+            step_dir = full if step_dir is None else step_dir + full
         step_dir = step_dir.astype(bf16)
 
         new_first = beta_first * first_moment + (1.0 - beta_first) * rotated

time: 358 us -> 331 us (0.925)
  waiting for transfers between devices: 190 us -> 153 us
  local copies, waits for them, and re-layouts: 35 us -> 41.5 us
    ppermute x5, waiting for transfers between devices: 47.3 us -> 24 us  [the longest x2 18 us: along(): return lax.ppermute(value, 'cols', route)]
    all_gather x2, waiting for transfers between devices: 8.85 us -> 0.01 us  [local(): lax.all_gather(x, 'cols', axis=1, tiled=True)]
    ppermute x5, starting transfers between devices: 17.1 us -> 25.1 us  [the longest x2 17.7 us: along(): return lax.ppermute(value, 'cols', route)]
    ppermute x33, starting transfers between devices: 43.2 us -> 38.5 us  [swap(): return lax.ppermute(block, 'rows', [(i, i ^ mask) for i in range(count)])]
    all_to_all x2, waiting for transfers between devices: 19 us -> 14.5 us  [local(): full = lax.all_to_all(term, 'cols', 0, 1).reshape(sub, cols * mid)]
  transfers between devices with their start and end apart: 45 -> 45, of which waited for: 25 -> 23; matrix products, arithmetic and copies ran while one was open for 19% -> 25% of each run, Pallas kernels for 0% -> 0%
where the time goes in v3:
time: 331 us; the launch traced here: 330 us
  waiting for transfers between devices  153 us (46%)
  starting transfers between devices  70.8 us (21%)
  local copies, waits for them, and re-layouts  41.5 us (13%)
  matrix products  35 us (11%)
  other arithmetic  15.2 us (5%)
  between operations  14.4 us (4%)
    ppermute x33, waiting for transfers between devices, swap(): return lax.ppermute(block, 'rows', [(i, i ^ mask) for i in range(count)])  112 us
    ppermute x33, starting transfers between devices, swap(): return lax.ppermute(block, 'rows', [(i, i ^ mask) for i in range(count)])  38.5 us
    ppermute x2, waiting for transfers between devices, along(): return lax.ppermute(value, 'cols', route)  18 us
    ppermute x2, starting transfers between devices, along(): return lax.ppermute(value, 'cols', route)  17.7 us
    all_to_all x2, waiting for transfers between devices, local(): full = lax.all_to_all(term, 'cols', 0, 1).reshape(sub, cols * mid)  14.5 us
    dot_general x3, matrix products, turn(): lax.dot_general(basis[c], half[:, span], (((0,), (0,)), ((), ())), prefer...  11.4 us
    dot_general x2, matrix products, product(): lax.dot_general(blocks, left, (((1,), (0,)), ((), ())), preferred_element...  8.68 us
    dynamic_update_slice x15, local copies, waits for them, and re-layouts, gather(): whole = lax.dynamic_update_index_in_dim(whole, term, me ^ mask, 0)  8.04 us
  transfers between devices with their start and end apart: 45, of which 23 were waited for; matrix products, arithmetic and copies ran while one was open for 25% of the time, Pallas kernels for 0%

profile of v3, /device:TPU:0, one launch (start us, length us, event | category | flops | bytes accessed | tf_op | source)
XLA Modules:
  0.0 330.0 jit_solution(3512873752952817284)
XLA Ops:
  7.2 3.1 collective-permute-start.1
  10.3 2.1 dynamic-slice_bitcast_fusion.15
  12.4 2.4 collective-permute-start.2
  14.8 9.4 %collective-permute-start = (bf16[1024,512]{1,0:T(8,128)(2,1)}, bf16[1024,512]{1,0:T(8,128)(2,1)}, u32[]{:S(2)}, u32[]{:S(2)}) collective-permute-start(bf16[1024,512]{1,0:T(8,128)(2,1)} %param.5), channel_id=1, source_target_pairs={{0,0},{1,1},{4,2},{5,3},{2,4},{3,5},{6,6},{7,7},{8,8},{9,9},{12,10... | collective-permute-start | bytes 3145736 | tf_op jit(solution)/shard_map/ppermute | solution.py:91
  27.4 4.7 %collective-permute-done.3 = bf16[2,128,512]{2,1,0:T(8,128)(2,1)} collective-permute-done((bf16[2,128,512]{2,1,0:T(8,128)(2,1)}, bf16[2,128,512]{2,1,0:T(8,128)(2,1)}, u32[]{:S(2)}, u32[]{:S(2)}) %collective-permute-start.3) | collective-permute-done | bytes 262176 | tf_op jit(solution)/shard_map/ppermute | solution.py:23
  35.7 8.3 %collective-permute-start.5 = (bf16[1024,512]{1,0:T(8,128)(2,1)}, bf16[1024,512]{1,0:T(8,128)(2,1)S(1)}, u32[]{:S(2)}, u32[]{:S(2)}) collective-permute-start(bf16[1024,512]{1,0:T(8,128)(2,1)} %param.5), channel_id=1, source_target_pairs={{0,4},{1,5},{4,6},{5,7},{2,0},{3,1},{6,2},{7,3},{8,12},{9,13},{12,... | collective-permute-start | bytes 3145736 | tf_op jit(solution)/shard_map/ppermute | solution.py:91
  43.9 4.7 %fusion.21 = bf16[2,512,1024]{2,1,0:T(8,128)(2,1)S(1)} fusion(bf16[1024,1024]{1,0:T(8,128)(2,1)} %pad_maximum_fusion, bf16[1,1024,512]{2,1,0:T(8,128)(2,1)S(1)} %bitcast.350, bf16[1,1024,512]{2,1,0:T(8,128)(2,1)} %bitcast.9, pred[]{:T(512)S(6)} %eq.4), kind=kOutput, calls=%fused_computation.29 | convolution fusion | flops 2151677952 | bytes 6291457 | tf_op jit(solution)/shard_map/dot_general | solution.py:71
  49.3 18.0 %collective-permute-done.5 = bf16[1024,512]{1,0:T(8,128)(2,1)S(1)} collective-permute-done((bf16[1024,512]{1,0:T(8,128)(2,1)}, bf16[1024,512]{1,0:T(8,128)(2,1)S(1)}, u32[]{:S(2)}, u32[]{:S(2)}) %collective-permute-start.5) | collective-permute-done | bytes 1048608 | tf_op jit(solution)/shard_map/ppermute | solution.py:91
  70.0 12.5 %collective-permute-done.8 = bf16[2,128,1024]{2,1,0:T(8,128)(2,1)S(1)} collective-permute-done((bf16[2,128,1024]{2,1,0:T(8,128)(2,1)S(1)}, bf16[2,128,1024]{2,1,0:T(8,128)(2,1)S(1)}, u32[]{:S(2)}, u32[]{:S(2)}) %collective-permute-start.8) | collective-permute-done | bytes 524320 | tf_op jit(solution)/shard_map/ppermute | solution.py:23
  82.8 2.4 fusion.45
  85.2 2.7 collective-permute-done.10
  87.8 4.0 %fusion.18 = bf16[2,512,1024]{2,1,0:T(8,128)(2,1)S(1)} fusion(bf16[1024,1024]{1,0:T(8,128)(2,1)} %pad_maximum_fusion, bf16[1,1024,512]{2,1,0:T(8,128)(2,1)S(1)} %bitcast.351, bf16[1,1024,512]{2,1,0:T(8,128)(2,1)S(1)} %bitcast.349, pred[]{:T(512)S(6)} %eq.4), kind=kOutput, calls=%fused_computation.28 | convolution fusion | flops 2151677952 | bytes 6291457 | tf_op jit(solution)/shard_map/dot_general | solution.py:71
  97.9 2.2 collective-permute-start.11
  101.9 8.6 %collective-permute-done.12 = bf16[2,128,1024]{2,1,0:T(8,128)(2,1)} collective-permute-done((bf16[2,128,1024]{2,1,0:T(8,128)(2,1)}, bf16[2,128,1024]{2,1,0:T(8,128)(2,1)}, u32[]{:S(2)}, u32[]{:S(2)}) %collective-permute-start.12) | collective-permute-done | bytes 524320 | tf_op jit(solution)/shard_map/ppermute | solution.py:23
  110.4 9.5 %collective-permute-done.13 = bf16[2,128,1024]{2,1,0:T(8,128)(2,1)} collective-permute-done((bf16[2,128,1024]{2,1,0:T(8,128)(2,1)}, bf16[2,128,1024]{2,1,0:T(8,128)(2,1)}, u32[]{:S(2)}, u32[]{:S(2)}) %collective-permute-start.13) | collective-permute-done | bytes 524320 | tf_op jit(solution)/shard_map/ppermute | solution.py:23
  122.8 2.1 collective-permute-start.15
  126.4 5.9 %collective-permute-done.15 = bf16[2,128,512]{2,1,0:T(8,128)(2,1)S(1)} collective-permute-done((bf16[2,128,512]{2,1,0:T(8,128)(2,1)S(1)}, bf16[2,128,512]{2,1,0:T(8,128)(2,1)S(1)}, u32[]{:S(2)}, u32[]{:S(2)}) %collective-permute-start.15) | collective-permute-done | bytes 262176 | tf_op jit(solution)/shard_map/ppermute | solution.py:109
  133.0 4.9 %convolution_convert_fusion = bf16[2048,512]{1,0:T(8,128)(2,1)S(1)} fusion(bf16[1024,2048]{1,0:T(8,128)(2,1)} %all-gather.8.cloned.1.call-done, bf16[1024,512]{1,0:T(8,128)(2,1)} %bitcast.32), kind=kOutput, calls=%fused_computation.1 | convolution fusion | flops 2148532224 | bytes 7340032 | tf_op jit(solution)/shard_map/dot_general | solution.py:136
  139.5 2.2 collective-permute-start.24
  141.7 12.3 %collective-permute-done.22 = bf16[2,256,512]{2,1,0:T(8,128)(2,1)S(1)} collective-permute-done((bf16[2,256,512]{2,1,0:T(8,128)(2,1)S(1)}, bf16[2,256,512]{2,1,0:T(8,128)(2,1)S(1)}, u32[]{:S(2)}, u32[]{:S(2)}) %collective-permute-start.22) | collective-permute-done | bytes 524320 | tf_op jit(solution)/shard_map/ppermute | solution.py:23
  154.0 8.0 %collective-permute-done.23 = bf16[2,256,512]{2,1,0:T(8,128)(2,1)S(1)} collective-permute-done((bf16[2,256,512]{2,1,0:T(8,128)(2,1)S(1)}, bf16[2,256,512]{2,1,0:T(8,128)(2,1)S(1)}, u32[]{:S(2)}, u32[]{:S(2)}) %collective-permute-start.23) | collective-permute-done | bytes 524320 | tf_op jit(solution)/shard_map/ppermute | solution.py:23
  169.7 3.8 %convolution_convert_fusion.1 = bf16[2048,256]{1,0:T(8,128)(2,1)S(1)} fusion(bf16[1024,2048]{1,0:T(8,128)(2,1)} %all-gather.6.cloned.1.call-done, bf16[1024,512]{1,0:T(8,128)(2,1)} %bitcast.32), kind=kOutput, calls=%fused_computation.2 | convolution fusion | flops 1074266112 | bytes 5767168 | tf_op jit(solution)/shard_map/dot_general | solution.py:136
  173.5 2.2 collective-permute-start.31
  176.3 2.7 convolution_convert_fusion.2
  179.1 3.1 collective-permute-done.25
  184.8 7.7 %collective-permute-done.26 = bf16[2,256,512]{2,1,0:T(8,128)(2,1)S(1)} collective-permute-done((bf16[2,256,512]{2,1,0:T(8,128)(2,1)}, bf16[2,256,512]{2,1,0:T(8,128)(2,1)S(1)}, u32[]{:S(2)}, u32[]{:S(2)}) %collective-permute-start.26) | collective-permute-done | bytes 524320 | tf_op jit(solution)/shard_map/ppermute | solution.py:23
  195.6 2.3 fusion.91
  197.9 12.3 %collective-permute-done.16 = bf16[2,256,256]{2,1,0:T(8,128)(2,1)S(1)} collective-permute-done((bf16[2,256,256]{2,1,0:T(8,128)(2,1)S(1)}, bf16[2,256,256]{2,1,0:T(8,128)(2,1)S(1)}, u32[]{:S(2)}, u32[]{:S(2)}) %collective-permute-start.16) | collective-permute-done | bytes 262176 | tf_op jit(solution)/shard_map/ppermute | solution.py:23
  210.8 3.3 %collective-permute-done.17 = bf16[2,256,256]{2,1,0:T(8,128)(2,1)S(1)} collective-permute-done((bf16[2,256,256]{2,1,0:T(8,128)(2,1)S(1)}, bf16[2,256,256]{2,1,0:T(8,128)(2,1)S(1)}, u32[]{:S(2)}, u32[]{:S(2)}) %collective-permute-start.17) | collective-permute-done | bytes 262176 | tf_op jit(solution)/shard_map/ppermute | solution.py:23
  215.5 2.3 collective-permute-start.19
  223.4 2.3 collective-permute-done.19
  227.1 4.1 %collective-permute-done.20 = bf16[2,256,256]{2,1,0:T(8,128)(2,1)S(1)} collective-permute-done((bf16[2,256,256]{2,1,0:T(8,128)(2,1)S(1)}, bf16[2,256,256]{2,1,0:T(8,128)(2,1)S(1)}, u32[]{:S(2)}, u32[]{:S(2)}) %collective-permute-start.20) | collective-permute-done | bytes 262176 | tf_op jit(solution)/shard_map/ppermute | solution.py:23
  231.3 9.9 %collective-permute-done.21 = bf16[2,256,256]{2,1,0:T(8,128)(2,1)S(1)} collective-permute-done((bf16[2,256,256]{2,1,0:T(8,128)(2,1)S(1)}, bf16[2,256,256]{2,1,0:T(8,128)(2,1)S(1)}, u32[]{:S(2)}, u32[]{:S(2)}) %collective-permute-start.21) | collective-permute-done | bytes 262176 | tf_op jit(solution)/shard_map/ppermute | solution.py:23
  243.8 3.6 %all-to-all-start = ((bf16[8,128,1,256]{1,3,2,0:T(8,128)(2,1)}), bf16[8,128,1,256]{1,3,2,0:T(8,128)(2,1)S(1)}, u32[]{:S(2)}, u32[]{:S(2)}) async-start(bf16[8,128,1,256]{1,3,2,0:T(8,128)(2,1)} %copy.55), calls=%async_computation | async-start | bytes 1048576 | tf_op jit(solution)/shard_map/all_to_all | solution.py:159
  249.6 4.1 %fusion.24 = bf16[1024,256]{1,0:T(8,128)(2,1)S(1)} fusion(bf16[1024,2048]{1,0:T(8,128)(2,1)} %all-gather.6.cloned.1.call-done, bf16[2048,256]{1,0:T(8,128)(2,1)} %bitcast.342, f32[1024,512]{1,0:T(8,128)} %copy-done.25), kind=kOutput, calls=%fused_computation.32 | convolution fusion | flops 1074266112 | bytes 6815744 | tf_op jit(solution)/shard_map/dot_general | solution.py:157
  254.6 8.1 %all-to-all-done = bf16[8,128,1,256]{1,3,2,0:T(8,128)(2,1)S(1)} async-done(((bf16[8,128,1,256]{1,3,2,0:T(8,128)(2,1)}), bf16[8,128,1,256]{1,3,2,0:T(8,128)(2,1)S(1)}, u32[]{:S(2)}, u32[]{:S(2)}) %all-to-all-start) | async-done | bytes 524320 | tf_op jit(solution)/shard_map/all_to_all | solution.py:159
  262.7 3.5 %all-to-all-start.1 = ((bf16[8,128,1,256]{1,3,2,0:T(8,128)(2,1)}), bf16[8,128,1,256]{1,3,2,0:T(8,128)(2,1)S(1)}, u32[]{:S(2)}, u32[]{:S(2)}) async-start(bf16[8,128,1,256]{1,3,2,0:T(8,128)(2,1)} %copy.62), calls=%async_computation.1 | async-start | bytes 1048576 | tf_op jit(solution)/shard_map/all_to_all | solution.py:159
  268.7 2.7 collective-permute-start.28
  272.3 2.8 fusion
  275.1 6.4 %all-to-all-done.1 = bf16[8,128,1,256]{1,3,2,0:T(8,128)(2,1)S(1)} async-done(((bf16[8,128,1,256]{1,3,2,0:T(8,128)(2,1)}), bf16[8,128,1,256]{1,3,2,0:T(8,128)(2,1)S(1)}, u32[]{:S(2)}, u32[]{:S(2)}) %all-to-all-start.1) | async-done | bytes 524320 | tf_op jit(solution)/shard_map/all_to_all | solution.py:159
  282.5 2.6 collective-permute-start.37
  290.2 5.7 %collective-permute-done.29 = bf16[128,2048]{0,1:T(8,128)(2,1)} collective-permute-done((bf16[128,2048]{0,1:T(8,128)(2,1)S(1)}, bf16[128,2048]{0,1:T(8,128)(2,1)}, u32[]{:S(2)}, u32[]{:S(2)}) %collective-permute-start.29) | collective-permute-done | bytes 524320 | tf_op jit(solution)/shard_map/ppermute | solution.py:23
  295.9 2.1 copy.58
  298.0 2.1 copy.59
  301.4 5.4 %fusion.89 = (bf16[1024,8,1,256]{0,3,2,1:T(8,128)(2,1)}, bf16[1024,8,1,256]{0,3,2,1:T(8,128)(2,1)S(1)}) fusion(bf16[1024,8,2,256]{0,3,2,1:T(8,128)(2,1)} %bitcast.313), kind=kLoop, calls=%fused_computation.153 | loop fusion | bytes 16777216 | tf_op jit(solution)/shard_map/slice | solution.py:161
  306.8 3.7 %fusion.92 = f32[1024,512]{1,0:T(8,128)} fusion(bf16[1024,2048]{0,1:T(8,128)(2,1)S(1)} %bitcast.324, bf16[512,2048]{1,0:T(8,128)(2,1)S(1)} %bitcast.330), kind=kOutput, calls=%fused_computation.156 | convolution fusion | flops 2147483648 | bytes 8388608 | tf_op jit(solution)/shard_map/dot_general | solution.py:160
  312.3 5.6 %collective-permute-done.38 = bf16[128,2048]{1,0:T(8,128)(2,1)} collective-permute-done((bf16[128,2048]{1,0:T(8,128)(2,1)}, bf16[128,2048]{1,0:T(8,128)(2,1)}, u32[]{:S(2)}, u32[]{:S(2)}) %collective-permute-start.38) | collective-permute-done | bytes 524320 | tf_op jit(solution)/shard_map/ppermute | solution.py:23
  320.1 3.4 %add_convert_fusion = bf16[1024,512]{1,0:T(8,128)(2,1)} fusion(f32[1024,512]{1,0:T(8,128)S(1)} %copy-done.26, bf16[1024,2048]{0,1:T(8,128)(2,1)S(1)} %bitcast.323, bf16[512,2048]{1,0:T(8,128)(2,1)S(1)} %bitcast.328), kind=kOutput, calls=%fused_computation.25 | convolution fusion | flops 2148532224 | bytes 9437184 | tf_op jit(solution)/shard_map/dot_general | solution.py:160
  (171 shorter events, 67.9 us)
Async XLA Ops:
  7.2 125.9 %all-gather.8.cloned.1.call-start = ((), (), s32[]{:S(2)}) async-start(), calls=%async_computation.4 | async-start | bytes 4718592 | tf_op jit(solution)/shard_map/all_gather | solution.py:129
  7.2 26.8 %collective-permute-start.1 = (bf16[1024,512]{1,0:T(8,128)(2,1)}, bf16[1024,512]{1,0:T(8,128)(2,1)S(1)}, u32[]{:S(2)}, u32[]{:S(2)}) collective-permute-start(bf16[1024,512]{1,0:T(8,128)(2,1)} %param.6), channel_id=1, source_target_pairs={{0,2},{1,3},{2,0},{3,1},{4,6},{5,7},{6,4},{7,5},{8,10},{9,11},{10,... | collective-permute-start | bytes 3145736 | tf_op jit(solution)/shard_map/ppermute | solution.py:83
  12.4 14.0 %collective-permute-start.2 = (bf16[2,128,512]{2,1,0:T(8,128)(2,1)}, bf16[2,128,512]{2,1,0:T(8,128)(2,1)}, u32[]{:S(2)}, u32[]{:S(2)}) collective-permute-start(bf16[2,128,512]{2,1,0:T(8,128)(2,1)} %get-tuple-element.54), channel_id=1, source_target_pairs={{0,24},{8,16},{16,8},{24,0},{1,25},{9,17},{17,9},{25,1},{2,26},{10... | collective-permute-start | bytes 786440 | tf_op jit(solution)/shard_map/ppermute | solution.py:23
  14.8 20.9 %collective-permute-start = (bf16[1024,512]{1,0:T(8,128)(2,1)}, bf16[1024,512]{1,0:T(8,128)(2,1)}, u32[]{:S(2)}, u32[]{:S(2)}) collective-permute-start(bf16[1024,512]{1,0:T(8,128)(2,1)} %param.5), channel_id=1, source_target_pairs={{0,0},{1,1},{4,2},{5,3},{2,4},{3,5},{6,6},{7,7},{8,8},{9,9},{12,10... | collective-permute-start | bytes 3145736 | tf_op jit(solution)/shard_map/ppermute | solution.py:91
  24.2 7.8 %collective-permute-start.3 = (bf16[2,128,512]{2,1,0:T(8,128)(2,1)}, bf16[2,128,512]{2,1,0:T(8,128)(2,1)}, u32[]{:S(2)}, u32[]{:S(2)}) collective-permute-start(bf16[2,128,512]{2,1,0:T(8,128)(2,1)} %get-tuple-element.53), channel_id=1, source_target_pairs={{0,8},{8,0},{16,24},{24,16},{1,9},{9,1},{17,25},{25,17},{2,10},{10... | collective-permute-start | bytes 786440 | tf_op jit(solution)/shard_map/ppermute | solution.py:23
  24.8 8.2 %collective-permute-start.4 = (bf16[2,128,512]{2,1,0:T(8,128)(2,1)S(1)}, bf16[2,128,512]{2,1,0:T(8,128)(2,1)}, u32[]{:S(2)}, u32[]{:S(2)}) collective-permute-start(bf16[2,128,512]{2,1,0:T(8,128)(2,1)S(1)} %get-tuple-element.52), channel_id=1, source_target_pairs={{0,16},{8,24},{16,0},{24,8},{1,17},{9,25},{17,1},{25,9},{2,18},{10... | collective-permute-start | bytes 786440 | tf_op jit(solution)/shard_map/ppermute | solution.py:23
  35.7 8.3 %collective-permute-start.6 = (bf16[1024,512]{1,0:T(8,128)(2,1)}, bf16[1024,512]{1,0:T(8,128)(2,1)S(1)}, u32[]{:S(2)}, u32[]{:S(2)}) collective-permute-start(bf16[1024,512]{1,0:T(8,128)(2,1)} %collective-permute-done), channel_id=1, source_target_pairs={{0,1},{1,0},{2,3},{3,2},{4,5},{5,4},{6,7},{7,6},{8,9},{9,8},{10,11... | collective-permute-start | bytes 3145736 | tf_op jit(solution)/shard_map/ppermute | solution.py:99
  35.7 31.7 %collective-permute-start.5 = (bf16[1024,512]{1,0:T(8,128)(2,1)}, bf16[1024,512]{1,0:T(8,128)(2,1)S(1)}, u32[]{:S(2)}, u32[]{:S(2)}) collective-permute-start(bf16[1024,512]{1,0:T(8,128)(2,1)} %param.5), channel_id=1, source_target_pairs={{0,4},{1,5},{4,6},{5,7},{2,0},{3,1},{6,2},{7,3},{8,12},{9,13},{12,... | collective-permute-start | bytes 3145736 | tf_op jit(solution)/shard_map/ppermute | solution.py:91
  48.8 18.6 %collective-permute-start.7 = (bf16[2,128,1024]{2,1,0:T(8,128)(2,1)S(1)}, bf16[2,128,1024]{2,1,0:T(8,128)(2,1)S(1)}, u32[]{:S(2)}, u32[]{:S(2)}) collective-permute-start(bf16[2,128,1024]{2,1,0:T(8,128)(2,1)S(1)} %get-tuple-element.43), channel_id=1, source_target_pairs={{0,24},{8,16},{16,8},{24,0},{1,25},{9,17},{17,9},{25,1},{2,26},{10... | collective-permute-start | bytes 1572872 | tf_op jit(solution)/shard_map/ppermute | solution.py:23
  68.8 100.8 %all-gather.6.cloned.1.call-start = ((), (), s32[]{:S(2)}) async-start(), calls=%async_computation.3 | async-start | bytes 4718592 | tf_op jit(solution)/shard_map/all_gather | solution.py:129
  68.9 13.6 %collective-permute-start.8 = (bf16[2,128,1024]{2,1,0:T(8,128)(2,1)S(1)}, bf16[2,128,1024]{2,1,0:T(8,128)(2,1)S(1)}, u32[]{:S(2)}, u32[]{:S(2)}) collective-permute-start(bf16[2,128,1024]{2,1,0:T(8,128)(2,1)S(1)} %get-tuple-element.41), channel_id=1, source_target_pairs={{0,8},{8,0},{16,24},{24,16},{1,9},{9,1},{17,25},{25,17},{2,10},{10... | collective-permute-start | bytes 1572872 | tf_op jit(solution)/shard_map/ppermute | solution.py:23
  69.5 13.3 %collective-permute-start.9 = (bf16[2,128,1024]{2,1,0:T(8,128)(2,1)S(1)}, bf16[2,128,1024]{2,1,0:T(8,128)(2,1)S(1)}, u32[]{:S(2)}, u32[]{:S(2)}) collective-permute-start(bf16[2,128,1024]{2,1,0:T(8,128)(2,1)S(1)} %get-tuple-element.42), channel_id=1, source_target_pairs={{0,16},{8,24},{16,0},{24,8},{1,17},{9,25},{17,1},{25,9},{2,18},{10... | collective-permute-start | bytes 1572872 | tf_op jit(solution)/shard_map/ppermute | solution.py:23
  85.2 2.7 collective-permute-start.10
  91.9 209.5 %all-gather.4.cloned.1.call-start = ((), (), s32[]{:S(2)}) async-start(), calls=%async_computation.2 | async-start | bytes 9437184 | tf_op jit(solution)/shard_map/all_gather | solution.py:130
  94.4 16.0 %collective-permute-start.12 = (bf16[2,128,1024]{2,1,0:T(8,128)(2,1)}, bf16[2,128,1024]{2,1,0:T(8,128)(2,1)}, u32[]{:S(2)}, u32[]{:S(2)}) collective-permute-start(bf16[2,128,1024]{2,1,0:T(8,128)(2,1)} %get-tuple-element.38), channel_id=1, source_target_pairs={{0,24},{8,16},{16,8},{24,0},{1,25},{9,17},{17,9},{25,1},{2,26},{10... | collective-permute-start | bytes 1572872 | tf_op jit(solution)/shard_map/ppermute | solution.py:23
  95.9 24.1 %collective-permute-start.13 = (bf16[2,128,1024]{2,1,0:T(8,128)(2,1)}, bf16[2,128,1024]{2,1,0:T(8,128)(2,1)}, u32[]{:S(2)}, u32[]{:S(2)}) collective-permute-start(bf16[2,128,1024]{2,1,0:T(8,128)(2,1)} %get-tuple-element.40), channel_id=1, source_target_pairs={{0,8},{8,0},{16,24},{24,16},{1,9},{9,1},{17,25},{25,17},{2,10},{10... | collective-permute-start | bytes 1572872 | tf_op jit(solution)/shard_map/ppermute | solution.py:23
  96.4 24.7 %collective-permute-start.14 = (bf16[2,128,1024]{2,1,0:T(8,128)(2,1)S(1)}, bf16[2,128,1024]{2,1,0:T(8,128)(2,1)}, u32[]{:S(2)}, u32[]{:S(2)}) collective-permute-start(bf16[2,128,1024]{2,1,0:T(8,128)(2,1)S(1)} %get-tuple-element.39), channel_id=1, source_target_pairs={{0,16},{8,24},{16,0},{24,8},{1,17},{9,25},{17,1},{25,9},{2,18},{10... | collective-permute-start | bytes 1572872 | tf_op jit(solution)/shard_map/ppermute | solution.py:23
  97.9 27.0 %collective-permute-start.11 = (bf16[2,128,512]{2,1,0:T(8,128)(2,1)S(1)}, bf16[2,128,512]{2,1,0:T(8,128)(2,1)S(1)}, u32[]{:S(2)}, u32[]{:S(2)}) collective-permute-start(bf16[2,128,512]{2,1,0:T(8,128)(2,1)S(1)} %slice.75), channel_id=1, source_target_pairs={{0,2},{1,3},{2,0},{3,1},{4,6},{5,7},{6,4},{7,5},{8,10},{9,11},{10,... | collective-permute-start | bytes 786440 | tf_op jit(solution)/shard_map/ppermute | solution.py:109
  122.8 9.5 %collective-permute-start.15 = (bf16[2,128,512]{2,1,0:T(8,128)(2,1)S(1)}, bf16[2,128,512]{2,1,0:T(8,128)(2,1)S(1)}, u32[]{:S(2)}, u32[]{:S(2)}) collective-permute-start(bf16[2,128,512]{2,1,0:T(8,128)(2,1)S(1)} %slice.77), channel_id=1, source_target_pairs={{0,2},{1,3},{2,0},{3,1},{4,6},{5,7},{6,4},{7,5},{8,10},{9,11},{10,... | collective-permute-start | bytes 786440 | tf_op jit(solution)/shard_map/ppermute | solution.py:109
  137.9 25.1 %copy-start.6 = (bf16[2048,512]{1,0:T(8,128)(2,1)}, bf16[2048,512]{1,0:T(8,128)(2,1)S(1)}, u32[]{:S(2)}) copy-start(bf16[2048,512]{1,0:T(8,128)(2,1)S(1)} %convolution_convert_fusion) | copy-start | bytes 6291460
  137.9 25.1 %copy-start = (f32[1024,512]{1,0:T(8,128)S(1)}, f32[1024,512]{1,0:T(8,128)}, u32[]{:S(2)}) copy-start(f32[1024,512]{1,0:T(8,128)} %param.9) | copy-start | bytes 6291460
  138.1 15.9 %collective-permute-start.22 = (bf16[2,256,512]{2,1,0:T(8,128)(2,1)S(1)}, bf16[2,256,512]{2,1,0:T(8,128)(2,1)S(1)}, u32[]{:S(2)}, u32[]{:S(2)}) collective-permute-start(bf16[2,256,512]{2,1,0:T(8,128)(2,1)S(1)} %get-tuple-element.35), channel_id=1, source_target_pairs={{0,24},{8,16},{16,8},{24,0},{1,25},{9,17},{17,9},{25,1},{2,26},{10... | collective-permute-start | bytes 1572872 | tf_op jit(solution)/shard_map/ppermute | solution.py:23
  138.9 23.1 %collective-permute-start.23 = (bf16[2,256,512]{2,1,0:T(8,128)(2,1)S(1)}, bf16[2,256,512]{2,1,0:T(8,128)(2,1)S(1)}, u32[]{:S(2)}, u32[]{:S(2)}) collective-permute-start(bf16[2,256,512]{2,1,0:T(8,128)(2,1)S(1)} %get-tuple-element.37), channel_id=1, source_target_pairs={{0,8},{8,0},{16,24},{24,16},{1,9},{9,1},{17,25},{25,17},{2,10},{10... | collective-permute-start | bytes 1572872 | tf_op jit(solution)/shard_map/ppermute | solution.py:23
  139.5 23.4 %collective-permute-start.24 = (bf16[2,256,512]{2,1,0:T(8,128)(2,1)S(1)}, bf16[2,256,512]{2,1,0:T(8,128)(2,1)S(1)}, u32[]{:S(2)}, u32[]{:S(2)}) collective-permute-start(bf16[2,256,512]{2,1,0:T(8,128)(2,1)S(1)} %get-tuple-element.36), channel_id=1, source_target_pairs={{0,16},{8,24},{16,0},{24,8},{1,17},{9,25},{17,1},{25,9},{2,18},{10... | collective-permute-start | bytes 1572872 | tf_op jit(solution)/shard_map/ppermute | solution.py:23
  166.2 16.0 %collective-permute-start.25 = (bf16[2,256,512]{2,1,0:T(8,128)(2,1)}, bf16[2,256,512]{2,1,0:T(8,128)(2,1)}, u32[]{:S(2)}, u32[]{:S(2)}) collective-permute-start(bf16[2,256,512]{2,1,0:T(8,128)(2,1)} %get-tuple-element.27), channel_id=1, source_target_pairs={{0,24},{8,16},{16,8},{24,0},{1,25},{9,17},{17,9},{25,1},{2,26},{10... | collective-permute-start | bytes 1572872 | tf_op jit(solution)/shard_map/ppermute | solution.py:23
  167.7 24.8 %collective-permute-start.26 = (bf16[2,256,512]{2,1,0:T(8,128)(2,1)}, bf16[2,256,512]{2,1,0:T(8,128)(2,1)S(1)}, u32[]{:S(2)}, u32[]{:S(2)}) collective-permute-start(bf16[2,256,512]{2,1,0:T(8,128)(2,1)} %get-tuple-element.27), channel_id=1, source_target_pairs={{0,8},{8,0},{16,24},{24,16},{1,9},{9,1},{17,25},{25,17},{2,10},{10... | collective-permute-start | bytes 1572872 | tf_op jit(solution)/shard_map/ppermute | solution.py:23
  168.3 25.8 %collective-permute-start.27 = (bf16[2,256,512]{2,1,0:T(8,128)(2,1)}, bf16[2,256,512]{2,1,0:T(8,128)(2,1)S(1)}, u32[]{:S(2)}, u32[]{:S(2)}) collective-permute-start(bf16[2,256,512]{2,1,0:T(8,128)(2,1)} %get-tuple-element.27), channel_id=1, source_target_pairs={{0,16},{8,24},{16,0},{24,8},{1,17},{9,25},{17,1},{25,9},{2,18},{10... | collective-permute-start | bytes 1572872 | tf_op jit(solution)/shard_map/ppermute | solution.py:23
  173.5 44.9 %collective-permute-start.31 = (bf16[2,256,256]{2,1,0:T(8,128)(2,1)S(1)}, bf16[2,256,256]{2,1,0:T(8,128)(2,1)S(1)}, u32[]{:S(2)}, u32[]{:S(2)}) collective-permute-start(bf16[2,256,256]{2,1,0:T(8,128)(2,1)S(1)} %get-tuple-element.44), channel_id=1, source_target_pairs={{0,24},{8,16},{16,8},{24,0},{1,25},{9,17},{17,9},{25,1},{2,26},{10... | collective-permute-start | bytes 786440 | tf_op jit(solution)/shard_map/ppermute | solution.py:23
  175.7 42.7 %collective-permute-start.32 = (bf16[2,256,256]{2,1,0:T(8,128)(2,1)S(1)}, bf16[2,256,256]{2,1,0:T(8,128)(2,1)S(1)}, u32[]{:S(2)}, u32[]{:S(2)}) collective-permute-start(bf16[2,256,256]{2,1,0:T(8,128)(2,1)S(1)} %get-tuple-element.46), channel_id=1, source_target_pairs={{0,8},{8,0},{16,24},{24,16},{1,9},{9,1},{17,25},{25,17},{2,10},{10... | collective-permute-start | bytes 786440 | tf_op jit(solution)/shard_map/ppermute | solution.py:23
  182.2 28.0 %collective-permute-start.16 = (bf16[2,256,256]{2,1,0:T(8,128)(2,1)S(1)}, bf16[2,256,256]{2,1,0:T(8,128)(2,1)S(1)}, u32[]{:S(2)}, u32[]{:S(2)}) collective-permute-start(bf16[2,256,256]{2,1,0:T(8,128)(2,1)S(1)} %get-tuple-element.49), channel_id=1, source_target_pairs={{0,24},{8,16},{16,8},{24,0},{1,25},{9,17},{17,9},{25,1},{2,26},{10... | collective-permute-start | bytes 786440 | tf_op jit(solution)/shard_map/ppermute | solution.py:23
  192.5 21.6 %collective-permute-start.17 = (bf16[2,256,256]{2,1,0:T(8,128)(2,1)S(1)}, bf16[2,256,256]{2,1,0:T(8,128)(2,1)S(1)}, u32[]{:S(2)}, u32[]{:S(2)}) collective-permute-start(bf16[2,256,256]{2,1,0:T(8,128)(2,1)S(1)} %get-tuple-element.51), channel_id=1, source_target_pairs={{0,8},{8,0},{16,24},{24,16},{1,9},{9,1},{17,25},{25,17},{2,10},{10... | collective-permute-start | bytes 786440 | tf_op jit(solution)/shard_map/ppermute | solution.py:23
  194.0 20.1 %collective-permute-start.18 = (bf16[2,256,256]{2,1,0:T(8,128)(2,1)S(1)}, bf16[2,256,256]{2,1,0:T(8,128)(2,1)S(1)}, u32[]{:S(2)}, u32[]{:S(2)}) collective-permute-start(bf16[2,256,256]{2,1,0:T(8,128)(2,1)S(1)} %get-tuple-element.50), channel_id=1, source_target_pairs={{0,16},{8,24},{16,0},{24,8},{1,17},{9,25},{17,1},{25,9},{2,18},{10... | collective-permute-start | bytes 786440 | tf_op jit(solution)/shard_map/ppermute | solution.py:23
  197.9 43.3 %copy-start.25 = (f32[1024,512]{1,0:T(8,128)}, f32[1024,512]{1,0:T(8,128)S(1)}, u32[]{:S(2)}) copy-start(f32[1024,512]{1,0:T(8,128)S(1)} %fusion.91) | copy-start | bytes 6291460
  210.2 8.2 %collective-permute-start.33 = (bf16[2,256,256]{2,1,0:T(8,128)(2,1)S(1)}, bf16[2,256,256]{2,1,0:T(8,128)(2,1)S(1)}, u32[]{:S(2)}, u32[]{:S(2)}) collective-permute-start(bf16[2,256,256]{2,1,0:T(8,128)(2,1)S(1)} %get-tuple-element.45), channel_id=1, source_target_pairs={{0,16},{8,24},{16,0},{24,8},{1,17},{9,25},{17,1},{25,9},{2,18},{10... | collective-permute-start | bytes 786440 | tf_op jit(solution)/shard_map/ppermute | solution.py:23
  215.5 10.1 %collective-permute-start.19 = (bf16[2,256,256]{2,1,0:T(8,128)(2,1)S(1)}, bf16[2,256,256]{2,1,0:T(8,128)(2,1)S(1)}, u32[]{:S(2)}, u32[]{:S(2)}) collective-permute-start(bf16[2,256,256]{2,1,0:T(8,128)(2,1)S(1)} %get-tuple-element.29), channel_id=1, source_target_pairs={{0,24},{8,16},{16,8},{24,0},{1,25},{9,17},{17,9},{25,1},{2,26},{10... | collective-permute-start | bytes 786440 | tf_op jit(solution)/shard_map/ppermute | solution.py:23
  217.8 13.4 %collective-permute-start.20 = (bf16[2,256,256]{2,1,0:T(8,128)(2,1)S(1)}, bf16[2,256,256]{2,1,0:T(8,128)(2,1)S(1)}, u32[]{:S(2)}, u32[]{:S(2)}) collective-permute-start(bf16[2,256,256]{2,1,0:T(8,128)(2,1)S(1)} %get-tuple-element.29), channel_id=1, source_target_pairs={{0,8},{8,0},{16,24},{24,16},{1,9},{9,1},{17,25},{25,17},{2,10},{10... | collective-permute-start | bytes 786440 | tf_op jit(solution)/shard_map/ppermute | solution.py:23
  219.9 27.5 %collective-permute-start.34 = (bf16[2,256,256]{2,1,0:T(8,128)(2,1)}, bf16[2,256,256]{2,1,0:T(8,128)(2,1)S(1)}, u32[]{:S(2)}, u32[]{:S(2)}) collective-permute-start(bf16[2,256,256]{2,1,0:T(8,128)(2,1)} %get-tuple-element.24), channel_id=1, source_target_pairs={{0,24},{8,16},{16,8},{24,0},{1,25},{9,17},{17,9},{25,1},{2,26},{10... | collective-permute-start | bytes 786440 | tf_op jit(solution)/shard_map/ppermute | solution.py:23
  221.4 26.7 %collective-permute-start.35 = (bf16[2,256,256]{2,1,0:T(8,128)(2,1)}, bf16[2,256,256]{2,1,0:T(8,128)(2,1)S(1)}, u32[]{:S(2)}, u32[]{:S(2)}) collective-permute-start(bf16[2,256,256]{2,1,0:T(8,128)(2,1)} %get-tuple-element.24), channel_id=1, source_target_pairs={{0,8},{8,0},{16,24},{24,16},{1,9},{9,1},{17,25},{25,17},{2,10},{10... | collective-permute-start | bytes 786440 | tf_op jit(solution)/shard_map/ppermute | solution.py:23
  222.0 26.9 %collective-permute-start.36 = (bf16[2,256,256]{2,1,0:T(8,128)(2,1)}, bf16[2,256,256]{2,1,0:T(8,128)(2,1)S(1)}, u32[]{:S(2)}, u32[]{:S(2)}) collective-permute-start(bf16[2,256,256]{2,1,0:T(8,128)(2,1)} %get-tuple-element.24), channel_id=1, source_target_pairs={{0,16},{8,24},{16,0},{24,8},{1,17},{9,25},{17,1},{25,9},{2,18},{10... | collective-permute-start | bytes 786440 | tf_op jit(solution)/shard_map/ppermute | solution.py:23
  225.7 15.5 %collective-permute-start.21 = (bf16[2,256,256]{2,1,0:T(8,128)(2,1)S(1)}, bf16[2,256,256]{2,1,0:T(8,128)(2,1)S(1)}, u32[]{:S(2)}, u32[]{:S(2)}) collective-permute-start(bf16[2,256,256]{2,1,0:T(8,128)(2,1)S(1)} %get-tuple-element.29), channel_id=1, source_target_pairs={{0,16},{8,24},{16,0},{24,8},{1,17},{9,25},{17,1},{25,9},{2,18},{10... | collective-permute-start | bytes 786440 | tf_op jit(solution)/shard_map/ppermute | solution.py:23
  243.8 19.0 %all-to-all-start = ((bf16[8,128,1,256]{1,3,2,0:T(8,128)(2,1)}), bf16[8,128,1,256]{1,3,2,0:T(8,128)(2,1)S(1)}, u32[]{:S(2)}, u32[]{:S(2)}) async-start(bf16[8,128,1,256]{1,3,2,0:T(8,128)(2,1)} %copy.55), calls=%async_computation | async-start | bytes 1048576 | tf_op jit(solution)/shard_map/all_to_all | solution.py:159
  262.7 18.8 %all-to-all-start.1 = ((bf16[8,128,1,256]{1,3,2,0:T(8,128)(2,1)}), bf16[8,128,1,256]{1,3,2,0:T(8,128)(2,1)S(1)}, u32[]{:S(2)}, u32[]{:S(2)}) async-start(bf16[8,128,1,256]{1,3,2,0:T(8,128)(2,1)} %copy.62), calls=%async_computation.1 | async-start | bytes 1048576 | tf_op jit(solution)/shard_map/all_to_all | solution.py:159
  268.7 19.0 %collective-permute-start.28 = (bf16[128,2048]{0,1:T(8,128)(2,1)S(1)}, bf16[128,2048]{0,1:T(8,128)(2,1)}, u32[]{:S(2)}, u32[]{:S(2)}) collective-permute-start(bf16[128,2048]{0,1:T(8,128)(2,1)S(1)} %bitcast.335), channel_id=1, source_target_pairs={{0,24},{8,16},{16,8},{24,0},{1,25},{9,17},{17,9},{25,1},{2,26},{10... | collective-permute-start | bytes 1572872 | tf_op jit(solution)/shard_map/ppermute | solution.py:23
  271.3 24.6 %collective-permute-start.29 = (bf16[128,2048]{0,1:T(8,128)(2,1)S(1)}, bf16[128,2048]{0,1:T(8,128)(2,1)}, u32[]{:S(2)}, u32[]{:S(2)}) collective-permute-start(bf16[128,2048]{0,1:T(8,128)(2,1)S(1)} %bitcast.336), channel_id=1, source_target_pairs={{0,8},{8,0},{16,24},{24,16},{1,9},{9,1},{17,25},{25,17},{2,10},{10... | collective-permute-start | bytes 1572872 | tf_op jit(solution)/shard_map/ppermute | solution.py:23
  271.8 26.2 %collective-permute-start.30 = (bf16[128,2048]{0,1:T(8,128)(2,1)S(1)}, bf16[128,2048]{0,1:T(8,128)(2,1)}, u32[]{:S(2)}, u32[]{:S(2)}) collective-permute-start(bf16[128,2048]{0,1:T(8,128)(2,1)S(1)} %bitcast.337), channel_id=1, source_target_pairs={{0,16},{8,24},{16,0},{24,8},{1,17},{9,25},{17,1},{25,9},{2,18},{10... | collective-permute-start | bytes 1572872 | tf_op jit(solution)/shard_map/ppermute | solution.py:23
  282.5 28.5 %collective-permute-start.37 = (bf16[128,2048]{1,0:T(8,128)(2,1)}, bf16[128,2048]{1,0:T(8,128)(2,1)}, u32[]{:S(2)}, u32[]{:S(2)}) collective-permute-start(bf16[128,2048]{1,0:T(8,128)(2,1)} %copy.64), channel_id=1, source_target_pairs={{0,24},{8,16},{16,8},{24,0},{1,25},{9,17},{17,9},{25,1},{2,26},{10... | collective-permute-start | bytes 1572872 | tf_op jit(solution)/shard_map/ppermute | solution.py:23
  285.1 32.8 %collective-permute-start.38 = (bf16[128,2048]{1,0:T(8,128)(2,1)}, bf16[128,2048]{1,0:T(8,128)(2,1)}, u32[]{:S(2)}, u32[]{:S(2)}) collective-permute-start(bf16[128,2048]{1,0:T(8,128)(2,1)} %copy.64), channel_id=1, source_target_pairs={{0,8},{8,0},{16,24},{24,16},{1,9},{9,1},{17,25},{25,17},{2,10},{10... | collective-permute-start | bytes 1572872 | tf_op jit(solution)/shard_map/ppermute | solution.py:23
  287.7 31.3 %collective-permute-start.39 = (bf16[128,2048]{1,0:T(8,128)(2,1)}, bf16[128,2048]{1,0:T(8,128)(2,1)}, u32[]{:S(2)}, u32[]{:S(2)}) collective-permute-start(bf16[128,2048]{1,0:T(8,128)(2,1)} %copy.64), channel_id=1, source_target_pairs={{0,16},{8,24},{16,0},{24,8},{1,17},{9,25},{17,1},{25,9},{2,18},{10... | collective-permute-start | bytes 1572872 | tf_op jit(solution)/shard_map/ppermute | solution.py:23
  (24 other events, 213.7 us)
Sparse Core Ops, SparseCore 0:
  69.0 52.1 all-gather.7
  122.8 46.6 all-gather.5
  171.6 80.2 all-gather.3

commit v4 on v3

--- a/solution.py
+++ b/solution.py
@@ -27,28 +27,47 @@
     return sorted(range(1, count), key=lambda mask: -mask.bit_count())
 
 
-def scatter_sum(parts, axis):
-    count = parts.shape[axis]
+def halve(parts, reverse):
+    count = parts.shape[0]
     me = lax.axis_index("rows")
-    got = [
-        swap(lax.dynamic_index_in_dim(parts, me ^ mask, axis, False), count, mask)
-        for mask in partners(count)
-    ]
-    total = lax.dynamic_index_in_dim(parts, me, axis, False).astype(f32)
-    for term in got:
-        total = total + term.astype(f32)
-    return total, got[0]
+    bits = list(range(count.bit_length() - 1))
+    held = bits[::-1]
+    parts = parts.reshape((2,) * len(held) + parts.shape[1:])
+    for bit in bits[::-1] if reverse else bits:
+        axis = held.index(bit)
+        mine = (me >> bit) & 1
+        got = swap(lax.dynamic_index_in_dim(parts, 1 - mine, axis, False), count, 1 << bit)
+        kept = lax.dynamic_index_in_dim(parts, mine, axis, False)
+        held.remove(bit)
+        total = kept.astype(f32) + got.astype(f32)
+        parts = total.astype(bf16) if held else total
+    return parts
+
+
+def scatter_sum(parts):
+    cut = parts.shape[1] // 2
+    return jnp.concatenate([halve(parts[:, :cut], False), halve(parts[:, cut:], True)], 0)
 
 
 def gather(block, count, before=None):
     me = lax.axis_index("rows")
-    got = [(mask, swap(block, count, mask)) for mask in partners(count)]
+    held = {0: block}
+    bits = [1 << b for b in range(count.bit_length() - 1)]
+    for bit in bits[:-2]:
+        held.update({mask ^ bit: swap(held[mask], count, bit) for mask in list(held)})
+    low, high = bits[-2:]
+    near = {m ^ b: swap(held[m], count, b) for b in (low, high) for m in list(held)}
+    cut = block.shape[0] // 2
+    far = {
+        m ^ low ^ high: jnp.concatenate(
+            [swap(near[m ^ low][:cut], count, high), swap(near[m ^ high][cut:], count, low)], 0
+        )
+        for m in held
+    }
     if before is not None:
         block, _ = lax.optimization_barrier((block, before))
-    whole = lax.dynamic_update_index_in_dim(
-        jnp.zeros((count,) + block.shape, block.dtype), block, me, 0
-    )
-    for mask, term in got:
+    whole = jnp.zeros((count,) + block.shape, block.dtype)
+    for mask, term in {**held, **near, **far, 0: block}.items():
         whole = lax.dynamic_update_index_in_dim(whole, term, me ^ mask, 0)
     return whole
 
@@ -100,10 +119,10 @@
         both = jnp.where(core == 0, jnp.stack([block, other]), jnp.stack([other, block]))
         parts = product(both, left_pair).reshape(2, rows, sub, 2 * width)
         mark = parts
-        sums, got = scatter_sum(parts, 1)
+        sums = scatter_sum(parts.swapaxes(0, 1))
         sums = sums.astype(bf16)
         if step == half - 2:
-            later, _, _ = lax.optimization_barrier((later, ahead, got))
+            later, ahead = lax.optimization_barrier((later, ahead))
         if step < half - 1:
             block, _ = lax.optimization_barrier((ahead, sums))
         got = lax.ppermute(sums[..., :width], "cols", [(i, i ^ 2) for i in range(cols)])
@@ -125,45 +144,34 @@
 
         dealt = deal(right_basis.reshape(per, rows, sub, width)).reshape(depth, width)
         half, dealt, mark = rotate_left(forget_grad, left_basis, dealt, rows, cols)
-        late, left, _ = lax.optimization_barrier((dealt[:, mid:], left_basis, mark))
-        basis = [lax.all_gather(x, "cols", axis=1, tiled=True) for x in (dealt[:, :mid], late)]
+        left, half = lax.optimization_barrier((left_basis, half))
+        right_rows = lax.all_gather(dealt, "cols", axis=1, tiled=True)
         left_rows = lax.all_gather(left, "cols", axis=1, tiled=True)
+        left_rows = left_rows.reshape(depth, cols, 2, mid)
 
-        first = first_moment.reshape(per, 2, mid, width)
-        second = second_moment.reshape(per, 2, mid, width)
-
-        def turn(c, span):
+        values = []
+        for span in spans:
             parts = lax.dot_general(
-                basis[c], half[:, span], (((0,), (0,)), ((), ())), preferred_element_type=f32
+                right_rows, half[:, span], (((0,), (0,)), ((), ())), preferred_element_type=f32
             ).astype(bf16)
-            return -scatter_sum(rows_first(parts).reshape(rows, per, mid, -1), 0)[0]
-
-        def normalize(c, span, value):
-            new_first = beta_first * first[:, c, :, span] + (1.0 - beta_first) * value
-            new_second = beta_second * second[:, c, :, span] + (1.0 - beta_second) * value * value
-            normal = new_first / corr_first / (jnp.sqrt(new_second / corr_second) + epsilon)
-            return gather(normal.astype(bf16), rows).reshape(cols * mid, -1)
-
-        value = turn(0, slice(0, width))
-        back = jnp.dot(basis[0], normalize(0, slice(0, width), value), preferred_element_type=f32)
-        values = [turn(1, span) for span in spans]
-        rotated = jnp.stack([value, jnp.concatenate(values, 2)], 1).reshape(depth, width)
+            values.append(-scatter_sum(rows_first(parts).reshape(rows, depth, mid)))
+        rotated = jnp.concatenate(values, 1)
 
         step_dir = None
-        left_rows = left_rows.reshape(depth, cols, 2, mid)
-        term = back
-        for c, span in enumerate(spans):
-            normals, _ = lax.optimization_barrier((normalize(1, span, values[c]), term))
-            term = jnp.dot(basis[1], normals, preferred_element_type=f32) + back[:, span]
-            term = rows_first(term.astype(bf16)).reshape(cols, sub, mid)
-            full = lax.all_to_all(term, "cols", 0, 1).reshape(sub, cols * mid)
-            full = lax.dot_general(
+        for c, (span, value) in enumerate(zip(spans, values)):
+            new_first = beta_first * first_moment[:, span] + (1.0 - beta_first) * value
+            new_second = beta_second * second_moment[:, span] + (1.0 - beta_second) * value * value
+            normal = new_first / corr_first / (jnp.sqrt(new_second / corr_second) + epsilon)
+            normals = gather(normal.astype(bf16), rows).reshape(rows * depth, mid)
+            term = jnp.dot(right_rows, normals, preferred_element_type=f32).astype(bf16)
+            term = lax.all_to_all(rows_first(term).reshape(cols, sub, mid), "cols", 0, 1)
+            term = lax.dot_general(
                 left_rows[:, :, c].reshape(depth, cols * mid),
-                gather(full, rows, step_dir).reshape(width, cols * mid),
+                gather(term.reshape(sub, cols * mid), rows).reshape(width, cols * mid),
                 (((1,), (1,)), ((), ())),
                 preferred_element_type=f32,
             )
-            step_dir = full if step_dir is None else step_dir + full
+            step_dir = term if step_dir is None else step_dir + term
         step_dir = step_dir.astype(bf16)
 
         new_first = beta_first * first_moment + (1.0 - beta_first) * rotated

time: 331 us -> 329 us (level)
  local copies, waits for them, and re-layouts: 41.5 us -> 29.1 us
  waiting for transfers between devices: 153 us -> 160 us
    ppermute x33 -> x35, waiting for transfers between devices: 112 us -> 87.1 us  [swap(): return lax.ppermute(block, 'rows', [(i, i ^ mask) for i in range(count)])]
    ppermute x2, waiting for transfers between devices: 5.92 us -> 25.6 us  [rotate_left(): lax.ppermute(sums[..., :width], 'cols', [(i, i ^ 2) for i in range(cols)])]
    all_gather x2 -> x1, waiting for transfers between devices: 0.01 us -> 7.36 us  [local(): right_rows = lax.all_gather(dealt, 'cols', axis=1, tiled=True)]
    dynamic_update_slice x15 -> x11, local copies, waits for them, and re-layouts: 8.04 us -> 4.21 us  [gather(): whole = lax.dynamic_update_index_in_dim(whole, term, me ^ mask, 0)]
    slice x3 -> x11, local copies, waits for them, and re-layouts: 1.15 us -> 4.66 us  [the longest x4 2.7 us: gather(): near[m ^ high][cut:]]
    ppermute x33 -> x35, starting transfers between devices: 38.5 us -> 39 us  [swap(): return lax.ppermute(block, 'rows', [(i, i ^ mask) for i in range(count)])]
    dot_general x8 -> x6, matrix products: 26.3 us -> 26 us  [the longest x2 9.44 us: local(): term = jnp.dot(right_rows, normals, preferred_element_type=f32).astype(bf16)]
  transfers between devices with their start and end apart: 45 -> 46, of which waited for: 23 -> 25; matrix products, arithmetic and copies ran while one was open for 25% -> 23% of each run, Pallas kernels for 0% -> 0%
where the time goes in v4:
time: 329 us; the launch traced here: 327 us
  waiting for transfers between devices  160 us (49%)
  starting transfers between devices  72.6 us (22%)
  matrix products  35.4 us (11%)
  local copies, waits for them, and re-layouts  29.1 us (9%)
  other arithmetic  15.2 us (5%)
  between operations  14.9 us (5%)
    ppermute x35, waiting for transfers between devices, swap(): return lax.ppermute(block, 'rows', [(i, i ^ mask) for i in range(count)])  87.1 us
    ppermute x35, starting transfers between devices, swap(): return lax.ppermute(block, 'rows', [(i, i ^ mask) for i in range(count)])  39 us
    ppermute x2, waiting for transfers between devices, rotate_left(): lax.ppermute(sums[..., :width], 'cols', [(i, i ^ 2) for i in range(cols)])  25.6 us
    ppermute x2, waiting for transfers between devices, along(): return lax.ppermute(value, 'cols', route)  21.2 us
    ppermute x2, starting transfers between devices, along(): return lax.ppermute(value, 'cols', route)  17.3 us
    all_to_all x2, waiting for transfers between devices, local(): lax.all_to_all(rows_first(term).reshape(cols, sub, mid), 'cols', 0, 1)  13.1 us
    dot_general x2, matrix products, local(): term = jnp.dot(right_rows, normals, preferred_element_type=f32).astype(bf16)  9.44 us
    dot_general x2, matrix products, product(): lax.dot_general(blocks, left, (((1,), (0,)), ((), ())), preferred_element...  9.39 us
  transfers between devices with their start and end apart: 46, of which 25 were waited for; matrix products, arithmetic and copies ran while one was open for 23% of the time, Pallas kernels for 0%

profile of v4, /device:TPU:0, one launch (start us, length us, event | category | flops | bytes accessed | tf_op | source)
XLA Modules:
  0.0 327.1 jit_solution(134227010655222640)
XLA Ops:
  7.2 3.1 collective-permute-start.1
  11.6 2.5 collective-permute-start.2
  14.1 9.5 %collective-permute-start = (bf16[1024,512]{1,0:T(8,128)(2,1)}, bf16[1024,512]{1,0:T(8,128)(2,1)}, u32[]{:S(2)}, u32[]{:S(2)}) collective-permute-start(bf16[1024,512]{1,0:T(8,128)(2,1)} %param.5), channel_id=1, source_target_pairs={{0,0},{1,1},{4,2},{5,3},{2,4},{3,5},{6,6},{7,7},{8,8},{9,9},{12,10... | collective-permute-start | bytes 3145736 | tf_op jit(solution)/shard_map/ppermute | solution.py:110
  25.7 5.3 %collective-permute-done.3 = bf16[2,128,512]{2,1,0:T(8,128)(2,1)S(1)} collective-permute-done((bf16[2,128,512]{2,1,0:T(8,128)(2,1)S(1)}, bf16[2,128,512]{2,1,0:T(8,128)(2,1)S(1)}, u32[]{:S(2)}, u32[]{:S(2)}) %collective-permute-start.3) | collective-permute-done | bytes 262176 | tf_op jit(solution)/shard_map/ppermute | solution.py:23
  31.3 2.4 collective-permute-done.1
  35.3 7.8 %collective-permute-start.11 = (bf16[1024,512]{1,0:T(8,128)(2,1)}, bf16[1024,512]{1,0:T(8,128)(2,1)}, u32[]{:S(2)}, u32[]{:S(2)}) collective-permute-start(bf16[1024,512]{1,0:T(8,128)(2,1)} %param.5), channel_id=1, source_target_pairs={{0,4},{1,5},{4,6},{5,7},{2,0},{3,1},{6,2},{7,3},{8,12},{9,13},{12,... | collective-permute-start | bytes 3145736 | tf_op jit(solution)/shard_map/ppermute | solution.py:110
  43.2 21.2 %collective-permute-done.11 = bf16[1024,512]{1,0:T(8,128)(2,1)} collective-permute-done((bf16[1024,512]{1,0:T(8,128)(2,1)}, bf16[1024,512]{1,0:T(8,128)(2,1)}, u32[]{:S(2)}, u32[]{:S(2)}) %collective-permute-start.11) | collective-permute-done | bytes 1048608 | tf_op jit(solution)/shard_map/ppermute | solution.py:110
  64.6 3.0 collective-permute-done.5
  67.6 4.7 %fusion.20 = bf16[2,512,1024]{2,1,0:T(8,128)(2,1)S(1)} fusion(bf16[1024,1024]{1,0:T(8,128)(2,1)S(1)} %pad_maximum_fusion, bf16[1,1024,512]{2,1,0:T(8,128)(2,1)} %bitcast.10, bf16[1,1024,512]{2,1,0:T(8,128)(2,1)} %bitcast.9, pred[]{:T(512)S(6)} %eq.4), kind=kOutput, calls=%fused_computation.27 | convolution fusion | flops 2151677952 | bytes 6291457 | tf_op jit(solution)/shard_map/dot_general | solution.py:90
  75.3 12.4 %collective-permute-done.8 = bf16[2,1,128,1024]{3,2,0,1:T(8,128)(2,1)} collective-permute-done((bf16[2,1,128,1024]{3,2,0,1:T(8,128)(2,1)}, bf16[2,1,128,1024]{3,2,0,1:T(8,128)(2,1)}, u32[]{:S(2)}, u32[]{:S(2)}) %collective-permute-start.8) | collective-permute-done | bytes 524320 | tf_op jit(solution)/shard_map/ppermute | solution.py:23
  92.2 4.7 %fusion.17 = bf16[2,512,1024]{2,1,0:T(8,128)(2,1)S(1)} fusion(bf16[1024,1024]{1,0:T(8,128)(2,1)S(1)} %copy-done.13, bf16[1,1024,512]{2,1,0:T(8,128)(2,1)} %bitcast.28, bf16[1,1024,512]{2,1,0:T(8,128)(2,1)} %bitcast.27, pred[]{:T(512)S(6)} %eq.4), kind=kOutput, calls=%fused_computation.26 | convolution fusion | flops 2151677952 | bytes 6291457 | tf_op jit(solution)/shard_map/dot_general | solution.py:90
  98.2 1.6 collective-permute-start.13
  99.8 2.6 collective-permute-start.10
  102.4 8.2 %collective-permute-done.15 = bf16[2,1,128,1024]{3,2,0,1:T(8,128)(2,1)S(1)} collective-permute-done((bf16[2,1,128,1024]{3,2,0,1:T(8,128)(2,1)S(1)}, bf16[2,1,128,1024]{3,2,0,1:T(8,128)(2,1)S(1)}, u32[]{:S(2)}, u32[]{:S(2)}) %collective-permute-start.15) | collective-permute-done | bytes 524320 | tf_op jit(solution)/shard_map/ppermute | solution.py:23
  113.0 4.8 %collective-permute-done.16 = bf16[1,128,1024]{2,1,0:T(8,128)(2,1)S(1)} collective-permute-done((bf16[1,128,1024]{2,1,0:T(8,128)(2,1)S(1)}, bf16[1,128,1024]{2,1,0:T(8,128)(2,1)S(1)}, u32[]{:S(2)}, u32[]{:S(2)}) %collective-permute-start.16) | collective-permute-done | bytes 262176 | tf_op jit(solution)/shard_map/ppermute | solution.py:23
  118.3 2.6 collective-permute-start.17
  120.9 11.8 %collective-permute-done.10 = bf16[2,128,512]{2,1,0:T(8,128)(2,1)S(1)} collective-permute-done((bf16[2,128,512]{2,1,0:T(8,128)(2,1)S(1)}, bf16[2,128,512]{2,1,0:T(8,128)(2,1)S(1)}, u32[]{:S(2)}, u32[]{:S(2)}) %collective-permute-start.10) | collective-permute-done | bytes 262176 | tf_op jit(solution)/shard_map/ppermute | solution.py:128
  132.8 13.7 %collective-permute-done.17 = bf16[2,128,512]{2,1,0:T(8,128)(2,1)S(1)} collective-permute-done((bf16[2,128,512]{2,1,0:T(8,128)(2,1)S(1)}, bf16[2,128,512]{2,1,0:T(8,128)(2,1)S(1)}, u32[]{:S(2)}, u32[]{:S(2)}) %collective-permute-start.17) | collective-permute-done | bytes 262176 | tf_op jit(solution)/shard_map/ppermute | solution.py:128
  147.8 7.4 %all-gather.5.cloned.1.call-done = bf16[1024,4096]{1,0:T(8,128)(2,1)} async-done(((bf16[1024,512]{1,0:T(8,128)(2,1)}), bf16[1024,4096]{1,0:T(8,128)(2,1)}) %all-gather.5.cloned.1.call-update) | async-done | bytes 8388624 | tf_op jit(solution)/shard_map/all_gather | solution.py:148
  155.2 6.0 %convolution_convert_fusion = bf16[4096,256]{1,0:T(8,128)(2,1)S(1)} fusion(bf16[1024,4096]{1,0:T(8,128)(2,1)} %all-gather.5.cloned.1.call-done, bf16[1024,512]{1,0:T(8,128)(2,1)S(1)} %bitcast.243), kind=kOutput, calls=%fused_computation | convolution fusion | flops 2148532224 | bytes 11010048 | tf_op jit(solution)/shard_map/dot_general | solution.py:154
  163.0 1.5 collective-permute-start.32
  164.5 2.5 convolution_convert_fusion.1
  168.5 7.7 %collective-permute-done.30 = bf16[2,512,256]{2,1,0:T(8,128)(2,1)S(1)} collective-permute-done((bf16[2,512,256]{2,1,0:T(8,128)(2,1)S(1)}, bf16[2,512,256]{2,1,0:T(8,128)(2,1)S(1)}, u32[]{:S(2)}, u32[]{:S(2)}) %collective-permute-start.30) | collective-permute-done | bytes 524320 | tf_op jit(solution)/shard_map/ppermute | solution.py:23
  176.4 1.5 collective-permute-start.31
  179.7 7.8 %collective-permute-done.18 = bf16[2,512,256]{2,1,0:T(8,128)(2,1)S(1)} collective-permute-done((bf16[2,512,256]{2,1,0:T(8,128)(2,1)S(1)}, bf16[2,512,256]{2,1,0:T(8,128)(2,1)S(1)}, u32[]{:S(2)}, u32[]{:S(2)}) %collective-permute-start.18) | collective-permute-done | bytes 524320 | tf_op jit(solution)/shard_map/ppermute | solution.py:23
  191.0 3.8 %collective-permute-done.31 = bf16[512,256]{1,0:T(8,128)(2,1)S(1)} collective-permute-done((bf16[512,256]{1,0:T(8,128)(2,1)S(1)}, bf16[512,256]{1,0:T(8,128)(2,1)S(1)}, u32[]{:S(2)}, u32[]{:S(2)}) %collective-permute-start.31) | collective-permute-done | bytes 262176 | tf_op jit(solution)/shard_map/ppermute | solution.py:23
  197.9 2.4 collective-permute-done.19
  203.6 7.2 %collective-permute-done.34 = bf16[1024,256]{1,0:T(8,128)(2,1)S(1)} collective-permute-done((bf16[1024,256]{1,0:T(8,128)(2,1)S(1)}, bf16[1024,256]{1,0:T(8,128)(2,1)S(1)}, u32[]{:S(2)}, u32[]{:S(2)}) %collective-permute-start.34) | collective-permute-done | bytes 524320 | tf_op jit(solution)/shard_map/ppermute | solution.py:23
  210.8 1.5 collective-permute-start.36
  213.1 8.9 %collective-permute-done.22 = bf16[1024,256]{1,0:T(8,128)(2,1)S(1)} collective-permute-done((bf16[1024,256]{1,0:T(8,128)(2,1)S(1)}, bf16[1024,256]{1,0:T(8,128)(2,1)S(1)}, u32[]{:S(2)}, u32[]{:S(2)}) %collective-permute-start.22) | collective-permute-done | bytes 524320 | tf_op jit(solution)/shard_map/ppermute | solution.py:23
  224.5 3.9 %collective-permute-done.36 = bf16[512,256]{1,0:T(8,128)(2,1)S(1)} collective-permute-done((bf16[512,256]{1,0:T(8,128)(2,1)S(1)}, bf16[512,256]{1,0:T(8,128)(2,1)S(1)}, u32[]{:S(2)}, u32[]{:S(2)}) %collective-permute-start.36) | collective-permute-done | bytes 262176 | tf_op jit(solution)/shard_map/ppermute | solution.py:23
  228.4 4.6 %collective-permute-done.24 = bf16[512,256]{1,0:T(8,128)(2,1)S(1)} collective-permute-done((bf16[512,256]{1,0:T(8,128)(2,1)S(1)}, bf16[512,256]{1,0:T(8,128)(2,1)S(1)}, u32[]{:S(2)}, u32[]{:S(2)}) %collective-permute-start.24) | collective-permute-done | bytes 262176 | tf_op jit(solution)/shard_map/ppermute | solution.py:23
  233.1 2.3 convolution_convert_fusion.2
  236.7 3.8 %all-to-all-start.1 = ((bf16[8,128,1,256]{1,3,2,0:T(8,128)(2,1)}), bf16[8,128,1,256]{1,3,2,0:T(8,128)(2,1)S(1)}, u32[]{:S(2)}, u32[]{:S(2)}) async-start(bf16[8,128,1,256]{1,3,2,0:T(8,128)(2,1)} %copy.45), calls=%async_computation.1 | async-start | bytes 1048576 | tf_op jit(solution)/shard_map/all_to_all | solution.py:167
  240.5 7.1 %convolution_convert_fusion.3 = bf16[1024,256]{1,0:T(8,128)(2,1)} fusion(bf16[1024,4096]{1,0:T(8,128)(2,1)} %all-gather.5.cloned.1.call-done, bf16[4096,256]{1,0:T(8,128)(2,1)} %bitcast.234), kind=kOutput, calls=%fused_computation.31 | convolution fusion | flops 2147745792 | bytes 11010048 | tf_op jit(solution)/shard_map/dot_general | solution.py:166
  247.6 2.0 copy.39
  249.7 6.2 %all-to-all-done.1 = bf16[8,128,1,256]{1,3,2,0:T(8,128)(2,1)S(1)} async-done(((bf16[8,128,1,256]{1,3,2,0:T(8,128)(2,1)}), bf16[8,128,1,256]{1,3,2,0:T(8,128)(2,1)S(1)}, u32[]{:S(2)}, u32[]{:S(2)}) %all-to-all-start.1) | async-done | bytes 524320 | tf_op jit(solution)/shard_map/all_to_all | solution.py:167
  255.9 4.1 %all-to-all-start = ((bf16[8,128,1,256]{1,3,2,0:T(8,128)(2,1)}), bf16[8,128,1,256]{1,3,2,0:T(8,128)(2,1)}, u32[]{:S(2)}, u32[]{:S(2)}) async-start(bf16[8,128,1,256]{1,3,2,0:T(8,128)(2,1)} %copy.39), calls=%async_computation | async-start | bytes 1048576 | tf_op jit(solution)/shard_map/all_to_all | solution.py:167
  262.6 2.8 fusion
  268.5 6.9 %all-to-all-done = bf16[8,128,1,256]{1,3,2,0:T(8,128)(2,1)} async-done(((bf16[8,128,1,256]{1,3,2,0:T(8,128)(2,1)}), bf16[8,128,1,256]{1,3,2,0:T(8,128)(2,1)}, u32[]{:S(2)}, u32[]{:S(2)}) %all-to-all-start) | async-done | bytes 524320 | tf_op jit(solution)/shard_map/all_to_all | solution.py:167
  277.4 6.0 %fusion.63 = (bf16[1024,8,1,256]{0,3,2,1:T(8,128)(2,1)}, bf16[1024,8,1,256]{0,3,2,1:T(8,128)(2,1)}) fusion(bf16[1024,8,2,256]{0,3,2,1:T(8,128)(2,1)} %bitcast.210), kind=kLoop, calls=%fused_computation.138 | loop fusion | bytes 16777216 | tf_op jit(solution)/shard_map/slice | solution.py:169
  287.3 1.7 slice.135
  290.5 2.7 collective-permute-done.27
  298.5 1.9 bitcast_dynamic-update-slice_fusion.1
  300.4 1.9 bitcast_dynamic-update-slice_fusion
  302.6 6.4 %collective-permute-done.29 = bf16[64,2048]{0,1:T(8,128)(2,1)} collective-permute-done((bf16[64,2048]{0,1:T(8,128)(2,1)}, bf16[64,2048]{0,1:T(8,128)(2,1)}, u32[]{:S(2)}, u32[]{:S(2)}) %collective-permute-start.29) | collective-permute-done | bytes 262176 | tf_op jit(solution)/shard_map/ppermute | solution.py:23
  311.1 4.7 %fusion.68 = f32[1024,512]{1,0:T(8,128)S(1)} fusion(bf16[1024,2048]{0,1:T(8,128)(2,1)} %bitcast.231, bf16[512,2048]{1,0:T(8,128)(2,1)S(1)} %bitcast.232), kind=kOutput, calls=%fused_computation.143 | convolution fusion | flops 2147483648 | bytes 8388608 | tf_op jit(solution)/shard_map/dot_general | solution.py:168
  316.9 3.4 %add_convert_fusion = bf16[1024,512]{1,0:T(8,128)(2,1)} fusion(f32[1024,512]{1,0:T(8,128)S(1)} %fusion.68, bf16[1024,2048]{0,1:T(8,128)(2,1)S(1)} %bitcast.230, bf16[512,2048]{1,0:T(8,128)(2,1)S(1)} %bitcast.235), kind=kOutput, calls=%fused_computation.23 | convolution fusion | flops 2148532224 | bytes 9437184 | tf_op jit(solution)/shard_map/dot_general | solution.py:168
  (174 shorter events, 59.4 us)
Async XLA Ops:
  7.2 148.0 %all-gather.5.cloned.1.call-start = ((), (), s32[]{:S(2)}) async-start(), calls=%async_computation.3 | async-start | bytes 9437184 | tf_op jit(solution)/shard_map/all_gather | solution.py:148
  7.2 26.6 %collective-permute-start.1 = (bf16[1024,512]{1,0:T(8,128)(2,1)}, bf16[1024,512]{1,0:T(8,128)(2,1)}, u32[]{:S(2)}, u32[]{:S(2)}) collective-permute-start(bf16[1024,512]{1,0:T(8,128)(2,1)} %param.6), channel_id=1, source_target_pairs={{0,2},{1,3},{2,0},{3,1},{4,6},{5,7},{6,4},{7,5},{8,10},{9,11},{10,... | collective-permute-start | bytes 3145736 | tf_op jit(solution)/shard_map/ppermute | solution.py:102
  10.3 23.5 %copy-start.7 = (bf16[1024,512]{1,0:T(8,128)(2,1)S(1)}, bf16[1024,512]{1,0:T(8,128)(2,1)}, u32[]{:S(2)}) copy-start(bf16[1024,512]{1,0:T(8,128)(2,1)} %param.6) | copy-start | bytes 3145732
  11.6 14.1 %collective-permute-start.2 = (bf16[2,128,512]{2,1,0:T(8,128)(2,1)S(1)}, bf16[2,128,512]{2,1,0:T(8,128)(2,1)S(1)}, u32[]{:S(2)}, u32[]{:S(2)}) collective-permute-start(bf16[2,128,512]{2,1,0:T(8,128)(2,1)S(1)} %get-tuple-element.39), channel_id=1, source_target_pairs={{0,24},{8,16},{16,8},{24,0},{1,25},{9,17},{17,9},{25,1},{2,26},{10... | collective-permute-start | bytes 786440 | tf_op jit(solution)/shard_map/ppermute | solution.py:23
  14.1 21.3 %collective-permute-start = (bf16[1024,512]{1,0:T(8,128)(2,1)}, bf16[1024,512]{1,0:T(8,128)(2,1)}, u32[]{:S(2)}, u32[]{:S(2)}) collective-permute-start(bf16[1024,512]{1,0:T(8,128)(2,1)} %param.5), channel_id=1, source_target_pairs={{0,0},{1,1},{4,2},{5,3},{2,4},{3,5},{6,6},{7,7},{8,8},{9,9},{12,10... | collective-permute-start | bytes 3145736 | tf_op jit(solution)/shard_map/ppermute | solution.py:110
  23.6 7.5 %collective-permute-start.3 = (bf16[2,128,512]{2,1,0:T(8,128)(2,1)S(1)}, bf16[2,128,512]{2,1,0:T(8,128)(2,1)S(1)}, u32[]{:S(2)}, u32[]{:S(2)}) collective-permute-start(bf16[2,128,512]{2,1,0:T(8,128)(2,1)S(1)} %get-tuple-element.38), channel_id=1, source_target_pairs={{0,8},{8,0},{16,24},{24,16},{1,9},{9,1},{17,25},{25,17},{2,10},{10... | collective-permute-start | bytes 786440 | tf_op jit(solution)/shard_map/ppermute | solution.py:23
  24.1 7.2 %collective-permute-start.4 = (bf16[2,128,512]{2,1,0:T(8,128)(2,1)S(1)}, bf16[2,128,512]{2,1,0:T(8,128)(2,1)S(1)}, u32[]{:S(2)}, u32[]{:S(2)}) collective-permute-start(bf16[2,128,512]{2,1,0:T(8,128)(2,1)S(1)} %get-tuple-element.37), channel_id=1, source_target_pairs={{0,16},{8,24},{16,0},{24,8},{1,17},{9,25},{17,1},{25,9},{2,18},{10... | collective-permute-start | bytes 786440 | tf_op jit(solution)/shard_map/ppermute | solution.py:23
  35.3 36.9 %copy-start.12 = (bf16[1024,1024]{1,0:T(8,128)(2,1)}, bf16[1024,1024]{1,0:T(8,128)(2,1)S(1)}, u32[]{:S(2)}) copy-start(bf16[1024,1024]{1,0:T(8,128)(2,1)S(1)} %pad_maximum_fusion) | copy-start | bytes 6291460
  35.3 29.1 %collective-permute-start.11 = (bf16[1024,512]{1,0:T(8,128)(2,1)}, bf16[1024,512]{1,0:T(8,128)(2,1)}, u32[]{:S(2)}, u32[]{:S(2)}) collective-permute-start(bf16[1024,512]{1,0:T(8,128)(2,1)} %param.5), channel_id=1, source_target_pairs={{0,4},{1,5},{4,6},{5,7},{2,0},{3,1},{6,2},{7,3},{8,12},{9,13},{12,... | collective-permute-start | bytes 3145736 | tf_op jit(solution)/shard_map/ppermute | solution.py:110
  64.5 213.0 %all-gather.3.cloned.1.call-start = ((), (), s32[]{:S(2)}) async-start(), calls=%async_computation.2 | async-start | bytes 9437184 | tf_op jit(solution)/shard_map/all_gather | solution.py:149
  64.5 3.1 collective-permute-start.5
  73.4 14.3 %collective-permute-start.8 = (bf16[2,1,128,1024]{3,2,0,1:T(8,128)(2,1)}, bf16[2,1,128,1024]{3,2,0,1:T(8,128)(2,1)}, u32[]{:S(2)}, u32[]{:S(2)}) collective-permute-start(bf16[2,1,128,1024]{3,2,0,1:T(8,128)(2,1)} %dynamic-slice_bitcast_fusion.6), channel_id=1, source_target_pairs={{0,16},{8,24},{16,0},{24,8},{1,17},{9,25},{17,1},{25,9},{2,18},{10... | collective-permute-start | bytes 1572872 | tf_op jit(solution)/shard_map/ppermute | solution.py:23
  73.9 18.3 %collective-permute-start.12 = (bf16[1024,512]{1,0:T(8,128)(2,1)}, bf16[1024,512]{1,0:T(8,128)(2,1)}, u32[]{:S(2)}, u32[]{:S(2)}) collective-permute-start(bf16[1024,512]{1,0:T(8,128)(2,1)} %collective-permute-done.11), channel_id=1, source_target_pairs={{0,1},{1,0},{2,3},{3,2},{4,5},{5,4},{6,7},{7,6},{8,9},{9,8},{10,11... | collective-permute-start | bytes 3145736 | tf_op jit(solution)/shard_map/ppermute | solution.py:118
  74.7 14.8 %collective-permute-start.6 = (bf16[2,1,128,1024]{3,2,1,0:T(8,128)(2,1)}, bf16[2,1,128,1024]{3,2,1,0:T(8,128)(2,1)}, u32[]{:S(2)}, u32[]{:S(2)}) collective-permute-start(bf16[2,1,128,1024]{3,2,1,0:T(8,128)(2,1)} %dynamic-slice_bitcast_fusion.7), channel_id=1, source_target_pairs={{0,8},{8,0},{16,24},{24,16},{1,9},{9,1},{17,25},{25,17},{2,10},{10... | collective-permute-start | bytes 1572872 | tf_op jit(solution)/shard_map/ppermute | solution.py:23
  89.0 9.1 %collective-permute-start.9 = (bf16[1,128,1024]{2,1,0:T(8,128)(2,1)S(1)}, bf16[1,128,1024]{2,1,0:T(8,128)(2,1)S(1)}, u32[]{:S(2)}, u32[]{:S(2)}) collective-permute-start(bf16[1,128,1024]{2,1,0:T(8,128)(2,1)S(1)} %dynamic-slice_bitcast_fusion.14), channel_id=1, source_target_pairs={{0,8},{8,0},{16,24},{24,16},{1,9},{9,1},{17,25},{25,17},{2,10},{10... | collective-permute-start | bytes 786440 | tf_op jit(solution)/shard_map/ppermute | solution.py:23
  90.8 8.9 %collective-permute-start.7 = (bf16[1,128,1024]{2,1,0:T(8,128)(2,1)S(1)}, bf16[1,128,1024]{2,1,0:T(8,128)(2,1)S(1)}, u32[]{:S(2)}, u32[]{:S(2)}) collective-permute-start(bf16[1,128,1024]{2,1,0:T(8,128)(2,1)S(1)} %dynamic-slice_bitcast_fusion.15), channel_id=1, source_target_pairs={{0,16},{8,24},{16,0},{24,8},{1,17},{9,25},{17,1},{25,9},{2,18},{10... | collective-permute-start | bytes 786440 | tf_op jit(solution)/shard_map/ppermute | solution.py:23
  97.3 13.3 %collective-permute-start.15 = (bf16[2,1,128,1024]{3,2,0,1:T(8,128)(2,1)S(1)}, bf16[2,1,128,1024]{3,2,0,1:T(8,128)(2,1)S(1)}, u32[]{:S(2)}, u32[]{:S(2)}) collective-permute-start(bf16[2,1,128,1024]{3,2,0,1:T(8,128)(2,1)S(1)} %dynamic-slice_bitcast_fusion.4), channel_id=1, source_target_pairs={{0,16},{8,24},{16,0},{24,8},{1,17},{9,25},{17,1},{25,9},{2,18},{10... | collective-permute-start | bytes 1572872 | tf_op jit(solution)/shard_map/ppermute | solution.py:23
  98.2 13.3 %collective-permute-start.13 = (bf16[2,1,128,1024]{3,2,1,0:T(8,128)(2,1)S(1)}, bf16[2,1,128,1024]{3,2,1,0:T(8,128)(2,1)S(1)}, u32[]{:S(2)}, u32[]{:S(2)}) collective-permute-start(bf16[2,1,128,1024]{3,2,1,0:T(8,128)(2,1)S(1)} %dynamic-slice_bitcast_fusion.5), channel_id=1, source_target_pairs={{0,8},{8,0},{16,24},{24,16},{1,9},{9,1},{17,25},{25,17},{2,10},{10... | collective-permute-start | bytes 1572872 | tf_op jit(solution)/shard_map/ppermute | solution.py:23
  99.8 32.9 %collective-permute-start.10 = (bf16[2,128,512]{2,1,0:T(8,128)(2,1)S(1)}, bf16[2,128,512]{2,1,0:T(8,128)(2,1)S(1)}, u32[]{:S(2)}, u32[]{:S(2)}) collective-permute-start(bf16[2,128,512]{2,1,0:T(8,128)(2,1)S(1)} %fusion.58), channel_id=1, source_target_pairs={{0,2},{1,3},{2,0},{3,1},{4,6},{5,7},{6,4},{7,5},{8,10},{9,11},{10,... | collective-permute-start | bytes 786440 | tf_op jit(solution)/shard_map/ppermute | solution.py:128
  110.8 6.9 %collective-permute-start.16 = (bf16[1,128,1024]{2,1,0:T(8,128)(2,1)S(1)}, bf16[1,128,1024]{2,1,0:T(8,128)(2,1)S(1)}, u32[]{:S(2)}, u32[]{:S(2)}) collective-permute-start(bf16[1,128,1024]{2,1,0:T(8,128)(2,1)S(1)} %dynamic-slice_bitcast_fusion.12), channel_id=1, source_target_pairs={{0,8},{8,0},{16,24},{24,16},{1,9},{9,1},{17,25},{25,17},{2,10},{10... | collective-permute-start | bytes 786440 | tf_op jit(solution)/shard_map/ppermute | solution.py:23
  111.7 6.5 %collective-permute-start.14 = (bf16[1,128,1024]{2,1,0:T(8,128)(2,1)S(1)}, bf16[1,128,1024]{2,1,0:T(8,128)(2,1)S(1)}, u32[]{:S(2)}, u32[]{:S(2)}) collective-permute-start(bf16[1,128,1024]{2,1,0:T(8,128)(2,1)S(1)} %dynamic-slice_bitcast_fusion.13), channel_id=1, source_target_pairs={{0,16},{8,24},{16,0},{24,8},{1,17},{9,25},{17,1},{25,9},{2,18},{10... | collective-permute-start | bytes 786440 | tf_op jit(solution)/shard_map/ppermute | solution.py:23
  118.3 28.2 %collective-permute-start.17 = (bf16[2,128,512]{2,1,0:T(8,128)(2,1)S(1)}, bf16[2,128,512]{2,1,0:T(8,128)(2,1)S(1)}, u32[]{:S(2)}, u32[]{:S(2)}) collective-permute-start(bf16[2,128,512]{2,1,0:T(8,128)(2,1)S(1)} %pad_maximum_fusion.3), channel_id=1, source_target_pairs={{0,2},{1,3},{2,0},{3,1},{4,6},{5,7},{6,4},{7,5},{8,10},{9,11},{10,... | collective-permute-start | bytes 786440 | tf_op jit(solution)/shard_map/ppermute | solution.py:128
  161.4 14.8 %collective-permute-start.30 = (bf16[2,512,256]{2,1,0:T(8,128)(2,1)S(1)}, bf16[2,512,256]{2,1,0:T(8,128)(2,1)S(1)}, u32[]{:S(2)}, u32[]{:S(2)}) collective-permute-start(bf16[2,512,256]{2,1,0:T(8,128)(2,1)S(1)} %dynamic-slice_bitcast_fusion.1), channel_id=1, source_target_pairs={{0,8},{8,0},{16,24},{24,16},{1,9},{9,1},{17,25},{25,17},{2,10},{10... | collective-permute-start | bytes 1572872 | tf_op jit(solution)/shard_map/ppermute | solution.py:23
  163.0 15.0 %collective-permute-start.32 = (bf16[2,512,256]{2,1,0:T(8,128)(2,1)S(1)}, bf16[2,512,256]{2,1,0:T(8,128)(2,1)S(1)}, u32[]{:S(2)}, u32[]{:S(2)}) collective-permute-start(bf16[2,512,256]{2,1,0:T(8,128)(2,1)S(1)} %dynamic-slice_bitcast_fusion), channel_id=1, source_target_pairs={{0,16},{8,24},{16,0},{24,8},{1,17},{9,25},{17,1},{25,9},{2,18},{10... | collective-permute-start | bytes 1572872 | tf_op jit(solution)/shard_map/ppermute | solution.py:23
  167.2 20.2 %collective-permute-start.18 = (bf16[2,512,256]{2,1,0:T(8,128)(2,1)S(1)}, bf16[2,512,256]{2,1,0:T(8,128)(2,1)S(1)}, u32[]{:S(2)}, u32[]{:S(2)}) collective-permute-start(bf16[2,512,256]{2,1,0:T(8,128)(2,1)S(1)} %dynamic-slice_bitcast_fusion.3), channel_id=1, source_target_pairs={{0,8},{8,0},{16,24},{24,16},{1,9},{9,1},{17,25},{25,17},{2,10},{10... | collective-permute-start | bytes 1572872 | tf_op jit(solution)/shard_map/ppermute | solution.py:23
  167.9 21.3 %collective-permute-start.20 = (bf16[2,512,256]{2,1,0:T(8,128)(2,1)S(1)}, bf16[2,512,256]{2,1,0:T(8,128)(2,1)S(1)}, u32[]{:S(2)}, u32[]{:S(2)}) collective-permute-start(bf16[2,512,256]{2,1,0:T(8,128)(2,1)S(1)} %dynamic-slice_bitcast_fusion.2), channel_id=1, source_target_pairs={{0,16},{8,24},{16,0},{24,8},{1,17},{9,25},{17,1},{25,9},{2,18},{10... | collective-permute-start | bytes 1572872 | tf_op jit(solution)/shard_map/ppermute | solution.py:23
  176.4 18.3 %collective-permute-start.31 = (bf16[512,256]{1,0:T(8,128)(2,1)S(1)}, bf16[512,256]{1,0:T(8,128)(2,1)S(1)}, u32[]{:S(2)}, u32[]{:S(2)}) collective-permute-start(bf16[512,256]{1,0:T(8,128)(2,1)S(1)} %dynamic-slice_bitcast_fusion.9), channel_id=1, source_target_pairs={{0,16},{8,24},{16,0},{24,8},{1,17},{9,25},{17,1},{25,9},{2,18},{10... | collective-permute-start | bytes 786440 | tf_op jit(solution)/shard_map/ppermute | solution.py:23
  178.1 16.7 %collective-permute-start.33 = (bf16[512,256]{1,0:T(8,128)(2,1)S(1)}, bf16[512,256]{1,0:T(8,128)(2,1)S(1)}, u32[]{:S(2)}, u32[]{:S(2)}) collective-permute-start(bf16[512,256]{1,0:T(8,128)(2,1)S(1)} %dynamic-slice_bitcast_fusion.8), channel_id=1, source_target_pairs={{0,8},{8,0},{16,24},{24,16},{1,9},{9,1},{17,25},{25,17},{2,10},{10... | collective-permute-start | bytes 786440 | tf_op jit(solution)/shard_map/ppermute | solution.py:23
  187.7 12.7 %collective-permute-start.19 = (bf16[512,256]{1,0:T(8,128)(2,1)S(1)}, bf16[512,256]{1,0:T(8,128)(2,1)S(1)}, u32[]{:S(2)}, u32[]{:S(2)}) collective-permute-start(bf16[512,256]{1,0:T(8,128)(2,1)S(1)} %dynamic-slice_bitcast_fusion.11), channel_id=1, source_target_pairs={{0,16},{8,24},{16,0},{24,8},{1,17},{9,25},{17,1},{25,9},{2,18},{10... | collective-permute-start | bytes 786440 | tf_op jit(solution)/shard_map/ppermute | solution.py:23
  189.4 11.0 %collective-permute-start.21 = (bf16[512,256]{1,0:T(8,128)(2,1)S(1)}, bf16[512,256]{1,0:T(8,128)(2,1)S(1)}, u32[]{:S(2)}, u32[]{:S(2)}) collective-permute-start(bf16[512,256]{1,0:T(8,128)(2,1)S(1)} %dynamic-slice_bitcast_fusion.10), channel_id=1, source_target_pairs={{0,8},{8,0},{16,24},{24,16},{1,9},{9,1},{17,25},{25,17},{2,10},{10... | collective-permute-start | bytes 786440 | tf_op jit(solution)/shard_map/ppermute | solution.py:23
  195.8 14.9 %collective-permute-start.34 = (bf16[1024,256]{1,0:T(8,128)(2,1)S(1)}, bf16[1024,256]{1,0:T(8,128)(2,1)S(1)}, u32[]{:S(2)}, u32[]{:S(2)}) collective-permute-start(bf16[1024,256]{1,0:T(8,128)(2,1)S(1)} %get-tuple-element.22), channel_id=1, source_target_pairs={{0,8},{8,0},{16,24},{24,16},{1,9},{9,1},{17,25},{25,17},{2,10},{10... | collective-permute-start | bytes 1572872 | tf_op jit(solution)/shard_map/ppermute | solution.py:23
  196.5 15.9 %collective-permute-start.35 = (bf16[1024,256]{1,0:T(8,128)(2,1)S(1)}, bf16[1024,256]{1,0:T(8,128)(2,1)S(1)}, u32[]{:S(2)}, u32[]{:S(2)}) collective-permute-start(bf16[1024,256]{1,0:T(8,128)(2,1)S(1)} %get-tuple-element.22), channel_id=1, source_target_pairs={{0,16},{8,24},{16,0},{24,8},{1,17},{9,25},{17,1},{25,9},{2,18},{10... | collective-permute-start | bytes 1572872 | tf_op jit(solution)/shard_map/ppermute | solution.py:23
  201.5 20.5 %collective-permute-start.22 = (bf16[1024,256]{1,0:T(8,128)(2,1)S(1)}, bf16[1024,256]{1,0:T(8,128)(2,1)S(1)}, u32[]{:S(2)}, u32[]{:S(2)}) collective-permute-start(bf16[1024,256]{1,0:T(8,128)(2,1)S(1)} %get-tuple-element.24), channel_id=1, source_target_pairs={{0,8},{8,0},{16,24},{24,16},{1,9},{9,1},{17,25},{25,17},{2,10},{10... | collective-permute-start | bytes 1572872 | tf_op jit(solution)/shard_map/ppermute | solution.py:23
  202.1 21.5 %collective-permute-start.23 = (bf16[1024,256]{1,0:T(8,128)(2,1)S(1)}, bf16[1024,256]{1,0:T(8,128)(2,1)S(1)}, u32[]{:S(2)}, u32[]{:S(2)}) collective-permute-start(bf16[1024,256]{1,0:T(8,128)(2,1)S(1)} %get-tuple-element.24), channel_id=1, source_target_pairs={{0,16},{8,24},{16,0},{24,8},{1,17},{9,25},{17,1},{25,9},{2,18},{10... | collective-permute-start | bytes 1572872 | tf_op jit(solution)/shard_map/ppermute | solution.py:23
  210.8 17.6 %collective-permute-start.36 = (bf16[512,256]{1,0:T(8,128)(2,1)S(1)}, bf16[512,256]{1,0:T(8,128)(2,1)S(1)}, u32[]{:S(2)}, u32[]{:S(2)}) collective-permute-start(bf16[512,256]{1,0:T(8,128)(2,1)S(1)} %slice.132), channel_id=1, source_target_pairs={{0,16},{8,24},{16,0},{24,8},{1,17},{9,25},{17,1},{25,9},{2,18},{10... | collective-permute-start | bytes 786440 | tf_op jit(solution)/shard_map/ppermute | solution.py:23
  212.4 16.1 %collective-permute-start.37 = (bf16[512,256]{1,0:T(8,128)(2,1)S(1)}, bf16[512,256]{1,0:T(8,128)(2,1)S(1)}, u32[]{:S(2)}, u32[]{:S(2)}) collective-permute-start(bf16[512,256]{1,0:T(8,128)(2,1)S(1)} %slice.133), channel_id=1, source_target_pairs={{0,8},{8,0},{16,24},{24,16},{1,9},{9,1},{17,25},{25,17},{2,10},{10... | collective-permute-start | bytes 786440 | tf_op jit(solution)/shard_map/ppermute | solution.py:23
  222.0 11.0 %collective-permute-start.24 = (bf16[512,256]{1,0:T(8,128)(2,1)S(1)}, bf16[512,256]{1,0:T(8,128)(2,1)S(1)}, u32[]{:S(2)}, u32[]{:S(2)}) collective-permute-start(bf16[512,256]{1,0:T(8,128)(2,1)S(1)} %slice.125), channel_id=1, source_target_pairs={{0,16},{8,24},{16,0},{24,8},{1,17},{9,25},{17,1},{25,9},{2,18},{10... | collective-permute-start | bytes 786440 | tf_op jit(solution)/shard_map/ppermute | solution.py:23
  223.6 9.5 %collective-permute-start.25 = (bf16[512,256]{1,0:T(8,128)(2,1)S(1)}, bf16[512,256]{1,0:T(8,128)(2,1)S(1)}, u32[]{:S(2)}, u32[]{:S(2)}) collective-permute-start(bf16[512,256]{1,0:T(8,128)(2,1)S(1)} %slice.126), channel_id=1, source_target_pairs={{0,8},{8,0},{16,24},{24,16},{1,9},{9,1},{17,25},{25,17},{2,10},{10... | collective-permute-start | bytes 786440 | tf_op jit(solution)/shard_map/ppermute | solution.py:23
  236.7 19.2 %all-to-all-start.1 = ((bf16[8,128,1,256]{1,3,2,0:T(8,128)(2,1)}), bf16[8,128,1,256]{1,3,2,0:T(8,128)(2,1)S(1)}, u32[]{:S(2)}, u32[]{:S(2)}) async-start(bf16[8,128,1,256]{1,3,2,0:T(8,128)(2,1)} %copy.45), calls=%async_computation.1 | async-start | bytes 1048576 | tf_op jit(solution)/shard_map/all_to_all | solution.py:167
  255.9 19.5 %all-to-all-start = ((bf16[8,128,1,256]{1,3,2,0:T(8,128)(2,1)}), bf16[8,128,1,256]{1,3,2,0:T(8,128)(2,1)}, u32[]{:S(2)}, u32[]{:S(2)}) async-start(bf16[8,128,1,256]{1,3,2,0:T(8,128)(2,1)} %copy.39), calls=%async_computation | async-start | bytes 1048576 | tf_op jit(solution)/shard_map/all_to_all | solution.py:167
  266.4 19.1 %collective-permute-start.38 = (bf16[128,2048]{1,0:T(8,128)(2,1)}, bf16[128,2048]{1,0:T(8,128)(2,1)}, u32[]{:S(2)}, u32[]{:S(2)}) collective-permute-start(bf16[128,2048]{1,0:T(8,128)(2,1)} %copy.47), channel_id=1, source_target_pairs={{0,8},{8,0},{16,24},{24,16},{1,9},{9,1},{17,25},{25,17},{2,10},{10... | collective-permute-start | bytes 1572872 | tf_op jit(solution)/shard_map/ppermute | solution.py:23
  267.0 20.3 %collective-permute-start.39 = (bf16[128,2048]{1,0:T(8,128)(2,1)}, bf16[128,2048]{1,0:T(8,128)(2,1)}, u32[]{:S(2)}, u32[]{:S(2)}) collective-permute-start(bf16[128,2048]{1,0:T(8,128)(2,1)} %copy.47), channel_id=1, source_target_pairs={{0,16},{8,24},{16,0},{24,8},{1,17},{9,25},{17,1},{25,9},{2,18},{10... | collective-permute-start | bytes 1572872 | tf_op jit(solution)/shard_map/ppermute | solution.py:23
  275.4 17.8 %collective-permute-start.27 = (bf16[128,2048]{0,1:T(8,128)(2,1)}, bf16[128,2048]{0,1:T(8,128)(2,1)S(1)}, u32[]{:S(2)}, u32[]{:S(2)}) collective-permute-start(bf16[128,2048]{0,1:T(8,128)(2,1)} %bitcast.68), channel_id=1, source_target_pairs={{0,16},{8,24},{16,0},{24,8},{1,17},{9,25},{17,1},{25,9},{2,18},{10... | collective-permute-start | bytes 1572872 | tf_op jit(solution)/shard_map/ppermute | solution.py:23
  276.9 18.8 %collective-permute-start.26 = (bf16[128,2048]{0,1:T(8,128)(2,1)}, bf16[128,2048]{0,1:T(8,128)(2,1)}, u32[]{:S(2)}, u32[]{:S(2)}) collective-permute-start(bf16[128,2048]{0,1:T(8,128)(2,1)} %bitcast.68), channel_id=1, source_target_pairs={{0,8},{8,0},{16,24},{24,16},{1,9},{9,1},{17,25},{25,17},{2,10},{10... | collective-permute-start | bytes 1572872 | tf_op jit(solution)/shard_map/ppermute | solution.py:23
  286.7 29.1 %collective-permute-start.40 = (bf16[64,2048]{1,0:T(8,128)(2,1)S(1)}, bf16[64,2048]{1,0:T(8,128)(2,1)}, u32[]{:S(2)}, u32[]{:S(2)}) collective-permute-start(bf16[64,2048]{1,0:T(8,128)(2,1)S(1)} %slice.134), channel_id=1, source_target_pairs={{0,16},{8,24},{16,0},{24,8},{1,17},{9,25},{17,1},{25,9},{2,18},{10... | collective-permute-start | bytes 786440 | tf_op jit(solution)/shard_map/ppermute | solution.py:23
  289.0 26.8 %collective-permute-start.41 = (bf16[64,2048]{1,0:T(8,128)(2,1)}, bf16[64,2048]{1,0:T(8,128)(2,1)}, u32[]{:S(2)}, u32[]{:S(2)}) collective-permute-start(bf16[64,2048]{1,0:T(8,128)(2,1)} %slice.135), channel_id=1, source_target_pairs={{0,8},{8,0},{16,24},{24,16},{1,9},{9,1},{17,25},{25,17},{2,10},{10... | collective-permute-start | bytes 786440 | tf_op jit(solution)/shard_map/ppermute | solution.py:23
  294.2 14.8 %collective-permute-start.29 = (bf16[64,2048]{0,1:T(8,128)(2,1)}, bf16[64,2048]{0,1:T(8,128)(2,1)}, u32[]{:S(2)}, u32[]{:S(2)}) collective-permute-start(bf16[64,2048]{0,1:T(8,128)(2,1)} %slice.128), channel_id=1, source_target_pairs={{0,8},{8,0},{16,24},{24,16},{1,9},{9,1},{17,25},{25,17},{2,10},{10... | collective-permute-start | bytes 786440 | tf_op jit(solution)/shard_map/ppermute | solution.py:23
  295.7 13.6 %collective-permute-start.28 = (bf16[64,2048]{0,1:T(8,128)(2,1)}, bf16[64,2048]{0,1:T(8,128)(2,1)}, u32[]{:S(2)}, u32[]{:S(2)}) collective-permute-start(bf16[64,2048]{0,1:T(8,128)(2,1)} %bitcast.209), channel_id=1, source_target_pairs={{0,16},{8,24},{16,0},{24,8},{1,17},{9,25},{17,1},{25,9},{2,18},{10... | collective-permute-start | bytes 786440 | tf_op jit(solution)/shard_map/ppermute | solution.py:23
  (13 other events, 63.8 us)
Sparse Core Ops, SparseCore 0:
  64.6 90.5 all-gather.4
  157.4 82.1 all-gather.2

commit v5 on v4

--- a/solution.py
+++ b/solution.py
@@ -65,11 +65,11 @@
         for m in held
     }
     if before is not None:
-        block, _ = lax.optimization_barrier((block, before))
+        block, before = lax.optimization_barrier((block, before))
     whole = jnp.zeros((count,) + block.shape, block.dtype)
     for mask, term in {**held, **near, **far, 0: block}.items():
         whole = lax.dynamic_update_index_in_dim(whole, term, me ^ mask, 0)
-    return whole
+    return whole if before is None else (whole, before)
 
 
 def deal(parts):
@@ -113,12 +113,10 @@
     block = along(0, grad)
     for step in range(half):
         if step < half - 1:
-            grad, block, left_pair, later = lax.optimization_barrier((grad, block, left_pair, later))
             ahead = along(step + 1, grad)
         other = lax.ppermute(block, "cols", [(i, i ^ 1) for i in range(cols)])
         both = jnp.where(core == 0, jnp.stack([block, other]), jnp.stack([other, block]))
         parts = product(both, left_pair).reshape(2, rows, sub, 2 * width)
-        mark = parts
         sums = scatter_sum(parts.swapaxes(0, 1))
         sums = sums.astype(bf16)
         if step == half - 2:
@@ -131,7 +129,7 @@
             whole = lax.dynamic_update_slice(
                 whole, value[None, None], (half_index, chip, 0, 0, 0)
             )
-    return whole.reshape(depth, width), later, mark
+    return whole.reshape(depth, width), later
 
 
 def make_local(rows, cols):
@@ -143,35 +141,50 @@
         spans = (slice(0, mid), slice(mid, width))
 
         dealt = deal(right_basis.reshape(per, rows, sub, width)).reshape(depth, width)
-        half, dealt, mark = rotate_left(forget_grad, left_basis, dealt, rows, cols)
+        half, dealt = rotate_left(forget_grad, left_basis, dealt, rows, cols)
         left, half = lax.optimization_barrier((left_basis, half))
         right_rows = lax.all_gather(dealt, "cols", axis=1, tiled=True)
         left_rows = lax.all_gather(left, "cols", axis=1, tiled=True)
         left_rows = left_rows.reshape(depth, cols, 2, mid)
 
-        values = []
-        for span in spans:
-            parts = lax.dot_general(
-                right_rows, half[:, span], (((0,), (0,)), ((), ())), preferred_element_type=f32
-            ).astype(bf16)
-            values.append(-scatter_sum(rows_first(parts).reshape(rows, depth, mid)))
+        parts = [
+            rows_first(
+                lax.dot_general(
+                    right_rows, half[:, span], (((0,), (0,)), ((), ())), preferred_element_type=f32
+                ).astype(bf16)
+            ).reshape(rows, depth, mid)
+            for span in spans
+        ]
+        value, parts[1] = lax.optimization_barrier((scatter_sum(parts[0]), parts[1]))
+        values = [value, scatter_sum(parts[1])]
+        values = [-value for value in values]
         rotated = jnp.concatenate(values, 1)
 
-        step_dir = None
-        for c, (span, value) in enumerate(zip(spans, values)):
-            new_first = beta_first * first_moment[:, span] + (1.0 - beta_first) * value
-            new_second = beta_second * second_moment[:, span] + (1.0 - beta_second) * value * value
-            normal = new_first / corr_first / (jnp.sqrt(new_second / corr_second) + epsilon)
-            normals = gather(normal.astype(bf16), rows).reshape(rows * depth, mid)
-            term = jnp.dot(right_rows, normals, preferred_element_type=f32).astype(bf16)
-            term = lax.all_to_all(rows_first(term).reshape(cols, sub, mid), "cols", 0, 1)
-            term = lax.dot_general(
+        def finish(term, c):
+            term = lax.all_to_all(term.reshape(cols, sub, mid), "cols", 0, 1)
+            return lax.dot_general(
                 left_rows[:, :, c].reshape(depth, cols * mid),
                 gather(term.reshape(sub, cols * mid), rows).reshape(width, cols * mid),
                 (((1,), (1,)), ((), ())),
                 preferred_element_type=f32,
             )
-            step_dir = term if step_dir is None else step_dir + term
+
+        step_dir = None
+        last = None
+        for c, (span, value) in enumerate(zip(spans, values)):
+            new_first = beta_first * first_moment[:, span] + (1.0 - beta_first) * value
+            new_second = beta_second * second_moment[:, span] + (1.0 - beta_second) * value * value
+            normal = new_first / corr_first / (jnp.sqrt(new_second / corr_second) + epsilon)
+            if last is None:
+                normals = gather(normal.astype(bf16), rows)
+            else:
+                normals, last = gather(normal.astype(bf16), rows, last)
+            normals = normals.reshape(rows * depth, mid)
+            if last is not None:
+                step_dir = finish(last, 0)
+            term = jnp.dot(right_rows, normals, preferred_element_type=f32).astype(bf16)
+            last = rows_first(term)
+        step_dir = (step_dir + finish(last, 1))
         step_dir = step_dir.astype(bf16)
 
         new_first = beta_first * first_moment + (1.0 - beta_first) * rotated

time: 329 us -> 324 us (0.985)
  other arithmetic: 15.2 us -> 9.38 us
  local copies, waits for them, and re-layouts: 29.1 us -> 34.6 us
  matrix products: 35.4 us -> 31.5 us
    ppermute x1, waiting for transfers between devices: 2.44 us -> 57.2 us  [rotate_left(): lax.ppermute(left, 'cols', [(i, i ^ 2) for i in range(cols)])]
    ppermute x2, waiting for transfers between devices: 25.6 us -> 9 us  [rotate_left(): lax.ppermute(sums[..., :width], 'cols', [(i, i ^ 2) for i in range(cols)])]
    ppermute x2, waiting for transfers between devices: 21.2 us -> 7.04 us  [along(): return lax.ppermute(value, 'cols', route)]
    all_to_all x2, waiting for transfers between devices: 13.1 us -> 0.01 us  [finish(): term = lax.all_to_all(term.reshape(cols, sub, mid), 'cols', 0, 1)]
    ppermute x2, starting transfers between devices: 17.3 us -> 5.97 us  [along(): return lax.ppermute(value, 'cols', route)]
    all_gather x1, waiting for transfers between devices: 7.36 us -> 0.02 us  [local(): right_rows = lax.all_gather(dealt, 'cols', axis=1, tiled=True)]
    ppermute x2, starting transfers between devices: 5.15 us -> 9.22 us  [rotate_left(): lax.ppermute(sums[..., :width], 'cols', [(i, i ^ 2) for i in range(cols)])]
  transfers between devices with their start and end apart: 46 -> 46, of which waited for: 25 -> 28; matrix products, arithmetic and copies ran while one was open for 23% -> 21% of each run, Pallas kernels for 0% -> 0%
where the time goes in v5:
time: 324 us; the launch traced here: 323 us
  waiting for transfers between devices  162 us (50%)
  starting transfers between devices  70.8 us (22%)
  local copies, waits for them, and re-layouts  34.6 us (11%)
  matrix products  31.5 us (10%)
  between operations  14.7 us (5%)
  other arithmetic  9.38 us (3%)
    ppermute x35, waiting for transfers between devices, swap(): return lax.ppermute(block, 'rows', [(i, i ^ mask) for i in range(count)])  88.6 us
    ppermute x1, waiting for transfers between devices, rotate_left(): lax.ppermute(left, 'cols', [(i, i ^ 2) for i in range(cols)])  57.2 us
    ppermute x35, starting transfers between devices, swap(): return lax.ppermute(block, 'rows', [(i, i ^ mask) for i in range(count)])  40.2 us
    all_to_all x2, starting transfers between devices, finish(): term = lax.all_to_all(term.reshape(cols, sub, mid), 'cols', 0, 1)  10.7 us
    ppermute x2, starting transfers between devices, rotate_left(): lax.ppermute(sums[..., :width], 'cols', [(i, i ^ 2) for i in range(cols)])  9.22 us
    ppermute x2, waiting for transfers between devices, rotate_left(): lax.ppermute(sums[..., :width], 'cols', [(i, i ^ 2) for i in range(cols)])  9 us
    dot_general x2, matrix products, local(): term = jnp.dot(right_rows, normals, preferred_element_type=f32).astype(bf16)  8.87 us
    dot_general x2, matrix products, product(): lax.dot_general(blocks, left, (((1,), (0,)), ((), ())), preferred_element...  8.55 us
  transfers between devices with their start and end apart: 46, of which 28 were waited for; matrix products, arithmetic and copies ran while one was open for 21% of the time, Pallas kernels for 0%

profile of v5, /device:TPU:0, one launch (start us, length us, event | category | flops | bytes accessed | tf_op | source)
XLA Modules:
  0.0 323.0 jit_solution(11134276676461176872)
XLA Ops:
  7.2 4.1 %collective-permute-start.11 = (bf16[1024,512]{1,0:T(8,128)(2,1)}, bf16[1024,512]{1,0:T(8,128)(2,1)}, u32[]{:S(2)}, u32[]{:S(2)}) collective-permute-start(bf16[1024,512]{1,0:T(8,128)(2,1)} %param.5), channel_id=1, source_target_pairs={{0,4},{1,5},{4,6},{5,7},{2,0},{3,1},{6,2},{7,3},{8,12},{9,13},{12,... | collective-permute-start | bytes 3145736 | tf_op jit(solution)/shard_map/ppermute | solution.py:110
  12.5 2.5 collective-permute-start.8
  17.2 5.6 %collective-permute-done.8 = bf16[2,128,512]{2,1,0:T(8,128)(2,1)} collective-permute-done((bf16[2,128,512]{2,1,0:T(8,128)(2,1)S(1)}, bf16[2,128,512]{2,1,0:T(8,128)(2,1)}, u32[]{:S(2)}, u32[]{:S(2)}) %collective-permute-start.8) | collective-permute-done | bytes 262176 | tf_op jit(solution)/shard_map/ppermute | solution.py:23
  23.8 3.1 collective-permute-done.9
  27.0 7.0 %collective-permute-done.11 = bf16[1024,512]{1,0:T(8,128)(2,1)} collective-permute-done((bf16[1024,512]{1,0:T(8,128)(2,1)}, bf16[1024,512]{1,0:T(8,128)(2,1)}, u32[]{:S(2)}, u32[]{:S(2)}) %collective-permute-start.11) | collective-permute-done | bytes 1048608 | tf_op jit(solution)/shard_map/ppermute | solution.py:110
  34.1 1.9 collective-permute-start
  36.0 4.0 %collective-permute-start.2 = (bf16[1024,512]{1,0:T(8,128)(2,1)S(1)}, bf16[1024,512]{1,0:T(8,128)(2,1)S(1)}, u32[]{:S(2)}, u32[]{:S(2)}) collective-permute-start(bf16[1024,512]{1,0:T(8,128)(2,1)S(1)} %copy-done.10), channel_id=1, source_target_pairs={{0,2},{1,3},{2,0},{3,1},{4,6},{5,7},{6,4},{7,5},{8,10},{9,11},{10,... | collective-permute-start | bytes 3145736 | tf_op jit(solution)/shard_map/ppermute | solution.py:102
  40.6 57.2 %collective-permute-done.2 = bf16[1024,512]{1,0:T(8,128)(2,1)S(1)} collective-permute-done((bf16[1024,512]{1,0:T(8,128)(2,1)S(1)}, bf16[1024,512]{1,0:T(8,128)(2,1)S(1)}, u32[]{:S(2)}, u32[]{:S(2)}) %collective-permute-start.2) | collective-permute-done | bytes 1048608 | tf_op jit(solution)/shard_map/ppermute | solution.py:102
  97.8 4.6 %fusion.15 = bf16[2,512,1024]{2,1,0:T(8,128)(2,1)S(1)} fusion(bf16[1,1024,512]{2,1,0:T(8,128)(2,1)} %bitcast.28, bf16[1,1024,512]{2,1,0:T(8,128)(2,1)} %bitcast.27, pred[]{:T(512)S(6)} %eq.4, bf16[1024,512]{1,0:T(8,128)(2,1)S(1)} %copy-done.10, bf16[1024,512]{1,0:T(8,128)(2,1)S(1)} %collective-permute-done.2), kind=kOutput, calls=%fused_computation.24 | convolution fusion | flops 2155872256 | bytes 6291457 | tf_op jit(solution)/shard_map/dot_general | solution.py:90
  104.3 4.0 %fusion.16 = bf16[2,512,1024]{2,1,0:T(8,128)(2,1)S(1)} fusion(bf16[1,1024,512]{2,1,0:T(8,128)(2,1)} %bitcast.1, bf16[1,1024,512]{2,1,0:T(8,128)(2,1)S(1)} %bitcast.242, pred[]{:T(512)S(6)} %eq.4, bf16[1024,512]{1,0:T(8,128)(2,1)S(1)} %copy-done.10, bf16[1024,512]{1,0:T(8,128)(2,1)S(1)} %collective-permute-done.2), kind=kOutput, calls=%fused_computation.25 | convolution fusion | flops 2155872256 | bytes 6291457 | tf_op jit(solution)/shard_map/dot_general | solution.py:90
  113.7 6.6 %collective-permute-done.5 = bf16[2,1,128,1024]{3,2,0,1:T(8,128)(2,1)S(1)} collective-permute-done((bf16[2,1,128,1024]{3,2,0,1:T(8,128)(2,1)S(1)}, bf16[2,1,128,1024]{3,2,0,1:T(8,128)(2,1)S(1)}, u32[]{:S(2)}, u32[]{:S(2)}) %collective-permute-start.5) | collective-permute-done | bytes 524320 | tf_op jit(solution)/shard_map/ppermute | solution.py:23
  122.1 6.7 %collective-permute-done.3 = bf16[2,1,128,1024]{3,2,1,0:T(8,128)(2,1)S(1)} collective-permute-done((bf16[2,1,128,1024]{3,2,1,0:T(8,128)(2,1)S(1)}, bf16[2,1,128,1024]{3,2,1,0:T(8,128)(2,1)S(1)}, u32[]{:S(2)}, u32[]{:S(2)}) %collective-permute-start.3) | collective-permute-done | bytes 524320 | tf_op jit(solution)/shard_map/ppermute | solution.py:23
  129.1 1.6 collective-permute-start.4
  131.5 3.0 collective-permute-done.6
  135.6 8.4 %collective-permute-start.7 = (bf16[2,128,512]{2,1,0:T(8,128)(2,1)S(1)}, bf16[2,128,512]{2,1,0:T(8,128)(2,1)S(1)}, u32[]{:S(2)}, u32[]{:S(2)}) collective-permute-start(bf16[2,128,512]{2,1,0:T(8,128)(2,1)S(1)} %fusion.52), channel_id=1, source_target_pairs={{0,2},{1,3},{2,0},{3,1},{4,6},{5,7},{6,4},{7,5},{8,10},{9,11},{10,... | collective-permute-start | bytes 786440 | tf_op jit(solution)/shard_map/ppermute | solution.py:126
  145.2 6.1 %collective-permute-done.7 = bf16[2,128,512]{2,1,0:T(8,128)(2,1)S(1)} collective-permute-done((bf16[2,128,512]{2,1,0:T(8,128)(2,1)S(1)}, bf16[2,128,512]{2,1,0:T(8,128)(2,1)S(1)}, u32[]{:S(2)}, u32[]{:S(2)}) %collective-permute-start.7) | collective-permute-done | bytes 262176 | tf_op jit(solution)/shard_map/ppermute | solution.py:126
  151.3 2.9 collective-permute-done.17
  155.6 5.9 %convolution_convert_fusion.1 = bf16[4096,256]{1,0:T(8,128)(2,1)S(1)} fusion(bf16[1024,4096]{1,0:T(8,128)(2,1)} %all-gather.5.cloned.1.call-done, bf16[1024,512]{1,0:T(8,128)(2,1)S(1)} %bitcast.238), kind=kOutput, calls=%fused_computation.1 | convolution fusion | flops 2148532224 | bytes 11010048 | tf_op jit(solution)/shard_map/dot_general | solution.py:152
  164.6 8.5 %collective-permute-done.18 = bf16[2,512,256]{2,1,0:T(8,128)(2,1)S(1)} collective-permute-done((bf16[2,512,256]{2,1,0:T(8,128)(2,1)S(1)}, bf16[2,512,256]{2,1,0:T(8,128)(2,1)S(1)}, u32[]{:S(2)}, u32[]{:S(2)}) %collective-permute-start.18) | collective-permute-done | bytes 524320 | tf_op jit(solution)/shard_map/ppermute | solution.py:23
  176.6 2.5 convolution_convert_fusion
  179.7 4.0 %collective-permute-done.21 = bf16[512,256]{1,0:T(8,128)(2,1)S(1)} collective-permute-done((bf16[512,256]{1,0:T(8,128)(2,1)S(1)}, bf16[512,256]{1,0:T(8,128)(2,1)S(1)}, u32[]{:S(2)}, u32[]{:S(2)}) %collective-permute-start.21) | collective-permute-done | bytes 262176 | tf_op jit(solution)/shard_map/ppermute | solution.py:23
  185.4 1.7 collective-permute-start.24
  188.1 2.1 collective-permute-start.26
  190.2 8.8 %collective-permute-done.22 = bf16[2,512,256]{2,1,0:T(8,128)(2,1)S(1)} collective-permute-done((bf16[2,512,256]{2,1,0:T(8,128)(2,1)S(1)}, bf16[2,512,256]{2,1,0:T(8,128)(2,1)S(1)}, u32[]{:S(2)}, u32[]{:S(2)}) %collective-permute-start.22) | collective-permute-done | bytes 524320 | tf_op jit(solution)/shard_map/ppermute | solution.py:23
  199.3 2.8 collective-permute-start.23
  202.3 7.9 %collective-permute-done.26 = bf16[1024,256]{1,0:T(8,128)(2,1)S(1)} collective-permute-done((bf16[1024,256]{1,0:T(8,128)(2,1)S(1)}, bf16[1024,256]{1,0:T(8,128)(2,1)S(1)}, u32[]{:S(2)}, u32[]{:S(2)}) %collective-permute-start.26) | collective-permute-done | bytes 524320 | tf_op jit(solution)/shard_map/ppermute | solution.py:23
  210.3 2.8 collective-permute-start.28
  213.8 2.2 collective-permute-done.25
  216.0 1.9 maximum_negate_fusion
  221.3 3.1 convolution_convert_fusion.3
  224.4 2.1 copy.40
  226.5 6.0 %all-to-all-start = ((bf16[8,128,1,256]{1,3,2,0:T(8,128)(2,1)}), bf16[8,128,1,256]{1,3,2,0:T(8,128)(2,1)}, u32[]{:S(2)}, u32[]{:S(2)}) async-start(bf16[8,128,1,256]{1,3,2,0:T(8,128)(2,1)} %copy.40), calls=%async_computation | async-start | bytes 1048576 | tf_op jit(solution)/shard_map/all_to_all | solution.py:164
  234.6 2.8 fusion
  238.4 1.9 collective-permute-start.36
  243.5 3.8 %collective-permute-done.36 = bf16[512,256]{1,0:T(8,128)(2,1)S(1)} collective-permute-done((bf16[512,256]{1,0:T(8,128)(2,1)S(1)}, bf16[512,256]{1,0:T(8,128)(2,1)S(1)}, u32[]{:S(2)}, u32[]{:S(2)}) %collective-permute-start.36) | collective-permute-done | bytes 262176 | tf_op jit(solution)/shard_map/ppermute | solution.py:23
  247.2 2.5 collective-permute-done.37
  249.8 5.7 %convolution_convert_fusion.2 = bf16[1024,256]{1,0:T(8,128)(2,1)S(1)} fusion(bf16[1024,4096]{1,0:T(8,128)(2,1)} %all-gather.5.cloned.1.call-done, bf16[4096,256]{1,0:T(8,128)(2,1)S(1)} %bitcast.230), kind=kOutput, calls=%fused_computation.28 | convolution fusion | flops 2147745792 | bytes 11010048 | tf_op jit(solution)/shard_map/dot_general | solution.py:185
  256.5 4.7 %all-to-all-start.1 = ((bf16[8,128,1,256]{1,3,2,0:T(8,128)(2,1)}), bf16[8,128,1,256]{1,3,2,0:T(8,128)(2,1)S(1)}, u32[]{:S(2)}, u32[]{:S(2)}) async-start(bf16[8,128,1,256]{1,3,2,0:T(8,128)(2,1)} %copy.45), calls=%async_computation.1 | async-start | bytes 1048576 | tf_op jit(solution)/shard_map/all_to_all | solution.py:164
  261.9 6.0 %fusion.56 = (bf16[1024,8,1,256]{0,3,2,1:T(8,128)(2,1)}, bf16[1024,8,1,256]{0,3,2,1:T(8,128)(2,1)}) fusion(bf16[1024,8,2,256]{0,3,2,1:T(8,128)(2,1)} %bitcast.205), kind=kLoop, calls=%fused_computation.136 | loop fusion | bytes 16777216 | tf_op jit(solution)/shard_map/slice | solution.py:166
  267.9 2.0 copy.41
  271.0 4.8 %collective-permute-done.31 = bf16[128,2048]{0,1:T(8,128)(2,1)S(1)} collective-permute-done((bf16[128,2048]{0,1:T(8,128)(2,1)}, bf16[128,2048]{0,1:T(8,128)(2,1)S(1)}, u32[]{:S(2)}, u32[]{:S(2)}) %collective-permute-start.31) | collective-permute-done | bytes 524320 | tf_op jit(solution)/shard_map/ppermute | solution.py:23
  277.6 2.1 copy.42
  284.3 1.7 collective-permute-start.39
  287.1 4.8 %collective-permute-done.33 = bf16[64,2048]{0,1:T(8,128)(2,1)} collective-permute-done((bf16[64,2048]{0,1:T(8,128)(2,1)}, bf16[64,2048]{0,1:T(8,128)(2,1)}, u32[]{:S(2)}, u32[]{:S(2)}) %collective-permute-start.33) | collective-permute-done | bytes 262176 | tf_op jit(solution)/shard_map/ppermute | solution.py:23
  294.5 7.4 %collective-permute-done.38 = bf16[128,2048]{1,0:T(8,128)(2,1)S(1)} collective-permute-done((bf16[128,2048]{1,0:T(8,128)(2,1)}, bf16[128,2048]{1,0:T(8,128)(2,1)S(1)}, u32[]{:S(2)}, u32[]{:S(2)}) %collective-permute-start.38) | collective-permute-done | bytes 524320 | tf_op jit(solution)/shard_map/ppermute | solution.py:23
  305.9 3.3 %collective-permute-done.40 = bf16[64,2048]{1,0:T(8,128)(2,1)S(1)} collective-permute-done((bf16[64,2048]{1,0:T(8,128)(2,1)S(1)}, bf16[64,2048]{1,0:T(8,128)(2,1)S(1)}, u32[]{:S(2)}, u32[]{:S(2)}) %collective-permute-start.40) | collective-permute-done | bytes 262176 | tf_op jit(solution)/shard_map/ppermute | solution.py:23
  310.4 2.4 fusion.61
  312.8 3.4 %add_convert_fusion = bf16[1024,512]{1,0:T(8,128)(2,1)} fusion(f32[1024,512]{1,0:T(8,128)S(1)} %fusion.61, bf16[1024,2048]{0,1:T(8,128)(2,1)S(1)} %bitcast.225, bf16[512,2048]{1,0:T(8,128)(2,1)S(1)} %bitcast.227), kind=kOutput, calls=%fused_computation.21 | convolution fusion | flops 2148532224 | bytes 9437184 | tf_op jit(solution)/shard_map/dot_general | solution.py:165
  (168 shorter events, 57.3 us)
Async XLA Ops:
  7.2 148.4 %all-gather.5.cloned.1.call-start = ((), (), s32[]{:S(2)}) async-start(), calls=%async_computation.3 | async-start | bytes 9437184 | tf_op jit(solution)/shard_map/all_gather | solution.py:146
  7.2 26.8 %collective-permute-start.11 = (bf16[1024,512]{1,0:T(8,128)(2,1)}, bf16[1024,512]{1,0:T(8,128)(2,1)}, u32[]{:S(2)}, u32[]{:S(2)}) collective-permute-start(bf16[1024,512]{1,0:T(8,128)(2,1)} %param.5), channel_id=1, source_target_pairs={{0,4},{1,5},{4,6},{5,7},{2,0},{3,1},{6,2},{7,3},{8,12},{9,13},{12,... | collective-permute-start | bytes 3145736 | tf_op jit(solution)/shard_map/ppermute | solution.py:110
  12.5 10.3 %collective-permute-start.8 = (bf16[2,128,512]{2,1,0:T(8,128)(2,1)S(1)}, bf16[2,128,512]{2,1,0:T(8,128)(2,1)}, u32[]{:S(2)}, u32[]{:S(2)}) collective-permute-start(bf16[2,128,512]{2,1,0:T(8,128)(2,1)S(1)} %get-tuple-element.39), channel_id=1, source_target_pairs={{0,24},{8,16},{16,8},{24,0},{1,25},{9,17},{17,9},{25,1},{2,26},{10... | collective-permute-start | bytes 786440 | tf_op jit(solution)/shard_map/ppermute | solution.py:23
  15.0 11.9 %collective-permute-start.9 = (bf16[2,128,512]{2,1,0:T(8,128)(2,1)S(1)}, bf16[2,128,512]{2,1,0:T(8,128)(2,1)S(1)}, u32[]{:S(2)}, u32[]{:S(2)}) collective-permute-start(bf16[2,128,512]{2,1,0:T(8,128)(2,1)S(1)} %get-tuple-element.38), channel_id=1, source_target_pairs={{0,8},{8,0},{16,24},{24,16},{1,9},{9,1},{17,25},{25,17},{2,10},{10... | collective-permute-start | bytes 786440 | tf_op jit(solution)/shard_map/ppermute | solution.py:23
  15.5 11.4 %collective-permute-start.10 = (bf16[2,128,512]{2,1,0:T(8,128)(2,1)S(1)}, bf16[2,128,512]{2,1,0:T(8,128)(2,1)S(1)}, u32[]{:S(2)}, u32[]{:S(2)}) collective-permute-start(bf16[2,128,512]{2,1,0:T(8,128)(2,1)S(1)} %get-tuple-element.37), channel_id=1, source_target_pairs={{0,16},{8,24},{16,0},{24,8},{1,17},{9,25},{17,1},{25,9},{2,18},{10... | collective-permute-start | bytes 786440 | tf_op jit(solution)/shard_map/ppermute | solution.py:23
  16.0 20.0 %copy-start.10 = (bf16[1024,512]{1,0:T(8,128)(2,1)S(1)}, bf16[1024,512]{1,0:T(8,128)(2,1)}, u32[]{:S(2)}) copy-start(bf16[1024,512]{1,0:T(8,128)(2,1)} %param.6) | copy-start | bytes 3145732
  34.1 227.8 %all-gather.3.cloned.1.call-start = ((), (), s32[]{:S(2)}) async-start(), calls=%async_computation.2 | async-start | bytes 9437184 | tf_op jit(solution)/shard_map/all_gather | solution.py:147
  34.1 5.9 %collective-permute-start = (bf16[1024,512]{1,0:T(8,128)(2,1)}, bf16[1024,512]{1,0:T(8,128)(2,1)S(1)}, u32[]{:S(2)}, u32[]{:S(2)}) collective-permute-start(bf16[1024,512]{1,0:T(8,128)(2,1)} %param.5), channel_id=1, source_target_pairs={{0,0},{1,1},{4,2},{5,3},{2,4},{3,5},{6,6},{7,7},{8,8},{9,9},{12,10... | collective-permute-start | bytes 3145736 | tf_op jit(solution)/shard_map/ppermute | solution.py:110
  36.0 61.8 %collective-permute-start.2 = (bf16[1024,512]{1,0:T(8,128)(2,1)S(1)}, bf16[1024,512]{1,0:T(8,128)(2,1)S(1)}, u32[]{:S(2)}, u32[]{:S(2)}) collective-permute-start(bf16[1024,512]{1,0:T(8,128)(2,1)S(1)} %copy-done.10), channel_id=1, source_target_pairs={{0,2},{1,3},{2,0},{3,1},{4,6},{5,7},{6,4},{7,5},{8,10},{9,11},{10,... | collective-permute-start | bytes 3145736 | tf_op jit(solution)/shard_map/ppermute | solution.py:102
  40.0 57.8 %collective-permute-start.12 = (bf16[1024,512]{1,0:T(8,128)(2,1)}, bf16[1024,512]{1,0:T(8,128)(2,1)}, u32[]{:S(2)}, u32[]{:S(2)}) collective-permute-start(bf16[1024,512]{1,0:T(8,128)(2,1)} %collective-permute-done.11), channel_id=1, source_target_pairs={{0,1},{1,0},{2,3},{3,2},{4,5},{5,4},{6,7},{7,6},{8,9},{9,8},{10,11... | collective-permute-start | bytes 3145736 | tf_op jit(solution)/shard_map/ppermute | solution.py:117
  40.1 64.2 %collective-permute-start.1 = (bf16[1024,512]{1,0:T(8,128)(2,1)S(1)}, bf16[1024,512]{1,0:T(8,128)(2,1)}, u32[]{:S(2)}, u32[]{:S(2)}) collective-permute-start(bf16[1024,512]{1,0:T(8,128)(2,1)S(1)} %collective-permute-done), channel_id=1, source_target_pairs={{0,1},{1,0},{2,3},{3,2},{4,5},{5,4},{6,7},{7,6},{8,9},{9,8},{10,11... | collective-permute-start | bytes 3145736 | tf_op jit(solution)/shard_map/ppermute | solution.py:117
  102.6 9.2 %collective-permute-start.15 = (bf16[2,1,128,1024]{3,2,0,1:T(8,128)(2,1)S(1)}, bf16[2,1,128,1024]{3,2,0,1:T(8,128)(2,1)S(1)}, u32[]{:S(2)}, u32[]{:S(2)}) collective-permute-start(bf16[2,1,128,1024]{3,2,0,1:T(8,128)(2,1)S(1)} %dynamic-slice_bitcast_fusion.4), channel_id=1, source_target_pairs={{0,16},{8,24},{16,0},{24,8},{1,17},{9,25},{17,1},{25,9},{2,18},{10... | collective-permute-start | bytes 1572872 | tf_op jit(solution)/shard_map/ppermute | solution.py:23
  108.5 11.8 %collective-permute-start.5 = (bf16[2,1,128,1024]{3,2,0,1:T(8,128)(2,1)S(1)}, bf16[2,1,128,1024]{3,2,0,1:T(8,128)(2,1)S(1)}, u32[]{:S(2)}, u32[]{:S(2)}) collective-permute-start(bf16[2,1,128,1024]{3,2,0,1:T(8,128)(2,1)S(1)} %dynamic-slice_bitcast_fusion.6), channel_id=1, source_target_pairs={{0,16},{8,24},{16,0},{24,8},{1,17},{9,25},{17,1},{25,9},{2,18},{10... | collective-permute-start | bytes 1572872 | tf_op jit(solution)/shard_map/ppermute | solution.py:23
  109.0 21.7 %collective-permute-start.13 = (bf16[2,1,128,1024]{3,2,1,0:T(8,128)(2,1)S(1)}, bf16[2,1,128,1024]{3,2,1,0:T(8,128)(2,1)S(1)}, u32[]{:S(2)}, u32[]{:S(2)}) collective-permute-start(bf16[2,1,128,1024]{3,2,1,0:T(8,128)(2,1)S(1)} %dynamic-slice_bitcast_fusion.5), channel_id=1, source_target_pairs={{0,8},{8,0},{16,24},{24,16},{1,9},{9,1},{17,25},{25,17},{2,10},{10... | collective-permute-start | bytes 1572872 | tf_op jit(solution)/shard_map/ppermute | solution.py:23
  110.7 18.2 %collective-permute-start.3 = (bf16[2,1,128,1024]{3,2,1,0:T(8,128)(2,1)S(1)}, bf16[2,1,128,1024]{3,2,1,0:T(8,128)(2,1)S(1)}, u32[]{:S(2)}, u32[]{:S(2)}) collective-permute-start(bf16[2,1,128,1024]{3,2,1,0:T(8,128)(2,1)S(1)} %dynamic-slice_bitcast_fusion.7), channel_id=1, source_target_pairs={{0,8},{8,0},{16,24},{24,16},{1,9},{9,1},{17,25},{25,17},{2,10},{10... | collective-permute-start | bytes 1572872 | tf_op jit(solution)/shard_map/ppermute | solution.py:23
  112.1 31.9 %collective-permute-start.16 = (bf16[1,128,1024]{2,1,0:T(8,128)(2,1)S(1)}, bf16[1,128,1024]{2,1,0:T(8,128)(2,1)S(1)}, u32[]{:S(2)}, u32[]{:S(2)}) collective-permute-start(bf16[1,128,1024]{2,1,0:T(8,128)(2,1)S(1)} %dynamic-slice_bitcast_fusion.12), channel_id=1, source_target_pairs={{0,8},{8,0},{16,24},{24,16},{1,9},{9,1},{17,25},{25,17},{2,10},{10... | collective-permute-start | bytes 786440 | tf_op jit(solution)/shard_map/ppermute | solution.py:23
  120.5 13.9 %collective-permute-start.6 = (bf16[1,128,1024]{2,1,0:T(8,128)(2,1)S(1)}, bf16[1,128,1024]{2,1,0:T(8,128)(2,1)S(1)}, u32[]{:S(2)}, u32[]{:S(2)}) collective-permute-start(bf16[1,128,1024]{2,1,0:T(8,128)(2,1)S(1)} %dynamic-slice_bitcast_fusion.17), channel_id=1, source_target_pairs={{0,8},{8,0},{16,24},{24,16},{1,9},{9,1},{17,25},{25,17},{2,10},{10... | collective-permute-start | bytes 786440 | tf_op jit(solution)/shard_map/ppermute | solution.py:23
  129.1 6.4 %collective-permute-start.4 = (bf16[1,128,1024]{2,1,0:T(8,128)(2,1)S(1)}, bf16[1,128,1024]{2,1,0:T(8,128)(2,1)S(1)}, u32[]{:S(2)}, u32[]{:S(2)}) collective-permute-start(bf16[1,128,1024]{2,1,0:T(8,128)(2,1)S(1)} %dynamic-slice_bitcast_fusion.18), channel_id=1, source_target_pairs={{0,16},{8,24},{16,0},{24,8},{1,17},{9,25},{17,1},{25,9},{2,18},{10... | collective-permute-start | bytes 786440 | tf_op jit(solution)/shard_map/ppermute | solution.py:23
  131.0 13.1 %collective-permute-start.14 = (bf16[1,128,1024]{2,1,0:T(8,128)(2,1)S(1)}, bf16[1,128,1024]{2,1,0:T(8,128)(2,1)S(1)}, u32[]{:S(2)}, u32[]{:S(2)}) collective-permute-start(bf16[1,128,1024]{2,1,0:T(8,128)(2,1)S(1)} %dynamic-slice_bitcast_fusion.13), channel_id=1, source_target_pairs={{0,16},{8,24},{16,0},{24,8},{1,17},{9,25},{17,1},{25,9},{2,18},{10... | collective-permute-start | bytes 786440 | tf_op jit(solution)/shard_map/ppermute | solution.py:23
  135.6 15.6 %collective-permute-start.7 = (bf16[2,128,512]{2,1,0:T(8,128)(2,1)S(1)}, bf16[2,128,512]{2,1,0:T(8,128)(2,1)S(1)}, u32[]{:S(2)}, u32[]{:S(2)}) collective-permute-start(bf16[2,128,512]{2,1,0:T(8,128)(2,1)S(1)} %fusion.52), channel_id=1, source_target_pairs={{0,2},{1,3},{2,0},{3,1},{4,6},{5,7},{6,4},{7,5},{8,10},{9,11},{10,... | collective-permute-start | bytes 786440 | tf_op jit(solution)/shard_map/ppermute | solution.py:126
  144.2 10.0 %collective-permute-start.17 = (bf16[2,128,512]{2,1,0:T(8,128)(2,1)S(1)}, bf16[2,128,512]{2,1,0:T(8,128)(2,1)S(1)}, u32[]{:S(2)}, u32[]{:S(2)}) collective-permute-start(bf16[2,128,512]{2,1,0:T(8,128)(2,1)S(1)} %pad_maximum_fusion.3), channel_id=1, source_target_pairs={{0,2},{1,3},{2,0},{3,1},{4,6},{5,7},{6,4},{7,5},{8,10},{9,11},{10,... | collective-permute-start | bytes 786440 | tf_op jit(solution)/shard_map/ppermute | solution.py:126
  161.7 11.4 %collective-permute-start.18 = (bf16[2,512,256]{2,1,0:T(8,128)(2,1)S(1)}, bf16[2,512,256]{2,1,0:T(8,128)(2,1)S(1)}, u32[]{:S(2)}, u32[]{:S(2)}) collective-permute-start(bf16[2,512,256]{2,1,0:T(8,128)(2,1)S(1)} %dynamic-slice_bitcast_fusion.3), channel_id=1, source_target_pairs={{0,8},{8,0},{16,24},{24,16},{1,9},{9,1},{17,25},{25,17},{2,10},{10... | collective-permute-start | bytes 1572872 | tf_op jit(solution)/shard_map/ppermute | solution.py:23
  163.0 12.3 %collective-permute-start.20 = (bf16[2,512,256]{2,1,0:T(8,128)(2,1)S(1)}, bf16[2,512,256]{2,1,0:T(8,128)(2,1)S(1)}, u32[]{:S(2)}, u32[]{:S(2)}) collective-permute-start(bf16[2,512,256]{2,1,0:T(8,128)(2,1)S(1)} %dynamic-slice_bitcast_fusion.2), channel_id=1, source_target_pairs={{0,16},{8,24},{16,0},{24,8},{1,17},{9,25},{17,1},{25,9},{2,18},{10... | collective-permute-start | bytes 1572872 | tf_op jit(solution)/shard_map/ppermute | solution.py:23
  173.2 6.4 %collective-permute-start.19 = (bf16[512,256]{1,0:T(8,128)(2,1)S(1)}, bf16[512,256]{1,0:T(8,128)(2,1)S(1)}, u32[]{:S(2)}, u32[]{:S(2)}) collective-permute-start(bf16[512,256]{1,0:T(8,128)(2,1)S(1)} %dynamic-slice_bitcast_fusion.11), channel_id=1, source_target_pairs={{0,16},{8,24},{16,0},{24,8},{1,17},{9,25},{17,1},{25,9},{2,18},{10... | collective-permute-start | bytes 786440 | tf_op jit(solution)/shard_map/ppermute | solution.py:23
  175.5 8.3 %collective-permute-start.21 = (bf16[512,256]{1,0:T(8,128)(2,1)S(1)}, bf16[512,256]{1,0:T(8,128)(2,1)S(1)}, u32[]{:S(2)}, u32[]{:S(2)}) collective-permute-start(bf16[512,256]{1,0:T(8,128)(2,1)S(1)} %dynamic-slice_bitcast_fusion.10), channel_id=1, source_target_pairs={{0,8},{8,0},{16,24},{24,16},{1,9},{9,1},{17,25},{25,17},{2,10},{10... | collective-permute-start | bytes 786440 | tf_op jit(solution)/shard_map/ppermute | solution.py:23
  184.1 14.9 %collective-permute-start.22 = (bf16[2,512,256]{2,1,0:T(8,128)(2,1)S(1)}, bf16[2,512,256]{2,1,0:T(8,128)(2,1)S(1)}, u32[]{:S(2)}, u32[]{:S(2)}) collective-permute-start(bf16[2,512,256]{2,1,0:T(8,128)(2,1)S(1)} %dynamic-slice_bitcast_fusion.1), channel_id=1, source_target_pairs={{0,8},{8,0},{16,24},{24,16},{1,9},{9,1},{17,25},{25,17},{2,10},{10... | collective-permute-start | bytes 1572872 | tf_op jit(solution)/shard_map/ppermute | solution.py:23
  185.4 16.7 %collective-permute-start.24 = (bf16[2,512,256]{2,1,0:T(8,128)(2,1)S(1)}, bf16[2,512,256]{2,1,0:T(8,128)(2,1)S(1)}, u32[]{:S(2)}, u32[]{:S(2)}) collective-permute-start(bf16[2,512,256]{2,1,0:T(8,128)(2,1)S(1)} %dynamic-slice_bitcast_fusion), channel_id=1, source_target_pairs={{0,16},{8,24},{16,0},{24,8},{1,17},{9,25},{17,1},{25,9},{2,18},{10... | collective-permute-start | bytes 1572872 | tf_op jit(solution)/shard_map/ppermute | solution.py:23
  188.1 22.2 %collective-permute-start.26 = (bf16[1024,256]{1,0:T(8,128)(2,1)S(1)}, bf16[1024,256]{1,0:T(8,128)(2,1)S(1)}, u32[]{:S(2)}, u32[]{:S(2)}) collective-permute-start(bf16[1024,256]{1,0:T(8,128)(2,1)S(1)} %get-tuple-element.22), channel_id=1, source_target_pairs={{0,8},{8,0},{16,24},{24,16},{1,9},{9,1},{17,25},{25,17},{2,10},{10... | collective-permute-start | bytes 1572872 | tf_op jit(solution)/shard_map/ppermute | solution.py:23
  190.2 22.9 %collective-permute-start.27 = (bf16[1024,256]{1,0:T(8,128)(2,1)S(1)}, bf16[1024,256]{1,0:T(8,128)(2,1)S(1)}, u32[]{:S(2)}, u32[]{:S(2)}) collective-permute-start(bf16[1024,256]{1,0:T(8,128)(2,1)S(1)} %get-tuple-element.22), channel_id=1, source_target_pairs={{0,16},{8,24},{16,0},{24,8},{1,17},{9,25},{17,1},{25,9},{2,18},{10... | collective-permute-start | bytes 1572872 | tf_op jit(solution)/shard_map/ppermute | solution.py:23
  199.3 14.4 %collective-permute-start.23 = (bf16[512,256]{1,0:T(8,128)(2,1)S(1)}, bf16[512,256]{1,0:T(8,128)(2,1)S(1)}, u32[]{:S(2)}, u32[]{:S(2)}) collective-permute-start(bf16[512,256]{1,0:T(8,128)(2,1)S(1)} %dynamic-slice_bitcast_fusion.9), channel_id=1, source_target_pairs={{0,16},{8,24},{16,0},{24,8},{1,17},{9,25},{17,1},{25,9},{2,18},{10... | collective-permute-start | bytes 786440 | tf_op jit(solution)/shard_map/ppermute | solution.py:23
  202.3 13.6 %collective-permute-start.25 = (bf16[512,256]{1,0:T(8,128)(2,1)S(1)}, bf16[512,256]{1,0:T(8,128)(2,1)S(1)}, u32[]{:S(2)}, u32[]{:S(2)}) collective-permute-start(bf16[512,256]{1,0:T(8,128)(2,1)S(1)} %dynamic-slice_bitcast_fusion.8), channel_id=1, source_target_pairs={{0,8},{8,0},{16,24},{24,16},{1,9},{9,1},{17,25},{25,17},{2,10},{10... | collective-permute-start | bytes 786440 | tf_op jit(solution)/shard_map/ppermute | solution.py:23
  210.3 10.3 %collective-permute-start.28 = (bf16[512,256]{1,0:T(8,128)(2,1)S(1)}, bf16[512,256]{1,0:T(8,128)(2,1)S(1)}, u32[]{:S(2)}, u32[]{:S(2)}) collective-permute-start(bf16[512,256]{1,0:T(8,128)(2,1)S(1)} %slice.125), channel_id=1, source_target_pairs={{0,16},{8,24},{16,0},{24,8},{1,17},{9,25},{17,1},{25,9},{2,18},{10... | collective-permute-start | bytes 786440 | tf_op jit(solution)/shard_map/ppermute | solution.py:23
  213.2 8.1 %collective-permute-start.29 = (bf16[512,256]{1,0:T(8,128)(2,1)S(1)}, bf16[512,256]{1,0:T(8,128)(2,1)S(1)}, u32[]{:S(2)}, u32[]{:S(2)}) collective-permute-start(bf16[512,256]{1,0:T(8,128)(2,1)S(1)} %slice.126), channel_id=1, source_target_pairs={{0,8},{8,0},{16,24},{24,16},{1,9},{9,1},{17,25},{25,17},{2,10},{10... | collective-permute-start | bytes 786440 | tf_op jit(solution)/shard_map/ppermute | solution.py:23
  217.9 19.5 %collective-permute-start.34 = (bf16[1024,256]{1,0:T(8,128)(2,1)}, bf16[1024,256]{1,0:T(8,128)(2,1)}, u32[]{:S(2)}, u32[]{:S(2)}) collective-permute-start(bf16[1024,256]{1,0:T(8,128)(2,1)} %get-tuple-element.20), channel_id=1, source_target_pairs={{0,8},{8,0},{16,24},{24,16},{1,9},{9,1},{17,25},{25,17},{2,10},{10... | collective-permute-start | bytes 1572872 | tf_op jit(solution)/shard_map/ppermute | solution.py:23
  219.0 21.2 %collective-permute-start.35 = (bf16[1024,256]{1,0:T(8,128)(2,1)}, bf16[1024,256]{1,0:T(8,128)(2,1)}, u32[]{:S(2)}, u32[]{:S(2)}) collective-permute-start(bf16[1024,256]{1,0:T(8,128)(2,1)} %get-tuple-element.20), channel_id=1, source_target_pairs={{0,16},{8,24},{16,0},{24,8},{1,17},{9,25},{17,1},{25,9},{2,18},{10... | collective-permute-start | bytes 1572872 | tf_op jit(solution)/shard_map/ppermute | solution.py:23
  226.5 30.0 %all-to-all-start = ((bf16[8,128,1,256]{1,3,2,0:T(8,128)(2,1)}), bf16[8,128,1,256]{1,3,2,0:T(8,128)(2,1)}, u32[]{:S(2)}, u32[]{:S(2)}) async-start(bf16[8,128,1,256]{1,3,2,0:T(8,128)(2,1)} %copy.40), calls=%async_computation | async-start | bytes 1048576 | tf_op jit(solution)/shard_map/all_to_all | solution.py:164
  238.4 8.8 %collective-permute-start.36 = (bf16[512,256]{1,0:T(8,128)(2,1)S(1)}, bf16[512,256]{1,0:T(8,128)(2,1)S(1)}, u32[]{:S(2)}, u32[]{:S(2)}) collective-permute-start(bf16[512,256]{1,0:T(8,128)(2,1)S(1)} %slice.130), channel_id=1, source_target_pairs={{0,16},{8,24},{16,0},{24,8},{1,17},{9,25},{17,1},{25,9},{2,18},{10... | collective-permute-start | bytes 786440 | tf_op jit(solution)/shard_map/ppermute | solution.py:23
  241.2 8.5 %collective-permute-start.37 = (bf16[512,256]{1,0:T(8,128)(2,1)S(1)}, bf16[512,256]{1,0:T(8,128)(2,1)S(1)}, u32[]{:S(2)}, u32[]{:S(2)}) collective-permute-start(bf16[512,256]{1,0:T(8,128)(2,1)S(1)} %slice.131), channel_id=1, source_target_pairs={{0,8},{8,0},{16,24},{24,16},{1,9},{9,1},{17,25},{25,17},{2,10},{10... | collective-permute-start | bytes 786440 | tf_op jit(solution)/shard_map/ppermute | solution.py:23
  256.5 25.3 %all-to-all-start.1 = ((bf16[8,128,1,256]{1,3,2,0:T(8,128)(2,1)}), bf16[8,128,1,256]{1,3,2,0:T(8,128)(2,1)S(1)}, u32[]{:S(2)}, u32[]{:S(2)}) async-start(bf16[8,128,1,256]{1,3,2,0:T(8,128)(2,1)} %copy.45), calls=%async_computation.1 | async-start | bytes 1048576 | tf_op jit(solution)/shard_map/all_to_all | solution.py:164
  261.2 14.5 %collective-permute-start.31 = (bf16[128,2048]{0,1:T(8,128)(2,1)}, bf16[128,2048]{0,1:T(8,128)(2,1)S(1)}, u32[]{:S(2)}, u32[]{:S(2)}) collective-permute-start(bf16[128,2048]{0,1:T(8,128)(2,1)} %bitcast.79), channel_id=1, source_target_pairs={{0,16},{8,24},{16,0},{24,8},{1,17},{9,25},{17,1},{25,9},{2,18},{10... | collective-permute-start | bytes 1572872 | tf_op jit(solution)/shard_map/ppermute | solution.py:23
  261.5 15.5 %collective-permute-start.30 = (bf16[128,2048]{0,1:T(8,128)(2,1)}, bf16[128,2048]{0,1:T(8,128)(2,1)}, u32[]{:S(2)}, u32[]{:S(2)}) collective-permute-start(bf16[128,2048]{0,1:T(8,128)(2,1)} %bitcast.79), channel_id=1, source_target_pairs={{0,8},{8,0},{16,24},{24,16},{1,9},{9,1},{17,25},{25,17},{2,10},{10... | collective-permute-start | bytes 1572872 | tf_op jit(solution)/shard_map/ppermute | solution.py:23
  276.7 15.1 %collective-permute-start.33 = (bf16[64,2048]{0,1:T(8,128)(2,1)}, bf16[64,2048]{0,1:T(8,128)(2,1)}, u32[]{:S(2)}, u32[]{:S(2)}) collective-permute-start(bf16[64,2048]{0,1:T(8,128)(2,1)} %slice.128), channel_id=1, source_target_pairs={{0,8},{8,0},{16,24},{24,16},{1,9},{9,1},{17,25},{25,17},{2,10},{10... | collective-permute-start | bytes 786440 | tf_op jit(solution)/shard_map/ppermute | solution.py:23
  277.0 15.2 %collective-permute-start.32 = (bf16[64,2048]{0,1:T(8,128)(2,1)}, bf16[64,2048]{0,1:T(8,128)(2,1)}, u32[]{:S(2)}, u32[]{:S(2)}) collective-permute-start(bf16[64,2048]{0,1:T(8,128)(2,1)} %bitcast.204), channel_id=1, source_target_pairs={{0,16},{8,24},{16,0},{24,8},{1,17},{9,25},{17,1},{25,9},{2,18},{10... | collective-permute-start | bytes 786440 | tf_op jit(solution)/shard_map/ppermute | solution.py:23
  282.8 19.0 %collective-permute-start.38 = (bf16[128,2048]{1,0:T(8,128)(2,1)}, bf16[128,2048]{1,0:T(8,128)(2,1)S(1)}, u32[]{:S(2)}, u32[]{:S(2)}) collective-permute-start(bf16[128,2048]{1,0:T(8,128)(2,1)} %copy.47), channel_id=1, source_target_pairs={{0,8},{8,0},{16,24},{24,16},{1,9},{9,1},{17,25},{25,17},{2,10},{10... | collective-permute-start | bytes 1572872 | tf_op jit(solution)/shard_map/ppermute | solution.py:23
  284.3 18.0 %collective-permute-start.39 = (bf16[128,2048]{1,0:T(8,128)(2,1)}, bf16[128,2048]{1,0:T(8,128)(2,1)}, u32[]{:S(2)}, u32[]{:S(2)}) collective-permute-start(bf16[128,2048]{1,0:T(8,128)(2,1)} %copy.47), channel_id=1, source_target_pairs={{0,16},{8,24},{16,0},{24,8},{1,17},{9,25},{17,1},{25,9},{2,18},{10... | collective-permute-start | bytes 1572872 | tf_op jit(solution)/shard_map/ppermute | solution.py:23
  294.4 15.9 %copy-start.8 = (bf16[4,128,2048]{2,1,0:T(8,128)(2,1)S(1)}, bf16[4,128,2048]{2,1,0:T(8,128)(2,1)}, u32[]{:S(2)}) copy-start(bf16[4,128,2048]{2,1,0:T(8,128)(2,1)} %copy-done.7) | copy-start | bytes 6291460
  301.9 7.3 %collective-permute-start.40 = (bf16[64,2048]{1,0:T(8,128)(2,1)S(1)}, bf16[64,2048]{1,0:T(8,128)(2,1)S(1)}, u32[]{:S(2)}, u32[]{:S(2)}) collective-permute-start(bf16[64,2048]{1,0:T(8,128)(2,1)S(1)} %slice.132), channel_id=1, source_target_pairs={{0,16},{8,24},{16,0},{24,8},{1,17},{9,25},{17,1},{25,9},{2,18},{10... | collective-permute-start | bytes 786440 | tf_op jit(solution)/shard_map/ppermute | solution.py:23
  303.2 7.1 %collective-permute-start.41 = (bf16[64,2048]{1,0:T(8,128)(2,1)S(1)}, bf16[64,2048]{1,0:T(8,128)(2,1)S(1)}, u32[]{:S(2)}, u32[]{:S(2)}) collective-permute-start(bf16[64,2048]{1,0:T(8,128)(2,1)S(1)} %slice.133), channel_id=1, source_target_pairs={{0,8},{8,0},{16,24},{24,16},{1,9},{9,1},{17,25},{25,17},{2,10},{10... | collective-permute-start | bytes 786440 | tf_op jit(solution)/shard_map/ppermute | solution.py:23
  (10 other events, 47.7 us)
Sparse Core Ops, SparseCore 0:
  34.2 97.1 all-gather.4
  155.7 86.9 all-gather.2

commit v6 on v5

--- a/solution.py
+++ b/solution.py
@@ -160,14 +160,18 @@
         values = [-value for value in values]
         rotated = jnp.concatenate(values, 1)
 
-        def finish(term, c):
+        def finish(term, c, before=None):
             term = lax.all_to_all(term.reshape(cols, sub, mid), "cols", 0, 1)
-            return lax.dot_general(
+            whole = gather(term.reshape(sub, cols * mid), rows, before)
+            if before is not None:
+                whole, before = whole
+            product = lax.dot_general(
                 left_rows[:, :, c].reshape(depth, cols * mid),
-                gather(term.reshape(sub, cols * mid), rows).reshape(width, cols * mid),
+                whole.reshape(width, cols * mid),
                 (((1,), (1,)), ((), ())),
                 preferred_element_type=f32,
             )
+            return product if before is None else before + product
 
         step_dir = None
         last = None
@@ -184,7 +188,7 @@
                 step_dir = finish(last, 0)
             term = jnp.dot(right_rows, normals, preferred_element_type=f32).astype(bf16)
             last = rows_first(term)
-        step_dir = (step_dir + finish(last, 1))
+        step_dir = finish(last, 1, step_dir)
         step_dir = step_dir.astype(bf16)
 
         new_first = beta_first * first_moment + (1.0 - beta_first) * rotated

time: 324 us -> 330 us (1.019)
  matrix products: 31.5 us -> 37.5 us
  waiting for transfers between devices: 162 us -> 157 us
  local copies, waits for them, and re-layouts: 34.6 us -> 39.1 us
    dot_general x2, matrix products: 5.75 us -> 12.1 us  [finish(): lax.dot_general(left_rows[:, :, c].reshape(depth, cols * mid), whole.resh...]
    ppermute x35, starting transfers between devices: 40.2 us -> 34 us  [swap(): return lax.ppermute(block, 'rows', [(i, i ^ mask) for i in range(count)])]
    ppermute x2, starting transfers between devices: 9.22 us -> 15.3 us  [rotate_left(): lax.ppermute(sums[..., :width], 'cols', [(i, i ^ 2) for i in range(cols)])]
    ppermute x2, waiting for transfers between devices: 9 us -> 5.29 us  [rotate_left(): lax.ppermute(sums[..., :width], 'cols', [(i, i ^ 2) for i in range(cols)])]
    broadcast_in_dim x5 -> x8, local copies, waits for them, and re-layouts: 5.58 us -> 9.02 us  [gather(): whole = lax.dynamic_update_index_in_dim(whole, term, me ^ mask, 0)]
    dynamic_update_slice x11 -> x13, local copies, waits for them, and re-layouts: 6.87 us -> 6.95 us  [gather(): whole = lax.dynamic_update_index_in_dim(whole, term, me ^ mask, 0)]
  transfers between devices with their start and end apart: 46 -> 46, of which waited for: 28 -> 25; matrix products, arithmetic and copies ran while one was open for 21% -> 23% of each run, Pallas kernels for 0% -> 0%
where the time goes in v6:
time: 330 us; the launch traced here: 328 us
  waiting for transfers between devices  157 us (48%)
  starting transfers between devices  69.8 us (21%)
  local copies, waits for them, and re-layouts  39.1 us (12%)
  matrix products  37.5 us (11%)
  between operations  14.7 us (4%)
  other arithmetic  10.8 us (3%)
    ppermute x35, waiting for transfers between devices, swap(): return lax.ppermute(block, 'rows', [(i, i ^ mask) for i in range(count)])  86.9 us
    ppermute x1, waiting for transfers between devices, rotate_left(): lax.ppermute(left, 'cols', [(i, i ^ 2) for i in range(cols)])  57.2 us
    ppermute x35, starting transfers between devices, swap(): return lax.ppermute(block, 'rows', [(i, i ^ mask) for i in range(count)])  34 us
    ppermute x2, starting transfers between devices, rotate_left(): lax.ppermute(sums[..., :width], 'cols', [(i, i ^ 2) for i in range(cols)])  15.3 us
    dot_general x2, matrix products, finish(): lax.dot_general(left_rows[:, :, c].reshape(depth, cols * mid), whole.resh...  12.1 us
    all_to_all x2, starting transfers between devices, finish(): term = lax.all_to_all(term.reshape(cols, sub, mid), 'cols', 0, 1)  9.83 us
    broadcast_in_dim x8, local copies, waits for them, and re-layouts, gather(): whole = lax.dynamic_update_index_in_dim(whole, term, me ^ mask, 0)  9.02 us
    dot_general x2, matrix products, local(): term = jnp.dot(right_rows, normals, preferred_element_type=f32).astype(bf16)  8.87 us
  transfers between devices with their start and end apart: 46, of which 25 were waited for; matrix products, arithmetic and copies ran while one was open for 23% of the time, Pallas kernels for 0%

profile of v6, /device:TPU:0, one launch (start us, length us, event | category | flops | bytes accessed | tf_op | source)
XLA Modules:
  0.0 328.4 jit_solution(14315414818877164677)
XLA Ops:
  7.2 4.1 %collective-permute-start.3 = (bf16[1024,512]{1,0:T(8,128)(2,1)}, bf16[1024,512]{1,0:T(8,128)(2,1)}, u32[]{:S(2)}, u32[]{:S(2)}) collective-permute-start(bf16[1024,512]{1,0:T(8,128)(2,1)} %param.5), channel_id=1, source_target_pairs={{0,4},{1,5},{4,6},{5,7},{2,0},{3,1},{6,2},{7,3},{8,12},{9,13},{12,... | collective-permute-start | bytes 3145736 | tf_op jit(solution)/shard_map/ppermute | solution.py:110
  12.5 2.5 collective-permute-start
  17.2 5.6 %collective-permute-done = bf16[2,128,512]{2,1,0:T(8,128)(2,1)} collective-permute-done((bf16[2,128,512]{2,1,0:T(8,128)(2,1)S(1)}, bf16[2,128,512]{2,1,0:T(8,128)(2,1)}, u32[]{:S(2)}, u32[]{:S(2)}) %collective-permute-start) | collective-permute-done | bytes 262176 | tf_op jit(solution)/shard_map/ppermute | solution.py:23
  23.8 3.1 collective-permute-done.1
  27.0 7.0 %collective-permute-done.3 = bf16[1024,512]{1,0:T(8,128)(2,1)} collective-permute-done((bf16[1024,512]{1,0:T(8,128)(2,1)}, bf16[1024,512]{1,0:T(8,128)(2,1)}, u32[]{:S(2)}, u32[]{:S(2)}) %collective-permute-start.3) | collective-permute-done | bytes 1048608 | tf_op jit(solution)/shard_map/ppermute | solution.py:110
  34.1 1.9 collective-permute-start.4
  36.0 4.0 %collective-permute-start.6 = (bf16[1024,512]{1,0:T(8,128)(2,1)S(1)}, bf16[1024,512]{1,0:T(8,128)(2,1)S(1)}, u32[]{:S(2)}, u32[]{:S(2)}) collective-permute-start(bf16[1024,512]{1,0:T(8,128)(2,1)S(1)} %copy-done.6), channel_id=1, source_target_pairs={{0,2},{1,3},{2,0},{3,1},{4,6},{5,7},{6,4},{7,5},{8,10},{9,11},{10,... | collective-permute-start | bytes 3145736 | tf_op jit(solution)/shard_map/ppermute | solution.py:102
  40.6 57.2 %collective-permute-done.6 = bf16[1024,512]{1,0:T(8,128)(2,1)S(1)} collective-permute-done((bf16[1024,512]{1,0:T(8,128)(2,1)S(1)}, bf16[1024,512]{1,0:T(8,128)(2,1)S(1)}, u32[]{:S(2)}, u32[]{:S(2)}) %collective-permute-start.6) | collective-permute-done | bytes 1048608 | tf_op jit(solution)/shard_map/ppermute | solution.py:102
  97.8 4.0 %fusion.16 = bf16[2,512,1024]{2,1,0:T(8,128)(2,1)S(1)} fusion(bf16[1,1024,512]{2,1,0:T(8,128)(2,1)} %bitcast.10, bf16[1,1024,512]{2,1,0:T(8,128)(2,1)S(1)} %bitcast.239, pred[]{:T(512)S(6)} %eq.4, bf16[1024,512]{1,0:T(8,128)(2,1)S(1)} %copy-done.6, bf16[1024,512]{1,0:T(8,128)(2,1)S(1)} %collective-permute-done.6), kind=kOutput, calls=%fused_computation.25 | convolution fusion | flops 2155872256 | bytes 6291457 | tf_op jit(solution)/shard_map/dot_general | solution.py:90
  102.1 1.6 collective-permute-start.7
  103.7 1.6 collective-permute-start.9
  105.3 4.1 %fusion.15 = bf16[2,512,1024]{2,1,0:T(8,128)(2,1)S(1)} fusion(bf16[1,1024,512]{2,1,0:T(8,128)(2,1)S(1)} %bitcast.240, bf16[1,1024,512]{2,1,0:T(8,128)(2,1)} %bitcast.27, pred[]{:T(512)S(6)} %eq.4, bf16[1024,512]{1,0:T(8,128)(2,1)S(1)} %copy-done.6, bf16[1024,512]{1,0:T(8,128)(2,1)S(1)} %collective-permute-done.6), kind=kOutput, calls=%fused_computation.24 | convolution fusion | flops 2155872256 | bytes 6291457 | tf_op jit(solution)/shard_map/dot_general | solution.py:90
  110.8 6.2 %collective-permute-done.7 = bf16[2,1,128,1024]{3,2,1,0:T(8,128)(2,1)S(1)} collective-permute-done((bf16[2,1,128,1024]{3,2,1,0:T(8,128)(2,1)S(1)}, bf16[2,1,128,1024]{3,2,1,0:T(8,128)(2,1)S(1)}, u32[]{:S(2)}, u32[]{:S(2)}) %collective-permute-start.7) | collective-permute-done | bytes 524320 | tf_op jit(solution)/shard_map/ppermute | solution.py:23
  118.8 1.6 collective-permute-start.10
  120.5 3.3 %collective-permute-done.13 = bf16[2,1,128,1024]{3,2,1,0:T(8,128)(2,1)S(1)} collective-permute-done((bf16[2,1,128,1024]{3,2,1,0:T(8,128)(2,1)S(1)}, bf16[2,1,128,1024]{3,2,1,0:T(8,128)(2,1)S(1)}, u32[]{:S(2)}, u32[]{:S(2)}) %collective-permute-start.13) | collective-permute-done | bytes 524320 | tf_op jit(solution)/shard_map/ppermute | solution.py:23
  127.1 11.0 %collective-permute-start.11 = (bf16[2,128,512]{2,1,0:T(8,128)(2,1)S(1)}, bf16[2,128,512]{2,1,0:T(8,128)(2,1)S(1)}, u32[]{:S(2)}, u32[]{:S(2)}) collective-permute-start(bf16[2,128,512]{2,1,0:T(8,128)(2,1)S(1)} %fusion.51), channel_id=1, source_target_pairs={{0,2},{1,3},{2,0},{3,1},{4,6},{5,7},{6,4},{7,5},{8,10},{9,11},{10,... | collective-permute-start | bytes 786440 | tf_op jit(solution)/shard_map/ppermute | solution.py:126
  138.3 4.3 %collective-permute-start.17 = (bf16[2,128,512]{2,1,0:T(8,128)(2,1)S(1)}, bf16[2,128,512]{2,1,0:T(8,128)(2,1)S(1)}, u32[]{:S(2)}, u32[]{:S(2)}) collective-permute-start(bf16[2,128,512]{2,1,0:T(8,128)(2,1)S(1)} %pad_maximum_fusion.3), channel_id=1, source_target_pairs={{0,2},{1,3},{2,0},{3,1},{4,6},{5,7},{6,4},{7,5},{8,10},{9,11},{10,... | collective-permute-start | bytes 786440 | tf_op jit(solution)/shard_map/ppermute | solution.py:126
  142.8 5.3 %collective-permute-done.17 = bf16[2,128,512]{2,1,0:T(8,128)(2,1)S(1)} collective-permute-done((bf16[2,128,512]{2,1,0:T(8,128)(2,1)S(1)}, bf16[2,128,512]{2,1,0:T(8,128)(2,1)S(1)}, u32[]{:S(2)}, u32[]{:S(2)}) %collective-permute-start.17) | collective-permute-done | bytes 262176 | tf_op jit(solution)/shard_map/ppermute | solution.py:126
  149.5 5.9 %convolution_convert_fusion.1 = bf16[4096,256]{1,0:T(8,128)(2,1)S(1)} fusion(bf16[1024,4096]{1,0:T(8,128)(2,1)} %all-gather.3.cloned.1.call-done, bf16[1024,512]{1,0:T(8,128)(2,1)S(1)} %bitcast.235), kind=kOutput, calls=%fused_computation.1 | convolution fusion | flops 2148532224 | bytes 11010048 | tf_op jit(solution)/shard_map/dot_general | solution.py:152
  155.6 1.6 collective-permute-start.20
  157.8 10.0 %collective-permute-done.20 = bf16[2,512,256]{2,1,0:T(8,128)(2,1)S(1)} collective-permute-done((bf16[2,512,256]{2,1,0:T(8,128)(2,1)S(1)}, bf16[2,512,256]{2,1,0:T(8,128)(2,1)S(1)}, u32[]{:S(2)}, u32[]{:S(2)}) %collective-permute-start.20) | collective-permute-done | bytes 524320 | tf_op jit(solution)/shard_map/ppermute | solution.py:23
  170.5 2.5 convolution_convert_fusion
  173.0 1.9 collective-permute-done.21
  174.9 2.9 collective-permute-done.19
  181.5 2.0 collective-permute-start.27
  183.5 9.6 %collective-permute-done.24 = bf16[2,512,256]{2,1,0:T(8,128)(2,1)S(1)} collective-permute-done((bf16[2,512,256]{2,1,0:T(8,128)(2,1)S(1)}, bf16[2,512,256]{2,1,0:T(8,128)(2,1)S(1)}, u32[]{:S(2)}, u32[]{:S(2)}) %collective-permute-start.24) | collective-permute-done | bytes 524320 | tf_op jit(solution)/shard_map/ppermute | solution.py:23
  193.6 1.9 collective-permute-start.23
  195.5 8.8 %collective-permute-done.27 = bf16[1024,256]{1,0:T(8,128)(2,1)S(1)} collective-permute-done((bf16[1024,256]{1,0:T(8,128)(2,1)S(1)}, bf16[1024,256]{1,0:T(8,128)(2,1)S(1)}, u32[]{:S(2)}, u32[]{:S(2)}) %collective-permute-start.27) | collective-permute-done | bytes 524320 | tf_op jit(solution)/shard_map/ppermute | solution.py:23
  204.5 1.6 collective-permute-start.28
  206.2 3.2 collective-permute-done.25
  210.0 1.9 maximum_negate_fusion
  215.6 3.1 convolution_convert_fusion.3
  218.7 2.1 copy.42
  220.8 5.1 %all-to-all-start.1 = ((bf16[8,128,1,256]{1,3,2,0:T(8,128)(2,1)}), bf16[8,128,1,256]{1,3,2,0:T(8,128)(2,1)}, u32[]{:S(2)}, u32[]{:S(2)}) async-start(bf16[8,128,1,256]{1,3,2,0:T(8,128)(2,1)} %copy.42), calls=%async_computation.1 | async-start | bytes 1048576 | tf_op jit(solution)/shard_map/all_to_all | solution.py:164
  227.9 2.8 fusion
  236.4 4.1 %collective-permute-done.33 = bf16[512,256]{1,0:T(8,128)(2,1)S(1)} collective-permute-done((bf16[512,256]{1,0:T(8,128)(2,1)S(1)}, bf16[512,256]{1,0:T(8,128)(2,1)S(1)}, u32[]{:S(2)}, u32[]{:S(2)}) %collective-permute-start.33) | collective-permute-done | bytes 262176 | tf_op jit(solution)/shard_map/ppermute | solution.py:23
  240.5 1.8 collective-permute-done.32
  242.4 5.7 %convolution_convert_fusion.2 = bf16[1024,256]{1,0:T(8,128)(2,1)S(1)} fusion(bf16[1024,4096]{1,0:T(8,128)(2,1)} %all-gather.3.cloned.1.call-done, bf16[4096,256]{1,0:T(8,128)(2,1)S(1)} %bitcast.224), kind=kOutput, calls=%fused_computation.28 | convolution fusion | flops 2147745792 | bytes 11010048 | tf_op jit(solution)/shard_map/dot_general | solution.py:189
  249.1 4.7 %all-to-all-start = ((bf16[8,128,1,256]{1,3,2,0:T(8,128)(2,1)}), bf16[8,128,1,256]{1,3,2,0:T(8,128)(2,1)S(1)}, u32[]{:S(2)}, u32[]{:S(2)}) async-start(bf16[8,128,1,256]{1,3,2,0:T(8,128)(2,1)} %copy.40), calls=%async_computation | async-start | bytes 1048576 | tf_op jit(solution)/shard_map/all_to_all | solution.py:164
  256.1 6.0 %fusion.55 = (bf16[1024,8,1,256]{0,3,2,1:T(8,128)(2,1)}, bf16[1024,8,1,256]{0,3,2,1:T(8,128)(2,1)}) fusion(bf16[1024,8,2,256]{0,3,2,1:T(8,128)(2,1)} %bitcast.201), kind=kLoop, calls=%fused_computation.136 | loop fusion | bytes 16777216 | tf_op jit(solution)/shard_map/slice | solution.py:169
  262.1 2.0 copy.43
  265.3 3.2 collective-permute-done.34
  268.5 2.0 copy.44
  278.8 7.8 %collective-permute-done.37 = bf16[64,2048]{0,1:T(8,128)(2,1)} collective-permute-done((bf16[64,2048]{0,1:T(8,128)(2,1)}, bf16[64,2048]{0,1:T(8,128)(2,1)}, u32[]{:S(2)}, u32[]{:S(2)}) %collective-permute-start.37) | collective-permute-done | bytes 262176 | tf_op jit(solution)/shard_map/ppermute | solution.py:23
  291.2 5.9 %fusion.60 = f32[1024,512]{1,0:T(8,128)} fusion(bf16[1024,2048]{0,1:T(8,128)(2,1)} %bitcast.220, bf16[512,2048]{1,0:T(8,128)(2,1)S(1)} %bitcast.223), kind=kOutput, calls=%fused_computation.141 | convolution fusion | flops 2147483648 | bytes 8388608 | tf_op jit(solution)/shard_map/dot_general | solution.py:168
  298.9 2.0 slice.133
  304.0 8.9 %collective-permute-done.41 = bf16[64,2048]{0,1:T(8,128)(2,1)} collective-permute-done((bf16[64,2048]{0,1:T(8,128)(2,1)}, bf16[64,2048]{0,1:T(8,128)(2,1)}, u32[]{:S(2)}, u32[]{:S(2)}) %collective-permute-start.41) | collective-permute-done | bytes 262176 | tf_op jit(solution)/shard_map/ppermute | solution.py:23
  315.3 6.2 %add_convert_fusion = bf16[1024,512]{1,0:T(8,128)(2,1)} fusion(f32[1024,512]{1,0:T(8,128)} %fusion.60, bf16[1024,2048]{0,1:T(8,128)(2,1)} %bitcast.219, bf16[512,2048]{1,0:T(8,128)(2,1)S(1)} %bitcast.221), kind=kOutput, calls=%fused_computation.21 | convolution fusion | flops 2148532224 | bytes 9437184 | tf_op jit(solution)/shard_map/dot_general | solution.py:168
  (163 shorter events, 57.5 us)
Async XLA Ops:
  7.2 142.3 %all-gather.3.cloned.1.call-start = ((), (), s32[]{:S(2)}) async-start(), calls=%async_computation.2 | async-start | bytes 9437184 | tf_op jit(solution)/shard_map/all_gather | solution.py:146
  7.2 26.8 %collective-permute-start.3 = (bf16[1024,512]{1,0:T(8,128)(2,1)}, bf16[1024,512]{1,0:T(8,128)(2,1)}, u32[]{:S(2)}, u32[]{:S(2)}) collective-permute-start(bf16[1024,512]{1,0:T(8,128)(2,1)} %param.5), channel_id=1, source_target_pairs={{0,4},{1,5},{4,6},{5,7},{2,0},{3,1},{6,2},{7,3},{8,12},{9,13},{12,... | collective-permute-start | bytes 3145736 | tf_op jit(solution)/shard_map/ppermute | solution.py:110
  12.5 10.3 %collective-permute-start = (bf16[2,128,512]{2,1,0:T(8,128)(2,1)S(1)}, bf16[2,128,512]{2,1,0:T(8,128)(2,1)}, u32[]{:S(2)}, u32[]{:S(2)}) collective-permute-start(bf16[2,128,512]{2,1,0:T(8,128)(2,1)S(1)} %get-tuple-element.43), channel_id=1, source_target_pairs={{0,24},{8,16},{16,8},{24,0},{1,25},{9,17},{17,9},{25,1},{2,26},{10... | collective-permute-start | bytes 786440 | tf_op jit(solution)/shard_map/ppermute | solution.py:23
  15.0 11.9 %collective-permute-start.1 = (bf16[2,128,512]{2,1,0:T(8,128)(2,1)S(1)}, bf16[2,128,512]{2,1,0:T(8,128)(2,1)S(1)}, u32[]{:S(2)}, u32[]{:S(2)}) collective-permute-start(bf16[2,128,512]{2,1,0:T(8,128)(2,1)S(1)} %get-tuple-element.42), channel_id=1, source_target_pairs={{0,8},{8,0},{16,24},{24,16},{1,9},{9,1},{17,25},{25,17},{2,10},{10... | collective-permute-start | bytes 786440 | tf_op jit(solution)/shard_map/ppermute | solution.py:23
  15.5 11.4 %collective-permute-start.2 = (bf16[2,128,512]{2,1,0:T(8,128)(2,1)S(1)}, bf16[2,128,512]{2,1,0:T(8,128)(2,1)S(1)}, u32[]{:S(2)}, u32[]{:S(2)}) collective-permute-start(bf16[2,128,512]{2,1,0:T(8,128)(2,1)S(1)} %get-tuple-element.41), channel_id=1, source_target_pairs={{0,16},{8,24},{16,0},{24,8},{1,17},{9,25},{17,1},{25,9},{2,18},{10... | collective-permute-start | bytes 786440 | tf_op jit(solution)/shard_map/ppermute | solution.py:23
  16.0 20.0 %copy-start.6 = (bf16[1024,512]{1,0:T(8,128)(2,1)S(1)}, bf16[1024,512]{1,0:T(8,128)(2,1)}, u32[]{:S(2)}) copy-start(bf16[1024,512]{1,0:T(8,128)(2,1)} %param.6) | copy-start | bytes 3145732
  34.1 222.1 %all-gather.5.cloned.1.call-start = ((), (), s32[]{:S(2)}) async-start(), calls=%async_computation.3 | async-start | bytes 9437184 | tf_op jit(solution)/shard_map/all_gather | solution.py:147
  34.1 5.9 %collective-permute-start.4 = (bf16[1024,512]{1,0:T(8,128)(2,1)}, bf16[1024,512]{1,0:T(8,128)(2,1)S(1)}, u32[]{:S(2)}, u32[]{:S(2)}) collective-permute-start(bf16[1024,512]{1,0:T(8,128)(2,1)} %param.5), channel_id=1, source_target_pairs={{0,0},{1,1},{4,2},{5,3},{2,4},{3,5},{6,6},{7,7},{8,8},{9,9},{12,10... | collective-permute-start | bytes 3145736 | tf_op jit(solution)/shard_map/ppermute | solution.py:110
  36.0 61.8 %collective-permute-start.6 = (bf16[1024,512]{1,0:T(8,128)(2,1)S(1)}, bf16[1024,512]{1,0:T(8,128)(2,1)S(1)}, u32[]{:S(2)}, u32[]{:S(2)}) collective-permute-start(bf16[1024,512]{1,0:T(8,128)(2,1)S(1)} %copy-done.6), channel_id=1, source_target_pairs={{0,2},{1,3},{2,0},{3,1},{4,6},{5,7},{6,4},{7,5},{8,10},{9,11},{10,... | collective-permute-start | bytes 3145736 | tf_op jit(solution)/shard_map/ppermute | solution.py:102
  40.0 57.8 %collective-permute-start.5 = (bf16[1024,512]{1,0:T(8,128)(2,1)S(1)}, bf16[1024,512]{1,0:T(8,128)(2,1)}, u32[]{:S(2)}, u32[]{:S(2)}) collective-permute-start(bf16[1024,512]{1,0:T(8,128)(2,1)S(1)} %collective-permute-done.4), channel_id=1, source_target_pairs={{0,1},{1,0},{2,3},{3,2},{4,5},{5,4},{6,7},{7,6},{8,9},{9,8},{10,11... | collective-permute-start | bytes 3145736 | tf_op jit(solution)/shard_map/ppermute | solution.py:117
  40.1 65.3 %collective-permute-start.12 = (bf16[1024,512]{1,0:T(8,128)(2,1)}, bf16[1024,512]{1,0:T(8,128)(2,1)S(1)}, u32[]{:S(2)}, u32[]{:S(2)}) collective-permute-start(bf16[1024,512]{1,0:T(8,128)(2,1)} %collective-permute-done.3), channel_id=1, source_target_pairs={{0,1},{1,0},{2,3},{3,2},{4,5},{5,4},{6,7},{7,6},{8,9},{9,8},{10,11... | collective-permute-start | bytes 3145736 | tf_op jit(solution)/shard_map/ppermute | solution.py:117
  102.1 14.9 %collective-permute-start.7 = (bf16[2,1,128,1024]{3,2,1,0:T(8,128)(2,1)S(1)}, bf16[2,1,128,1024]{3,2,1,0:T(8,128)(2,1)S(1)}, u32[]{:S(2)}, u32[]{:S(2)}) collective-permute-start(bf16[2,1,128,1024]{3,2,1,0:T(8,128)(2,1)S(1)} %dynamic-slice_bitcast_fusion.7), channel_id=1, source_target_pairs={{0,8},{8,0},{16,24},{24,16},{1,9},{9,1},{17,25},{25,17},{2,10},{10... | collective-permute-start | bytes 1572872 | tf_op jit(solution)/shard_map/ppermute | solution.py:23
  103.7 14.9 %collective-permute-start.9 = (bf16[2,1,128,1024]{3,2,0,1:T(8,128)(2,1)S(1)}, bf16[2,1,128,1024]{3,2,0,1:T(8,128)(2,1)S(1)}, u32[]{:S(2)}, u32[]{:S(2)}) collective-permute-start(bf16[2,1,128,1024]{3,2,0,1:T(8,128)(2,1)S(1)} %dynamic-slice_bitcast_fusion.6), channel_id=1, source_target_pairs={{0,16},{8,24},{16,0},{24,8},{1,17},{9,25},{17,1},{25,9},{2,18},{10... | collective-permute-start | bytes 1572872 | tf_op jit(solution)/shard_map/ppermute | solution.py:23
  109.7 14.1 %collective-permute-start.13 = (bf16[2,1,128,1024]{3,2,1,0:T(8,128)(2,1)S(1)}, bf16[2,1,128,1024]{3,2,1,0:T(8,128)(2,1)S(1)}, u32[]{:S(2)}, u32[]{:S(2)}) collective-permute-start(bf16[2,1,128,1024]{3,2,1,0:T(8,128)(2,1)S(1)} %dynamic-slice_bitcast_fusion.5), channel_id=1, source_target_pairs={{0,8},{8,0},{16,24},{24,16},{1,9},{9,1},{17,25},{25,17},{2,10},{10... | collective-permute-start | bytes 1572872 | tf_op jit(solution)/shard_map/ppermute | solution.py:23
  110.3 14.3 %collective-permute-start.15 = (bf16[2,1,128,1024]{3,2,0,1:T(8,128)(2,1)S(1)}, bf16[2,1,128,1024]{3,2,0,1:T(8,128)(2,1)S(1)}, u32[]{:S(2)}, u32[]{:S(2)}) collective-permute-start(bf16[2,1,128,1024]{3,2,0,1:T(8,128)(2,1)S(1)} %dynamic-slice_bitcast_fusion.4), channel_id=1, source_target_pairs={{0,16},{8,24},{16,0},{24,8},{1,17},{9,25},{17,1},{25,9},{2,18},{10... | collective-permute-start | bytes 1572872 | tf_op jit(solution)/shard_map/ppermute | solution.py:23
  117.2 9.7 %collective-permute-start.8 = (bf16[1,128,1024]{2,1,0:T(8,128)(2,1)S(1)}, bf16[1,128,1024]{2,1,0:T(8,128)(2,1)S(1)}, u32[]{:S(2)}, u32[]{:S(2)}) collective-permute-start(bf16[1,128,1024]{2,1,0:T(8,128)(2,1)S(1)} %dynamic-slice_bitcast_fusion.15), channel_id=1, source_target_pairs={{0,16},{8,24},{16,0},{24,8},{1,17},{9,25},{17,1},{25,9},{2,18},{10... | collective-permute-start | bytes 786440 | tf_op jit(solution)/shard_map/ppermute | solution.py:23
  118.8 8.2 %collective-permute-start.10 = (bf16[1,128,1024]{2,1,0:T(8,128)(2,1)S(1)}, bf16[1,128,1024]{2,1,0:T(8,128)(2,1)S(1)}, u32[]{:S(2)}, u32[]{:S(2)}) collective-permute-start(bf16[1,128,1024]{2,1,0:T(8,128)(2,1)S(1)} %dynamic-slice_bitcast_fusion.14), channel_id=1, source_target_pairs={{0,8},{8,0},{16,24},{24,16},{1,9},{9,1},{17,25},{25,17},{2,10},{10... | collective-permute-start | bytes 786440 | tf_op jit(solution)/shard_map/ppermute | solution.py:23
  124.0 14.1 %collective-permute-start.14 = (bf16[1,128,1024]{2,1,0:T(8,128)(2,1)S(1)}, bf16[1,128,1024]{2,1,0:T(8,128)(2,1)S(1)}, u32[]{:S(2)}, u32[]{:S(2)}) collective-permute-start(bf16[1,128,1024]{2,1,0:T(8,128)(2,1)S(1)} %dynamic-slice_bitcast_fusion.13), channel_id=1, source_target_pairs={{0,16},{8,24},{16,0},{24,8},{1,17},{9,25},{17,1},{25,9},{2,18},{10... | collective-permute-start | bytes 786440 | tf_op jit(solution)/shard_map/ppermute | solution.py:23
  124.8 13.5 %collective-permute-start.16 = (bf16[1,128,1024]{2,1,0:T(8,128)(2,1)S(1)}, bf16[1,128,1024]{2,1,0:T(8,128)(2,1)S(1)}, u32[]{:S(2)}, u32[]{:S(2)}) collective-permute-start(bf16[1,128,1024]{2,1,0:T(8,128)(2,1)S(1)} %dynamic-slice_bitcast_fusion.12), channel_id=1, source_target_pairs={{0,8},{8,0},{16,24},{24,16},{1,9},{9,1},{17,25},{25,17},{2,10},{10... | collective-permute-start | bytes 786440 | tf_op jit(solution)/shard_map/ppermute | solution.py:23
  127.1 15.6 %collective-permute-start.11 = (bf16[2,128,512]{2,1,0:T(8,128)(2,1)S(1)}, bf16[2,128,512]{2,1,0:T(8,128)(2,1)S(1)}, u32[]{:S(2)}, u32[]{:S(2)}) collective-permute-start(bf16[2,128,512]{2,1,0:T(8,128)(2,1)S(1)} %fusion.51), channel_id=1, source_target_pairs={{0,2},{1,3},{2,0},{3,1},{4,6},{5,7},{6,4},{7,5},{8,10},{9,11},{10,... | collective-permute-start | bytes 786440 | tf_op jit(solution)/shard_map/ppermute | solution.py:126
  138.3 9.8 %collective-permute-start.17 = (bf16[2,128,512]{2,1,0:T(8,128)(2,1)S(1)}, bf16[2,128,512]{2,1,0:T(8,128)(2,1)S(1)}, u32[]{:S(2)}, u32[]{:S(2)}) collective-permute-start(bf16[2,128,512]{2,1,0:T(8,128)(2,1)S(1)} %pad_maximum_fusion.3), channel_id=1, source_target_pairs={{0,2},{1,3},{2,0},{3,1},{4,6},{5,7},{6,4},{7,5},{8,10},{9,11},{10,... | collective-permute-start | bytes 786440 | tf_op jit(solution)/shard_map/ppermute | solution.py:126
  155.4 15.1 %copy-start.7 = (bf16[1024,4096]{1,0:T(8,128)(2,1)S(1)}, bf16[1024,4096]{1,0:T(8,128)(2,1)}, u32[]{:S(2)}) copy-start(bf16[1024,4096]{1,0:T(8,128)(2,1)} %all-gather.3.cloned.1.call-done) | copy-start | bytes 25165828
  155.6 12.3 %collective-permute-start.20 = (bf16[2,512,256]{2,1,0:T(8,128)(2,1)S(1)}, bf16[2,512,256]{2,1,0:T(8,128)(2,1)S(1)}, u32[]{:S(2)}, u32[]{:S(2)}) collective-permute-start(bf16[2,512,256]{2,1,0:T(8,128)(2,1)S(1)} %dynamic-slice_bitcast_fusion.2), channel_id=1, source_target_pairs={{0,16},{8,24},{16,0},{24,8},{1,17},{9,25},{17,1},{25,9},{2,18},{10... | collective-permute-start | bytes 1572872 | tf_op jit(solution)/shard_map/ppermute | solution.py:23
  157.3 12.9 %collective-permute-start.18 = (bf16[2,512,256]{2,1,0:T(8,128)(2,1)S(1)}, bf16[2,512,256]{2,1,0:T(8,128)(2,1)S(1)}, u32[]{:S(2)}, u32[]{:S(2)}) collective-permute-start(bf16[2,512,256]{2,1,0:T(8,128)(2,1)S(1)} %dynamic-slice_bitcast_fusion.3), channel_id=1, source_target_pairs={{0,8},{8,0},{16,24},{24,16},{1,9},{9,1},{17,25},{25,17},{2,10},{10... | collective-permute-start | bytes 1572872 | tf_op jit(solution)/shard_map/ppermute | solution.py:23
  168.1 6.8 %collective-permute-start.21 = (bf16[512,256]{1,0:T(8,128)(2,1)S(1)}, bf16[512,256]{1,0:T(8,128)(2,1)S(1)}, u32[]{:S(2)}, u32[]{:S(2)}) collective-permute-start(bf16[512,256]{1,0:T(8,128)(2,1)S(1)} %dynamic-slice_bitcast_fusion.10), channel_id=1, source_target_pairs={{0,8},{8,0},{16,24},{24,16},{1,9},{9,1},{17,25},{25,17},{2,10},{10... | collective-permute-start | bytes 786440 | tf_op jit(solution)/shard_map/ppermute | solution.py:23
  170.4 7.5 %collective-permute-start.19 = (bf16[512,256]{1,0:T(8,128)(2,1)S(1)}, bf16[512,256]{1,0:T(8,128)(2,1)S(1)}, u32[]{:S(2)}, u32[]{:S(2)}) collective-permute-start(bf16[512,256]{1,0:T(8,128)(2,1)S(1)} %dynamic-slice_bitcast_fusion.11), channel_id=1, source_target_pairs={{0,16},{8,24},{16,0},{24,8},{1,17},{9,25},{17,1},{25,9},{2,18},{10... | collective-permute-start | bytes 786440 | tf_op jit(solution)/shard_map/ppermute | solution.py:23
  178.2 14.9 %collective-permute-start.24 = (bf16[2,512,256]{2,1,0:T(8,128)(2,1)S(1)}, bf16[2,512,256]{2,1,0:T(8,128)(2,1)S(1)}, u32[]{:S(2)}, u32[]{:S(2)}) collective-permute-start(bf16[2,512,256]{2,1,0:T(8,128)(2,1)S(1)} %dynamic-slice_bitcast_fusion), channel_id=1, source_target_pairs={{0,16},{8,24},{16,0},{24,8},{1,17},{9,25},{17,1},{25,9},{2,18},{10... | collective-permute-start | bytes 1572872 | tf_op jit(solution)/shard_map/ppermute | solution.py:23
  178.3 15.1 %collective-permute-start.22 = (bf16[2,512,256]{2,1,0:T(8,128)(2,1)S(1)}, bf16[2,512,256]{2,1,0:T(8,128)(2,1)S(1)}, u32[]{:S(2)}, u32[]{:S(2)}) collective-permute-start(bf16[2,512,256]{2,1,0:T(8,128)(2,1)S(1)} %dynamic-slice_bitcast_fusion.1), channel_id=1, source_target_pairs={{0,8},{8,0},{16,24},{24,16},{1,9},{9,1},{17,25},{25,17},{2,10},{10... | collective-permute-start | bytes 1572872 | tf_op jit(solution)/shard_map/ppermute | solution.py:23
  181.2 23.3 %collective-permute-start.26 = (bf16[1024,256]{1,0:T(8,128)(2,1)S(1)}, bf16[1024,256]{1,0:T(8,128)(2,1)S(1)}, u32[]{:S(2)}, u32[]{:S(2)}) collective-permute-start(bf16[1024,256]{1,0:T(8,128)(2,1)S(1)} %get-tuple-element.26), channel_id=1, source_target_pairs={{0,8},{8,0},{16,24},{24,16},{1,9},{9,1},{17,25},{25,17},{2,10},{10... | collective-permute-start | bytes 1572872 | tf_op jit(solution)/shard_map/ppermute | solution.py:23
  181.5 22.9 %collective-permute-start.27 = (bf16[1024,256]{1,0:T(8,128)(2,1)S(1)}, bf16[1024,256]{1,0:T(8,128)(2,1)S(1)}, u32[]{:S(2)}, u32[]{:S(2)}) collective-permute-start(bf16[1024,256]{1,0:T(8,128)(2,1)S(1)} %get-tuple-element.26), channel_id=1, source_target_pairs={{0,16},{8,24},{16,0},{24,8},{1,17},{9,25},{17,1},{25,9},{2,18},{10... | collective-permute-start | bytes 1572872 | tf_op jit(solution)/shard_map/ppermute | solution.py:23
  193.3 16.0 %collective-permute-start.25 = (bf16[512,256]{1,0:T(8,128)(2,1)S(1)}, bf16[512,256]{1,0:T(8,128)(2,1)S(1)}, u32[]{:S(2)}, u32[]{:S(2)}) collective-permute-start(bf16[512,256]{1,0:T(8,128)(2,1)S(1)} %dynamic-slice_bitcast_fusion.8), channel_id=1, source_target_pairs={{0,8},{8,0},{16,24},{24,16},{1,9},{9,1},{17,25},{25,17},{2,10},{10... | collective-permute-start | bytes 786440 | tf_op jit(solution)/shard_map/ppermute | solution.py:23
  193.6 16.3 %collective-permute-start.23 = (bf16[512,256]{1,0:T(8,128)(2,1)S(1)}, bf16[512,256]{1,0:T(8,128)(2,1)S(1)}, u32[]{:S(2)}, u32[]{:S(2)}) collective-permute-start(bf16[512,256]{1,0:T(8,128)(2,1)S(1)} %dynamic-slice_bitcast_fusion.9), channel_id=1, source_target_pairs={{0,16},{8,24},{16,0},{24,8},{1,17},{9,25},{17,1},{25,9},{2,18},{10... | collective-permute-start | bytes 786440 | tf_op jit(solution)/shard_map/ppermute | solution.py:23
  204.4 10.5 %collective-permute-start.29 = (bf16[512,256]{1,0:T(8,128)(2,1)S(1)}, bf16[512,256]{1,0:T(8,128)(2,1)S(1)}, u32[]{:S(2)}, u32[]{:S(2)}) collective-permute-start(bf16[512,256]{1,0:T(8,128)(2,1)S(1)} %slice.125), channel_id=1, source_target_pairs={{0,8},{8,0},{16,24},{24,16},{1,9},{9,1},{17,25},{25,17},{2,10},{10... | collective-permute-start | bytes 786440 | tf_op jit(solution)/shard_map/ppermute | solution.py:23
  204.5 11.0 %collective-permute-start.28 = (bf16[512,256]{1,0:T(8,128)(2,1)S(1)}, bf16[512,256]{1,0:T(8,128)(2,1)S(1)}, u32[]{:S(2)}, u32[]{:S(2)}) collective-permute-start(bf16[512,256]{1,0:T(8,128)(2,1)S(1)} %slice.124), channel_id=1, source_target_pairs={{0,16},{8,24},{16,0},{24,8},{1,17},{9,25},{17,1},{25,9},{2,18},{10... | collective-permute-start | bytes 786440 | tf_op jit(solution)/shard_map/ppermute | solution.py:23
  211.9 21.0 %collective-permute-start.30 = (bf16[1024,256]{1,0:T(8,128)(2,1)}, bf16[1024,256]{1,0:T(8,128)(2,1)}, u32[]{:S(2)}, u32[]{:S(2)}) collective-permute-start(bf16[1024,256]{1,0:T(8,128)(2,1)} %get-tuple-element.20), channel_id=1, source_target_pairs={{0,8},{8,0},{16,24},{24,16},{1,9},{9,1},{17,25},{25,17},{2,10},{10... | collective-permute-start | bytes 1572872 | tf_op jit(solution)/shard_map/ppermute | solution.py:23
  213.0 17.7 %collective-permute-start.31 = (bf16[1024,256]{1,0:T(8,128)(2,1)}, bf16[1024,256]{1,0:T(8,128)(2,1)}, u32[]{:S(2)}, u32[]{:S(2)}) collective-permute-start(bf16[1024,256]{1,0:T(8,128)(2,1)} %get-tuple-element.20), channel_id=1, source_target_pairs={{0,16},{8,24},{16,0},{24,8},{1,17},{9,25},{17,1},{25,9},{2,18},{10... | collective-permute-start | bytes 1572872 | tf_op jit(solution)/shard_map/ppermute | solution.py:23
  220.8 28.4 %all-to-all-start.1 = ((bf16[8,128,1,256]{1,3,2,0:T(8,128)(2,1)}), bf16[8,128,1,256]{1,3,2,0:T(8,128)(2,1)}, u32[]{:S(2)}, u32[]{:S(2)}) async-start(bf16[8,128,1,256]{1,3,2,0:T(8,128)(2,1)} %copy.42), calls=%async_computation.1 | async-start | bytes 1048576 | tf_op jit(solution)/shard_map/all_to_all | solution.py:164
  231.7 8.8 %collective-permute-start.33 = (bf16[512,256]{1,0:T(8,128)(2,1)S(1)}, bf16[512,256]{1,0:T(8,128)(2,1)S(1)}, u32[]{:S(2)}, u32[]{:S(2)}) collective-permute-start(bf16[512,256]{1,0:T(8,128)(2,1)S(1)} %slice.127), channel_id=1, source_target_pairs={{0,8},{8,0},{16,24},{24,16},{1,9},{9,1},{17,25},{25,17},{2,10},{10... | collective-permute-start | bytes 786440 | tf_op jit(solution)/shard_map/ppermute | solution.py:23
  233.8 8.5 %collective-permute-start.32 = (bf16[512,256]{1,0:T(8,128)(2,1)S(1)}, bf16[512,256]{1,0:T(8,128)(2,1)S(1)}, u32[]{:S(2)}, u32[]{:S(2)}) collective-permute-start(bf16[512,256]{1,0:T(8,128)(2,1)S(1)} %slice.126), channel_id=1, source_target_pairs={{0,16},{8,24},{16,0},{24,8},{1,17},{9,25},{17,1},{25,9},{2,18},{10... | collective-permute-start | bytes 786440 | tf_op jit(solution)/shard_map/ppermute | solution.py:23
  249.1 27.9 %all-to-all-start = ((bf16[8,128,1,256]{1,3,2,0:T(8,128)(2,1)}), bf16[8,128,1,256]{1,3,2,0:T(8,128)(2,1)S(1)}, u32[]{:S(2)}, u32[]{:S(2)}) async-start(bf16[8,128,1,256]{1,3,2,0:T(8,128)(2,1)} %copy.40), calls=%async_computation | async-start | bytes 1048576 | tf_op jit(solution)/shard_map/all_to_all | solution.py:164
  253.8 14.7 %collective-permute-start.34 = (bf16[128,2048]{0,1:T(8,128)(2,1)}, bf16[128,2048]{0,1:T(8,128)(2,1)}, u32[]{:S(2)}, u32[]{:S(2)}) collective-permute-start(bf16[128,2048]{0,1:T(8,128)(2,1)} %bitcast.88), channel_id=1, source_target_pairs={{0,8},{8,0},{16,24},{24,16},{1,9},{9,1},{17,25},{25,17},{2,10},{10... | collective-permute-start | bytes 1572872 | tf_op jit(solution)/shard_map/ppermute | solution.py:23
  254.8 15.8 %collective-permute-start.35 = (bf16[128,2048]{0,1:T(8,128)(2,1)}, bf16[128,2048]{0,1:T(8,128)(2,1)S(1)}, u32[]{:S(2)}, u32[]{:S(2)}) collective-permute-start(bf16[128,2048]{0,1:T(8,128)(2,1)} %bitcast.88), channel_id=1, source_target_pairs={{0,16},{8,24},{16,0},{24,8},{1,17},{9,25},{17,1},{25,9},{2,18},{10... | collective-permute-start | bytes 1572872 | tf_op jit(solution)/shard_map/ppermute | solution.py:23
  271.5 15.1 %collective-permute-start.37 = (bf16[64,2048]{0,1:T(8,128)(2,1)}, bf16[64,2048]{0,1:T(8,128)(2,1)}, u32[]{:S(2)}, u32[]{:S(2)}) collective-permute-start(bf16[64,2048]{0,1:T(8,128)(2,1)} %slice.130), channel_id=1, source_target_pairs={{0,8},{8,0},{16,24},{24,16},{1,9},{9,1},{17,25},{25,17},{2,10},{10... | collective-permute-start | bytes 786440 | tf_op jit(solution)/shard_map/ppermute | solution.py:23
  272.4 15.2 %collective-permute-start.36 = (bf16[64,2048]{0,1:T(8,128)(2,1)}, bf16[64,2048]{0,1:T(8,128)(2,1)}, u32[]{:S(2)}, u32[]{:S(2)}) collective-permute-start(bf16[64,2048]{0,1:T(8,128)(2,1)} %bitcast.199), channel_id=1, source_target_pairs={{0,16},{8,24},{16,0},{24,8},{1,17},{9,25},{17,1},{25,9},{2,18},{10... | collective-permute-start | bytes 786440 | tf_op jit(solution)/shard_map/ppermute | solution.py:23
  277.0 20.6 %collective-permute-start.38 = (bf16[128,2048]{0,1:T(8,128)(2,1)S(1)}, bf16[128,2048]{0,1:T(8,128)(2,1)}, u32[]{:S(2)}, u32[]{:S(2)}) collective-permute-start(bf16[128,2048]{0,1:T(8,128)(2,1)S(1)} %bitcast.229), channel_id=1, source_target_pairs={{0,8},{8,0},{16,24},{24,16},{1,9},{9,1},{17,25},{25,17},{2,10},{10... | collective-permute-start | bytes 1572872 | tf_op jit(solution)/shard_map/ppermute | solution.py:23
  277.4 21.5 %collective-permute-start.39 = (bf16[128,2048]{0,1:T(8,128)(2,1)S(1)}, bf16[128,2048]{0,1:T(8,128)(2,1)}, u32[]{:S(2)}, u32[]{:S(2)}) collective-permute-start(bf16[128,2048]{0,1:T(8,128)(2,1)S(1)} %bitcast.230), channel_id=1, source_target_pairs={{0,16},{8,24},{16,0},{24,8},{1,17},{9,25},{17,1},{25,9},{2,18},{10... | collective-permute-start | bytes 1572872 | tf_op jit(solution)/shard_map/ppermute | solution.py:23
  300.9 12.0 %collective-permute-start.41 = (bf16[64,2048]{0,1:T(8,128)(2,1)}, bf16[64,2048]{0,1:T(8,128)(2,1)}, u32[]{:S(2)}, u32[]{:S(2)}) collective-permute-start(bf16[64,2048]{0,1:T(8,128)(2,1)} %slice.133), channel_id=1, source_target_pairs={{0,8},{8,0},{16,24},{24,16},{1,9},{9,1},{17,25},{25,17},{2,10},{10... | collective-permute-start | bytes 786440 | tf_op jit(solution)/shard_map/ppermute | solution.py:23
  302.1 11.5 %collective-permute-start.40 = (bf16[64,2048]{0,1:T(8,128)(2,1)}, bf16[64,2048]{0,1:T(8,128)(2,1)}, u32[]{:S(2)}, u32[]{:S(2)}) collective-permute-start(bf16[64,2048]{0,1:T(8,128)(2,1)} %bitcast.200), channel_id=1, source_target_pairs={{0,16},{8,24},{16,0},{24,8},{1,17},{9,25},{17,1},{25,9},{2,18},{10... | collective-permute-start | bytes 786440 | tf_op jit(solution)/shard_map/ppermute | solution.py:23
  (6 other events, 15.8 us)
Sparse Core Ops, SparseCore 0:
  34.2 97.1 all-gather.2
  149.6 84.0 all-gather.4

commit v7 on v5

--- a/solution.py
+++ b/solution.py
@@ -138,7 +138,7 @@
         per = cols // rows
         sub = width // rows
         mid = width // 2
-        spans = (slice(0, mid), slice(mid, width))
+        spans = (slice(mid, width), slice(0, mid))
 
         dealt = deal(right_basis.reshape(per, rows, sub, width)).reshape(depth, width)
         half, dealt = rotate_left(forget_grad, left_basis, dealt, rows, cols)
@@ -158,12 +158,12 @@
         value, parts[1] = lax.optimization_barrier((scatter_sum(parts[0]), parts[1]))
         values = [value, scatter_sum(parts[1])]
         values = [-value for value in values]
-        rotated = jnp.concatenate(values, 1)
+        rotated = jnp.concatenate(values[::-1], 1)
 
         def finish(term, c):
             term = lax.all_to_all(term.reshape(cols, sub, mid), "cols", 0, 1)
             return lax.dot_general(
-                left_rows[:, :, c].reshape(depth, cols * mid),
+                left_rows[:, :, 1 - c].reshape(depth, cols * mid),
                 gather(term.reshape(sub, cols * mid), rows).reshape(width, cols * mid),
                 (((1,), (1,)), ((), ())),
                 preferred_element_type=f32,

time: 324 us -> 324 us (level)
  no operation moved by 1% of the time
where the time goes in v7:
time: 324 us; the launch traced here: 323 us
  waiting for transfers between devices  162 us (50%)
  starting transfers between devices  70.9 us (22%)
  local copies, waits for them, and re-layouts  34.6 us (11%)
  matrix products  31.5 us (10%)
  between operations  14.7 us (5%)
  other arithmetic  9.37 us (3%)
    ppermute x35, waiting for transfers between devices, swap(): return lax.ppermute(block, 'rows', [(i, i ^ mask) for i in range(count)])  88.5 us
    ppermute x1, waiting for transfers between devices, rotate_left(): lax.ppermute(left, 'cols', [(i, i ^ 2) for i in range(cols)])  57.2 us
    ppermute x35, starting transfers between devices, swap(): return lax.ppermute(block, 'rows', [(i, i ^ mask) for i in range(count)])  40.3 us
    all_to_all x2, starting transfers between devices, finish(): term = lax.all_to_all(term.reshape(cols, sub, mid), 'cols', 0, 1)  10.7 us
    ppermute x2, starting transfers between devices, rotate_left(): lax.ppermute(sums[..., :width], 'cols', [(i, i ^ 2) for i in range(cols)])  9.22 us
    ppermute x2, waiting for transfers between devices, rotate_left(): lax.ppermute(sums[..., :width], 'cols', [(i, i ^ 2) for i in range(cols)])  9 us
    dot_general x2, matrix products, local(): term = jnp.dot(right_rows, normals, preferred_element_type=f32).astype(bf16)  8.86 us
    dot_general x2, matrix products, product(): lax.dot_general(blocks, left, (((1,), (0,)), ((), ())), preferred_element...  8.55 us
  transfers between devices with their start and end apart: 46, of which 28 were waited for; matrix products, arithmetic and copies ran while one was open for 21% of the time, Pallas kernels for 0%

profile of v7, /device:TPU:0, one launch (start us, length us, event | category | flops | bytes accessed | tf_op | source)
XLA Modules:
  0.0 323.0 jit_solution(9102154522297449414)
XLA Ops:
  7.2 4.1 %collective-permute-start.11 = (bf16[1024,512]{1,0:T(8,128)(2,1)}, bf16[1024,512]{1,0:T(8,128)(2,1)}, u32[]{:S(2)}, u32[]{:S(2)}) collective-permute-start(bf16[1024,512]{1,0:T(8,128)(2,1)} %param.5), channel_id=1, source_target_pairs={{0,4},{1,5},{4,6},{5,7},{2,0},{3,1},{6,2},{7,3},{8,12},{9,13},{12,... | collective-permute-start | bytes 3145736 | tf_op jit(solution)/shard_map/ppermute | solution.py:110
  12.5 2.5 collective-permute-start.8
  17.2 5.6 %collective-permute-done.8 = bf16[2,128,512]{2,1,0:T(8,128)(2,1)} collective-permute-done((bf16[2,128,512]{2,1,0:T(8,128)(2,1)S(1)}, bf16[2,128,512]{2,1,0:T(8,128)(2,1)}, u32[]{:S(2)}, u32[]{:S(2)}) %collective-permute-start.8) | collective-permute-done | bytes 262176 | tf_op jit(solution)/shard_map/ppermute | solution.py:23
  23.8 3.1 collective-permute-done.9
  27.0 7.0 %collective-permute-done.11 = bf16[1024,512]{1,0:T(8,128)(2,1)} collective-permute-done((bf16[1024,512]{1,0:T(8,128)(2,1)}, bf16[1024,512]{1,0:T(8,128)(2,1)}, u32[]{:S(2)}, u32[]{:S(2)}) %collective-permute-start.11) | collective-permute-done | bytes 1048608 | tf_op jit(solution)/shard_map/ppermute | solution.py:110
  34.1 1.9 collective-permute-start
  36.0 4.0 %collective-permute-start.2 = (bf16[1024,512]{1,0:T(8,128)(2,1)S(1)}, bf16[1024,512]{1,0:T(8,128)(2,1)S(1)}, u32[]{:S(2)}, u32[]{:S(2)}) collective-permute-start(bf16[1024,512]{1,0:T(8,128)(2,1)S(1)} %copy-done.10), channel_id=1, source_target_pairs={{0,2},{1,3},{2,0},{3,1},{4,6},{5,7},{6,4},{7,5},{8,10},{9,11},{10,... | collective-permute-start | bytes 3145736 | tf_op jit(solution)/shard_map/ppermute | solution.py:102
  40.6 57.2 %collective-permute-done.2 = bf16[1024,512]{1,0:T(8,128)(2,1)S(1)} collective-permute-done((bf16[1024,512]{1,0:T(8,128)(2,1)S(1)}, bf16[1024,512]{1,0:T(8,128)(2,1)S(1)}, u32[]{:S(2)}, u32[]{:S(2)}) %collective-permute-start.2) | collective-permute-done | bytes 1048608 | tf_op jit(solution)/shard_map/ppermute | solution.py:102
  97.8 4.6 %fusion.15 = bf16[2,512,1024]{2,1,0:T(8,128)(2,1)S(1)} fusion(bf16[1,1024,512]{2,1,0:T(8,128)(2,1)} %bitcast.28, bf16[1,1024,512]{2,1,0:T(8,128)(2,1)} %bitcast.27, pred[]{:T(512)S(6)} %eq.4, bf16[1024,512]{1,0:T(8,128)(2,1)S(1)} %copy-done.10, bf16[1024,512]{1,0:T(8,128)(2,1)S(1)} %collective-permute-done.2), kind=kOutput, calls=%fused_computation.24 | convolution fusion | flops 2155872256 | bytes 6291457 | tf_op jit(solution)/shard_map/dot_general | solution.py:90
  104.3 4.0 %fusion.16 = bf16[2,512,1024]{2,1,0:T(8,128)(2,1)S(1)} fusion(bf16[1,1024,512]{2,1,0:T(8,128)(2,1)} %bitcast.1, bf16[1,1024,512]{2,1,0:T(8,128)(2,1)S(1)} %bitcast.242, pred[]{:T(512)S(6)} %eq.4, bf16[1024,512]{1,0:T(8,128)(2,1)S(1)} %copy-done.10, bf16[1024,512]{1,0:T(8,128)(2,1)S(1)} %collective-permute-done.2), kind=kOutput, calls=%fused_computation.25 | convolution fusion | flops 2155872256 | bytes 6291457 | tf_op jit(solution)/shard_map/dot_general | solution.py:90
  113.7 6.6 %collective-permute-done.5 = bf16[2,1,128,1024]{3,2,0,1:T(8,128)(2,1)S(1)} collective-permute-done((bf16[2,1,128,1024]{3,2,0,1:T(8,128)(2,1)S(1)}, bf16[2,1,128,1024]{3,2,0,1:T(8,128)(2,1)S(1)}, u32[]{:S(2)}, u32[]{:S(2)}) %collective-permute-start.5) | collective-permute-done | bytes 524320 | tf_op jit(solution)/shard_map/ppermute | solution.py:23
  122.1 6.7 %collective-permute-done.3 = bf16[2,1,128,1024]{3,2,1,0:T(8,128)(2,1)S(1)} collective-permute-done((bf16[2,1,128,1024]{3,2,1,0:T(8,128)(2,1)S(1)}, bf16[2,1,128,1024]{3,2,1,0:T(8,128)(2,1)S(1)}, u32[]{:S(2)}, u32[]{:S(2)}) %collective-permute-start.3) | collective-permute-done | bytes 524320 | tf_op jit(solution)/shard_map/ppermute | solution.py:23
  129.1 1.6 collective-permute-start.4
  131.5 3.0 collective-permute-done.6
  135.6 8.4 %collective-permute-start.7 = (bf16[2,128,512]{2,1,0:T(8,128)(2,1)S(1)}, bf16[2,128,512]{2,1,0:T(8,128)(2,1)S(1)}, u32[]{:S(2)}, u32[]{:S(2)}) collective-permute-start(bf16[2,128,512]{2,1,0:T(8,128)(2,1)S(1)} %fusion.52), channel_id=1, source_target_pairs={{0,2},{1,3},{2,0},{3,1},{4,6},{5,7},{6,4},{7,5},{8,10},{9,11},{10,... | collective-permute-start | bytes 786440 | tf_op jit(solution)/shard_map/ppermute | solution.py:126
  145.2 6.1 %collective-permute-done.7 = bf16[2,128,512]{2,1,0:T(8,128)(2,1)S(1)} collective-permute-done((bf16[2,128,512]{2,1,0:T(8,128)(2,1)S(1)}, bf16[2,128,512]{2,1,0:T(8,128)(2,1)S(1)}, u32[]{:S(2)}, u32[]{:S(2)}) %collective-permute-start.7) | collective-permute-done | bytes 262176 | tf_op jit(solution)/shard_map/ppermute | solution.py:126
  151.3 2.9 collective-permute-done.17
  155.6 5.9 %convolution_convert_fusion.1 = bf16[4096,256]{1,0:T(8,128)(2,1)S(1)} fusion(bf16[1024,4096]{1,0:T(8,128)(2,1)} %all-gather.5.cloned.1.call-done, bf16[1024,512]{1,0:T(8,128)(2,1)S(1)} %bitcast.238), kind=kOutput, calls=%fused_computation.1 | convolution fusion | flops 2148532224 | bytes 11010048 | tf_op jit(solution)/shard_map/dot_general | solution.py:152
  164.6 8.5 %collective-permute-done.18 = bf16[2,512,256]{2,1,0:T(8,128)(2,1)S(1)} collective-permute-done((bf16[2,512,256]{2,1,0:T(8,128)(2,1)S(1)}, bf16[2,512,256]{2,1,0:T(8,128)(2,1)S(1)}, u32[]{:S(2)}, u32[]{:S(2)}) %collective-permute-start.18) | collective-permute-done | bytes 524320 | tf_op jit(solution)/shard_map/ppermute | solution.py:23
  176.6 2.5 convolution_convert_fusion
  179.7 4.0 %collective-permute-done.21 = bf16[512,256]{1,0:T(8,128)(2,1)S(1)} collective-permute-done((bf16[512,256]{1,0:T(8,128)(2,1)S(1)}, bf16[512,256]{1,0:T(8,128)(2,1)S(1)}, u32[]{:S(2)}, u32[]{:S(2)}) %collective-permute-start.21) | collective-permute-done | bytes 262176 | tf_op jit(solution)/shard_map/ppermute | solution.py:23
  185.4 1.7 collective-permute-start.24
  188.1 2.1 collective-permute-start.26
  190.2 8.8 %collective-permute-done.22 = bf16[2,512,256]{2,1,0:T(8,128)(2,1)S(1)} collective-permute-done((bf16[2,512,256]{2,1,0:T(8,128)(2,1)S(1)}, bf16[2,512,256]{2,1,0:T(8,128)(2,1)S(1)}, u32[]{:S(2)}, u32[]{:S(2)}) %collective-permute-start.22) | collective-permute-done | bytes 524320 | tf_op jit(solution)/shard_map/ppermute | solution.py:23
  199.2 2.8 collective-permute-start.23
  202.3 7.9 %collective-permute-done.26 = bf16[1024,256]{1,0:T(8,128)(2,1)S(1)} collective-permute-done((bf16[1024,256]{1,0:T(8,128)(2,1)S(1)}, bf16[1024,256]{1,0:T(8,128)(2,1)S(1)}, u32[]{:S(2)}, u32[]{:S(2)}) %collective-permute-start.26) | collective-permute-done | bytes 524320 | tf_op jit(solution)/shard_map/ppermute | solution.py:23
  210.3 2.8 collective-permute-start.28
  213.8 2.1 collective-permute-done.25
  215.9 1.9 maximum_negate_fusion
  221.3 3.1 convolution_convert_fusion.3
  224.4 2.1 copy.40
  226.5 6.0 %all-to-all-start = ((bf16[8,128,1,256]{1,3,2,0:T(8,128)(2,1)}), bf16[8,128,1,256]{1,3,2,0:T(8,128)(2,1)}, u32[]{:S(2)}, u32[]{:S(2)}) async-start(bf16[8,128,1,256]{1,3,2,0:T(8,128)(2,1)} %copy.40), calls=%async_computation | async-start | bytes 1048576 | tf_op jit(solution)/shard_map/all_to_all | solution.py:164
  234.6 2.8 fusion
  238.4 1.8 collective-permute-start.36
  243.4 3.8 %collective-permute-done.36 = bf16[512,256]{1,0:T(8,128)(2,1)S(1)} collective-permute-done((bf16[512,256]{1,0:T(8,128)(2,1)S(1)}, bf16[512,256]{1,0:T(8,128)(2,1)S(1)}, u32[]{:S(2)}, u32[]{:S(2)}) %collective-permute-start.36) | collective-permute-done | bytes 262176 | tf_op jit(solution)/shard_map/ppermute | solution.py:23
  247.2 2.5 collective-permute-done.37
  249.7 5.7 %convolution_convert_fusion.2 = bf16[1024,256]{1,0:T(8,128)(2,1)S(1)} fusion(bf16[1024,4096]{1,0:T(8,128)(2,1)} %all-gather.5.cloned.1.call-done, bf16[4096,256]{1,0:T(8,128)(2,1)S(1)} %bitcast.230), kind=kOutput, calls=%fused_computation.28 | convolution fusion | flops 2147745792 | bytes 11010048 | tf_op jit(solution)/shard_map/dot_general | solution.py:185
  256.5 4.7 %all-to-all-start.1 = ((bf16[8,128,1,256]{1,3,2,0:T(8,128)(2,1)}), bf16[8,128,1,256]{1,3,2,0:T(8,128)(2,1)S(1)}, u32[]{:S(2)}, u32[]{:S(2)}) async-start(bf16[8,128,1,256]{1,3,2,0:T(8,128)(2,1)} %copy.45), calls=%async_computation.1 | async-start | bytes 1048576 | tf_op jit(solution)/shard_map/all_to_all | solution.py:164
  261.9 6.0 %fusion.56 = (bf16[1024,8,1,256]{0,3,2,1:T(8,128)(2,1)}, bf16[1024,8,1,256]{0,3,2,1:T(8,128)(2,1)}) fusion(bf16[1024,8,2,256]{0,3,2,1:T(8,128)(2,1)} %bitcast.205), kind=kLoop, calls=%fused_computation.136 | loop fusion | bytes 16777216 | tf_op jit(solution)/shard_map/slice | solution.py:166
  267.8 2.0 copy.41
  271.0 4.7 %collective-permute-done.31 = bf16[128,2048]{0,1:T(8,128)(2,1)S(1)} collective-permute-done((bf16[128,2048]{0,1:T(8,128)(2,1)}, bf16[128,2048]{0,1:T(8,128)(2,1)S(1)}, u32[]{:S(2)}, u32[]{:S(2)}) %collective-permute-start.31) | collective-permute-done | bytes 524320 | tf_op jit(solution)/shard_map/ppermute | solution.py:23
  277.6 2.1 copy.42
  284.2 1.7 collective-permute-start.39
  287.1 4.8 %collective-permute-done.33 = bf16[64,2048]{0,1:T(8,128)(2,1)} collective-permute-done((bf16[64,2048]{0,1:T(8,128)(2,1)}, bf16[64,2048]{0,1:T(8,128)(2,1)}, u32[]{:S(2)}, u32[]{:S(2)}) %collective-permute-start.33) | collective-permute-done | bytes 262176 | tf_op jit(solution)/shard_map/ppermute | solution.py:23
  294.4 7.4 %collective-permute-done.38 = bf16[128,2048]{1,0:T(8,128)(2,1)S(1)} collective-permute-done((bf16[128,2048]{1,0:T(8,128)(2,1)}, bf16[128,2048]{1,0:T(8,128)(2,1)S(1)}, u32[]{:S(2)}, u32[]{:S(2)}) %collective-permute-start.38) | collective-permute-done | bytes 524320 | tf_op jit(solution)/shard_map/ppermute | solution.py:23
  305.8 3.3 %collective-permute-done.40 = bf16[64,2048]{1,0:T(8,128)(2,1)S(1)} collective-permute-done((bf16[64,2048]{1,0:T(8,128)(2,1)S(1)}, bf16[64,2048]{1,0:T(8,128)(2,1)S(1)}, u32[]{:S(2)}, u32[]{:S(2)}) %collective-permute-start.40) | collective-permute-done | bytes 262176 | tf_op jit(solution)/shard_map/ppermute | solution.py:23
  310.4 2.4 fusion.61
  312.8 3.4 %add_convert_fusion = bf16[1024,512]{1,0:T(8,128)(2,1)} fusion(f32[1024,512]{1,0:T(8,128)S(1)} %fusion.61, bf16[1024,2048]{0,1:T(8,128)(2,1)S(1)} %bitcast.225, bf16[512,2048]{1,0:T(8,128)(2,1)S(1)} %bitcast.227), kind=kOutput, calls=%fused_computation.21 | convolution fusion | flops 2148532224 | bytes 9437184 | tf_op jit(solution)/shard_map/dot_general | solution.py:165
  (168 shorter events, 57.4 us)
Async XLA Ops:
  7.2 148.4 %all-gather.5.cloned.1.call-start = ((), (), s32[]{:S(2)}) async-start(), calls=%async_computation.3 | async-start | bytes 9437184 | tf_op jit(solution)/shard_map/all_gather | solution.py:146
  7.2 26.8 %collective-permute-start.11 = (bf16[1024,512]{1,0:T(8,128)(2,1)}, bf16[1024,512]{1,0:T(8,128)(2,1)}, u32[]{:S(2)}, u32[]{:S(2)}) collective-permute-start(bf16[1024,512]{1,0:T(8,128)(2,1)} %param.5), channel_id=1, source_target_pairs={{0,4},{1,5},{4,6},{5,7},{2,0},{3,1},{6,2},{7,3},{8,12},{9,13},{12,... | collective-permute-start | bytes 3145736 | tf_op jit(solution)/shard_map/ppermute | solution.py:110
  12.5 10.3 %collective-permute-start.8 = (bf16[2,128,512]{2,1,0:T(8,128)(2,1)S(1)}, bf16[2,128,512]{2,1,0:T(8,128)(2,1)}, u32[]{:S(2)}, u32[]{:S(2)}) collective-permute-start(bf16[2,128,512]{2,1,0:T(8,128)(2,1)S(1)} %get-tuple-element.39), channel_id=1, source_target_pairs={{0,24},{8,16},{16,8},{24,0},{1,25},{9,17},{17,9},{25,1},{2,26},{10... | collective-permute-start | bytes 786440 | tf_op jit(solution)/shard_map/ppermute | solution.py:23
  15.0 11.9 %collective-permute-start.9 = (bf16[2,128,512]{2,1,0:T(8,128)(2,1)S(1)}, bf16[2,128,512]{2,1,0:T(8,128)(2,1)S(1)}, u32[]{:S(2)}, u32[]{:S(2)}) collective-permute-start(bf16[2,128,512]{2,1,0:T(8,128)(2,1)S(1)} %get-tuple-element.38), channel_id=1, source_target_pairs={{0,8},{8,0},{16,24},{24,16},{1,9},{9,1},{17,25},{25,17},{2,10},{10... | collective-permute-start | bytes 786440 | tf_op jit(solution)/shard_map/ppermute | solution.py:23
  15.5 11.4 %collective-permute-start.10 = (bf16[2,128,512]{2,1,0:T(8,128)(2,1)S(1)}, bf16[2,128,512]{2,1,0:T(8,128)(2,1)S(1)}, u32[]{:S(2)}, u32[]{:S(2)}) collective-permute-start(bf16[2,128,512]{2,1,0:T(8,128)(2,1)S(1)} %get-tuple-element.37), channel_id=1, source_target_pairs={{0,16},{8,24},{16,0},{24,8},{1,17},{9,25},{17,1},{25,9},{2,18},{10... | collective-permute-start | bytes 786440 | tf_op jit(solution)/shard_map/ppermute | solution.py:23
  16.0 20.0 %copy-start.10 = (bf16[1024,512]{1,0:T(8,128)(2,1)S(1)}, bf16[1024,512]{1,0:T(8,128)(2,1)}, u32[]{:S(2)}) copy-start(bf16[1024,512]{1,0:T(8,128)(2,1)} %param.6) | copy-start | bytes 3145732
  34.1 227.8 %all-gather.3.cloned.1.call-start = ((), (), s32[]{:S(2)}) async-start(), calls=%async_computation.2 | async-start | bytes 9437184 | tf_op jit(solution)/shard_map/all_gather | solution.py:147
  34.1 5.9 %collective-permute-start = (bf16[1024,512]{1,0:T(8,128)(2,1)}, bf16[1024,512]{1,0:T(8,128)(2,1)S(1)}, u32[]{:S(2)}, u32[]{:S(2)}) collective-permute-start(bf16[1024,512]{1,0:T(8,128)(2,1)} %param.5), channel_id=1, source_target_pairs={{0,0},{1,1},{4,2},{5,3},{2,4},{3,5},{6,6},{7,7},{8,8},{9,9},{12,10... | collective-permute-start | bytes 3145736 | tf_op jit(solution)/shard_map/ppermute | solution.py:110
  36.0 61.8 %collective-permute-start.2 = (bf16[1024,512]{1,0:T(8,128)(2,1)S(1)}, bf16[1024,512]{1,0:T(8,128)(2,1)S(1)}, u32[]{:S(2)}, u32[]{:S(2)}) collective-permute-start(bf16[1024,512]{1,0:T(8,128)(2,1)S(1)} %copy-done.10), channel_id=1, source_target_pairs={{0,2},{1,3},{2,0},{3,1},{4,6},{5,7},{6,4},{7,5},{8,10},{9,11},{10,... | collective-permute-start | bytes 3145736 | tf_op jit(solution)/shard_map/ppermute | solution.py:102
  40.0 57.8 %collective-permute-start.12 = (bf16[1024,512]{1,0:T(8,128)(2,1)}, bf16[1024,512]{1,0:T(8,128)(2,1)}, u32[]{:S(2)}, u32[]{:S(2)}) collective-permute-start(bf16[1024,512]{1,0:T(8,128)(2,1)} %collective-permute-done.11), channel_id=1, source_target_pairs={{0,1},{1,0},{2,3},{3,2},{4,5},{5,4},{6,7},{7,6},{8,9},{9,8},{10,11... | collective-permute-start | bytes 3145736 | tf_op jit(solution)/shard_map/ppermute | solution.py:117
  40.1 64.2 %collective-permute-start.1 = (bf16[1024,512]{1,0:T(8,128)(2,1)S(1)}, bf16[1024,512]{1,0:T(8,128)(2,1)}, u32[]{:S(2)}, u32[]{:S(2)}) collective-permute-start(bf16[1024,512]{1,0:T(8,128)(2,1)S(1)} %collective-permute-done), channel_id=1, source_target_pairs={{0,1},{1,0},{2,3},{3,2},{4,5},{5,4},{6,7},{7,6},{8,9},{9,8},{10,11... | collective-permute-start | bytes 3145736 | tf_op jit(solution)/shard_map/ppermute | solution.py:117
  102.6 9.2 %collective-permute-start.15 = (bf16[2,1,128,1024]{3,2,0,1:T(8,128)(2,1)S(1)}, bf16[2,1,128,1024]{3,2,0,1:T(8,128)(2,1)S(1)}, u32[]{:S(2)}, u32[]{:S(2)}) collective-permute-start(bf16[2,1,128,1024]{3,2,0,1:T(8,128)(2,1)S(1)} %dynamic-slice_bitcast_fusion.4), channel_id=1, source_target_pairs={{0,16},{8,24},{16,0},{24,8},{1,17},{9,25},{17,1},{25,9},{2,18},{10... | collective-permute-start | bytes 1572872 | tf_op jit(solution)/shard_map/ppermute | solution.py:23
  108.5 11.8 %collective-permute-start.5 = (bf16[2,1,128,1024]{3,2,0,1:T(8,128)(2,1)S(1)}, bf16[2,1,128,1024]{3,2,0,1:T(8,128)(2,1)S(1)}, u32[]{:S(2)}, u32[]{:S(2)}) collective-permute-start(bf16[2,1,128,1024]{3,2,0,1:T(8,128)(2,1)S(1)} %dynamic-slice_bitcast_fusion.6), channel_id=1, source_target_pairs={{0,16},{8,24},{16,0},{24,8},{1,17},{9,25},{17,1},{25,9},{2,18},{10... | collective-permute-start | bytes 1572872 | tf_op jit(solution)/shard_map/ppermute | solution.py:23
  109.0 21.7 %collective-permute-start.13 = (bf16[2,1,128,1024]{3,2,1,0:T(8,128)(2,1)S(1)}, bf16[2,1,128,1024]{3,2,1,0:T(8,128)(2,1)S(1)}, u32[]{:S(2)}, u32[]{:S(2)}) collective-permute-start(bf16[2,1,128,1024]{3,2,1,0:T(8,128)(2,1)S(1)} %dynamic-slice_bitcast_fusion.5), channel_id=1, source_target_pairs={{0,8},{8,0},{16,24},{24,16},{1,9},{9,1},{17,25},{25,17},{2,10},{10... | collective-permute-start | bytes 1572872 | tf_op jit(solution)/shard_map/ppermute | solution.py:23
  110.7 18.2 %collective-permute-start.3 = (bf16[2,1,128,1024]{3,2,1,0:T(8,128)(2,1)S(1)}, bf16[2,1,128,1024]{3,2,1,0:T(8,128)(2,1)S(1)}, u32[]{:S(2)}, u32[]{:S(2)}) collective-permute-start(bf16[2,1,128,1024]{3,2,1,0:T(8,128)(2,1)S(1)} %dynamic-slice_bitcast_fusion.7), channel_id=1, source_target_pairs={{0,8},{8,0},{16,24},{24,16},{1,9},{9,1},{17,25},{25,17},{2,10},{10... | collective-permute-start | bytes 1572872 | tf_op jit(solution)/shard_map/ppermute | solution.py:23
  112.1 31.9 %collective-permute-start.16 = (bf16[1,128,1024]{2,1,0:T(8,128)(2,1)S(1)}, bf16[1,128,1024]{2,1,0:T(8,128)(2,1)S(1)}, u32[]{:S(2)}, u32[]{:S(2)}) collective-permute-start(bf16[1,128,1024]{2,1,0:T(8,128)(2,1)S(1)} %dynamic-slice_bitcast_fusion.12), channel_id=1, source_target_pairs={{0,8},{8,0},{16,24},{24,16},{1,9},{9,1},{17,25},{25,17},{2,10},{10... | collective-permute-start | bytes 786440 | tf_op jit(solution)/shard_map/ppermute | solution.py:23
  120.5 13.9 %collective-permute-start.6 = (bf16[1,128,1024]{2,1,0:T(8,128)(2,1)S(1)}, bf16[1,128,1024]{2,1,0:T(8,128)(2,1)S(1)}, u32[]{:S(2)}, u32[]{:S(2)}) collective-permute-start(bf16[1,128,1024]{2,1,0:T(8,128)(2,1)S(1)} %dynamic-slice_bitcast_fusion.17), channel_id=1, source_target_pairs={{0,8},{8,0},{16,24},{24,16},{1,9},{9,1},{17,25},{25,17},{2,10},{10... | collective-permute-start | bytes 786440 | tf_op jit(solution)/shard_map/ppermute | solution.py:23
  129.1 6.4 %collective-permute-start.4 = (bf16[1,128,1024]{2,1,0:T(8,128)(2,1)S(1)}, bf16[1,128,1024]{2,1,0:T(8,128)(2,1)S(1)}, u32[]{:S(2)}, u32[]{:S(2)}) collective-permute-start(bf16[1,128,1024]{2,1,0:T(8,128)(2,1)S(1)} %dynamic-slice_bitcast_fusion.18), channel_id=1, source_target_pairs={{0,16},{8,24},{16,0},{24,8},{1,17},{9,25},{17,1},{25,9},{2,18},{10... | collective-permute-start | bytes 786440 | tf_op jit(solution)/shard_map/ppermute | solution.py:23
  131.0 13.1 %collective-permute-start.14 = (bf16[1,128,1024]{2,1,0:T(8,128)(2,1)S(1)}, bf16[1,128,1024]{2,1,0:T(8,128)(2,1)S(1)}, u32[]{:S(2)}, u32[]{:S(2)}) collective-permute-start(bf16[1,128,1024]{2,1,0:T(8,128)(2,1)S(1)} %dynamic-slice_bitcast_fusion.13), channel_id=1, source_target_pairs={{0,16},{8,24},{16,0},{24,8},{1,17},{9,25},{17,1},{25,9},{2,18},{10... | collective-permute-start | bytes 786440 | tf_op jit(solution)/shard_map/ppermute | solution.py:23
  135.6 15.6 %collective-permute-start.7 = (bf16[2,128,512]{2,1,0:T(8,128)(2,1)S(1)}, bf16[2,128,512]{2,1,0:T(8,128)(2,1)S(1)}, u32[]{:S(2)}, u32[]{:S(2)}) collective-permute-start(bf16[2,128,512]{2,1,0:T(8,128)(2,1)S(1)} %fusion.52), channel_id=1, source_target_pairs={{0,2},{1,3},{2,0},{3,1},{4,6},{5,7},{6,4},{7,5},{8,10},{9,11},{10,... | collective-permute-start | bytes 786440 | tf_op jit(solution)/shard_map/ppermute | solution.py:126
  144.2 10.0 %collective-permute-start.17 = (bf16[2,128,512]{2,1,0:T(8,128)(2,1)S(1)}, bf16[2,128,512]{2,1,0:T(8,128)(2,1)S(1)}, u32[]{:S(2)}, u32[]{:S(2)}) collective-permute-start(bf16[2,128,512]{2,1,0:T(8,128)(2,1)S(1)} %pad_maximum_fusion.3), channel_id=1, source_target_pairs={{0,2},{1,3},{2,0},{3,1},{4,6},{5,7},{6,4},{7,5},{8,10},{9,11},{10,... | collective-permute-start | bytes 786440 | tf_op jit(solution)/shard_map/ppermute | solution.py:126
  161.7 11.4 %collective-permute-start.18 = (bf16[2,512,256]{2,1,0:T(8,128)(2,1)S(1)}, bf16[2,512,256]{2,1,0:T(8,128)(2,1)S(1)}, u32[]{:S(2)}, u32[]{:S(2)}) collective-permute-start(bf16[2,512,256]{2,1,0:T(8,128)(2,1)S(1)} %dynamic-slice_bitcast_fusion.3), channel_id=1, source_target_pairs={{0,8},{8,0},{16,24},{24,16},{1,9},{9,1},{17,25},{25,17},{2,10},{10... | collective-permute-start | bytes 1572872 | tf_op jit(solution)/shard_map/ppermute | solution.py:23
  163.0 12.3 %collective-permute-start.20 = (bf16[2,512,256]{2,1,0:T(8,128)(2,1)S(1)}, bf16[2,512,256]{2,1,0:T(8,128)(2,1)S(1)}, u32[]{:S(2)}, u32[]{:S(2)}) collective-permute-start(bf16[2,512,256]{2,1,0:T(8,128)(2,1)S(1)} %dynamic-slice_bitcast_fusion.2), channel_id=1, source_target_pairs={{0,16},{8,24},{16,0},{24,8},{1,17},{9,25},{17,1},{25,9},{2,18},{10... | collective-permute-start | bytes 1572872 | tf_op jit(solution)/shard_map/ppermute | solution.py:23
  173.2 6.4 %collective-permute-start.19 = (bf16[512,256]{1,0:T(8,128)(2,1)S(1)}, bf16[512,256]{1,0:T(8,128)(2,1)S(1)}, u32[]{:S(2)}, u32[]{:S(2)}) collective-permute-start(bf16[512,256]{1,0:T(8,128)(2,1)S(1)} %dynamic-slice_bitcast_fusion.11), channel_id=1, source_target_pairs={{0,16},{8,24},{16,0},{24,8},{1,17},{9,25},{17,1},{25,9},{2,18},{10... | collective-permute-start | bytes 786440 | tf_op jit(solution)/shard_map/ppermute | solution.py:23
  175.5 8.3 %collective-permute-start.21 = (bf16[512,256]{1,0:T(8,128)(2,1)S(1)}, bf16[512,256]{1,0:T(8,128)(2,1)S(1)}, u32[]{:S(2)}, u32[]{:S(2)}) collective-permute-start(bf16[512,256]{1,0:T(8,128)(2,1)S(1)} %dynamic-slice_bitcast_fusion.10), channel_id=1, source_target_pairs={{0,8},{8,0},{16,24},{24,16},{1,9},{9,1},{17,25},{25,17},{2,10},{10... | collective-permute-start | bytes 786440 | tf_op jit(solution)/shard_map/ppermute | solution.py:23
  184.1 14.9 %collective-permute-start.22 = (bf16[2,512,256]{2,1,0:T(8,128)(2,1)S(1)}, bf16[2,512,256]{2,1,0:T(8,128)(2,1)S(1)}, u32[]{:S(2)}, u32[]{:S(2)}) collective-permute-start(bf16[2,512,256]{2,1,0:T(8,128)(2,1)S(1)} %dynamic-slice_bitcast_fusion.1), channel_id=1, source_target_pairs={{0,8},{8,0},{16,24},{24,16},{1,9},{9,1},{17,25},{25,17},{2,10},{10... | collective-permute-start | bytes 1572872 | tf_op jit(solution)/shard_map/ppermute | solution.py:23
  185.4 16.7 %collective-permute-start.24 = (bf16[2,512,256]{2,1,0:T(8,128)(2,1)S(1)}, bf16[2,512,256]{2,1,0:T(8,128)(2,1)S(1)}, u32[]{:S(2)}, u32[]{:S(2)}) collective-permute-start(bf16[2,512,256]{2,1,0:T(8,128)(2,1)S(1)} %dynamic-slice_bitcast_fusion), channel_id=1, source_target_pairs={{0,16},{8,24},{16,0},{24,8},{1,17},{9,25},{17,1},{25,9},{2,18},{10... | collective-permute-start | bytes 1572872 | tf_op jit(solution)/shard_map/ppermute | solution.py:23
  188.1 22.2 %collective-permute-start.26 = (bf16[1024,256]{1,0:T(8,128)(2,1)S(1)}, bf16[1024,256]{1,0:T(8,128)(2,1)S(1)}, u32[]{:S(2)}, u32[]{:S(2)}) collective-permute-start(bf16[1024,256]{1,0:T(8,128)(2,1)S(1)} %get-tuple-element.22), channel_id=1, source_target_pairs={{0,8},{8,0},{16,24},{24,16},{1,9},{9,1},{17,25},{25,17},{2,10},{10... | collective-permute-start | bytes 1572872 | tf_op jit(solution)/shard_map/ppermute | solution.py:23
  190.2 22.9 %collective-permute-start.27 = (bf16[1024,256]{1,0:T(8,128)(2,1)S(1)}, bf16[1024,256]{1,0:T(8,128)(2,1)S(1)}, u32[]{:S(2)}, u32[]{:S(2)}) collective-permute-start(bf16[1024,256]{1,0:T(8,128)(2,1)S(1)} %get-tuple-element.22), channel_id=1, source_target_pairs={{0,16},{8,24},{16,0},{24,8},{1,17},{9,25},{17,1},{25,9},{2,18},{10... | collective-permute-start | bytes 1572872 | tf_op jit(solution)/shard_map/ppermute | solution.py:23
  199.2 14.5 %collective-permute-start.23 = (bf16[512,256]{1,0:T(8,128)(2,1)S(1)}, bf16[512,256]{1,0:T(8,128)(2,1)S(1)}, u32[]{:S(2)}, u32[]{:S(2)}) collective-permute-start(bf16[512,256]{1,0:T(8,128)(2,1)S(1)} %dynamic-slice_bitcast_fusion.9), channel_id=1, source_target_pairs={{0,16},{8,24},{16,0},{24,8},{1,17},{9,25},{17,1},{25,9},{2,18},{10... | collective-permute-start | bytes 786440 | tf_op jit(solution)/shard_map/ppermute | solution.py:23
  202.3 13.6 %collective-permute-start.25 = (bf16[512,256]{1,0:T(8,128)(2,1)S(1)}, bf16[512,256]{1,0:T(8,128)(2,1)S(1)}, u32[]{:S(2)}, u32[]{:S(2)}) collective-permute-start(bf16[512,256]{1,0:T(8,128)(2,1)S(1)} %dynamic-slice_bitcast_fusion.8), channel_id=1, source_target_pairs={{0,8},{8,0},{16,24},{24,16},{1,9},{9,1},{17,25},{25,17},{2,10},{10... | collective-permute-start | bytes 786440 | tf_op jit(solution)/shard_map/ppermute | solution.py:23
  210.3 10.3 %collective-permute-start.28 = (bf16[512,256]{1,0:T(8,128)(2,1)S(1)}, bf16[512,256]{1,0:T(8,128)(2,1)S(1)}, u32[]{:S(2)}, u32[]{:S(2)}) collective-permute-start(bf16[512,256]{1,0:T(8,128)(2,1)S(1)} %slice.125), channel_id=1, source_target_pairs={{0,16},{8,24},{16,0},{24,8},{1,17},{9,25},{17,1},{25,9},{2,18},{10... | collective-permute-start | bytes 786440 | tf_op jit(solution)/shard_map/ppermute | solution.py:23
  213.1 8.1 %collective-permute-start.29 = (bf16[512,256]{1,0:T(8,128)(2,1)S(1)}, bf16[512,256]{1,0:T(8,128)(2,1)S(1)}, u32[]{:S(2)}, u32[]{:S(2)}) collective-permute-start(bf16[512,256]{1,0:T(8,128)(2,1)S(1)} %slice.126), channel_id=1, source_target_pairs={{0,8},{8,0},{16,24},{24,16},{1,9},{9,1},{17,25},{25,17},{2,10},{10... | collective-permute-start | bytes 786440 | tf_op jit(solution)/shard_map/ppermute | solution.py:23
  217.9 19.5 %collective-permute-start.34 = (bf16[1024,256]{1,0:T(8,128)(2,1)}, bf16[1024,256]{1,0:T(8,128)(2,1)}, u32[]{:S(2)}, u32[]{:S(2)}) collective-permute-start(bf16[1024,256]{1,0:T(8,128)(2,1)} %get-tuple-element.20), channel_id=1, source_target_pairs={{0,8},{8,0},{16,24},{24,16},{1,9},{9,1},{17,25},{25,17},{2,10},{10... | collective-permute-start | bytes 1572872 | tf_op jit(solution)/shard_map/ppermute | solution.py:23
  219.0 21.2 %collective-permute-start.35 = (bf16[1024,256]{1,0:T(8,128)(2,1)}, bf16[1024,256]{1,0:T(8,128)(2,1)}, u32[]{:S(2)}, u32[]{:S(2)}) collective-permute-start(bf16[1024,256]{1,0:T(8,128)(2,1)} %get-tuple-element.20), channel_id=1, source_target_pairs={{0,16},{8,24},{16,0},{24,8},{1,17},{9,25},{17,1},{25,9},{2,18},{10... | collective-permute-start | bytes 1572872 | tf_op jit(solution)/shard_map/ppermute | solution.py:23
  226.5 30.0 %all-to-all-start = ((bf16[8,128,1,256]{1,3,2,0:T(8,128)(2,1)}), bf16[8,128,1,256]{1,3,2,0:T(8,128)(2,1)}, u32[]{:S(2)}, u32[]{:S(2)}) async-start(bf16[8,128,1,256]{1,3,2,0:T(8,128)(2,1)} %copy.40), calls=%async_computation | async-start | bytes 1048576 | tf_op jit(solution)/shard_map/all_to_all | solution.py:164
  238.4 8.8 %collective-permute-start.36 = (bf16[512,256]{1,0:T(8,128)(2,1)S(1)}, bf16[512,256]{1,0:T(8,128)(2,1)S(1)}, u32[]{:S(2)}, u32[]{:S(2)}) collective-permute-start(bf16[512,256]{1,0:T(8,128)(2,1)S(1)} %slice.130), channel_id=1, source_target_pairs={{0,16},{8,24},{16,0},{24,8},{1,17},{9,25},{17,1},{25,9},{2,18},{10... | collective-permute-start | bytes 786440 | tf_op jit(solution)/shard_map/ppermute | solution.py:23
  241.2 8.5 %collective-permute-start.37 = (bf16[512,256]{1,0:T(8,128)(2,1)S(1)}, bf16[512,256]{1,0:T(8,128)(2,1)S(1)}, u32[]{:S(2)}, u32[]{:S(2)}) collective-permute-start(bf16[512,256]{1,0:T(8,128)(2,1)S(1)} %slice.131), channel_id=1, source_target_pairs={{0,8},{8,0},{16,24},{24,16},{1,9},{9,1},{17,25},{25,17},{2,10},{10... | collective-permute-start | bytes 786440 | tf_op jit(solution)/shard_map/ppermute | solution.py:23
  256.5 25.3 %all-to-all-start.1 = ((bf16[8,128,1,256]{1,3,2,0:T(8,128)(2,1)}), bf16[8,128,1,256]{1,3,2,0:T(8,128)(2,1)S(1)}, u32[]{:S(2)}, u32[]{:S(2)}) async-start(bf16[8,128,1,256]{1,3,2,0:T(8,128)(2,1)} %copy.45), calls=%async_computation.1 | async-start | bytes 1048576 | tf_op jit(solution)/shard_map/all_to_all | solution.py:164
  261.2 14.5 %collective-permute-start.31 = (bf16[128,2048]{0,1:T(8,128)(2,1)}, bf16[128,2048]{0,1:T(8,128)(2,1)S(1)}, u32[]{:S(2)}, u32[]{:S(2)}) collective-permute-start(bf16[128,2048]{0,1:T(8,128)(2,1)} %bitcast.79), channel_id=1, source_target_pairs={{0,16},{8,24},{16,0},{24,8},{1,17},{9,25},{17,1},{25,9},{2,18},{10... | collective-permute-start | bytes 1572872 | tf_op jit(solution)/shard_map/ppermute | solution.py:23
  261.5 15.5 %collective-permute-start.30 = (bf16[128,2048]{0,1:T(8,128)(2,1)}, bf16[128,2048]{0,1:T(8,128)(2,1)}, u32[]{:S(2)}, u32[]{:S(2)}) collective-permute-start(bf16[128,2048]{0,1:T(8,128)(2,1)} %bitcast.79), channel_id=1, source_target_pairs={{0,8},{8,0},{16,24},{24,16},{1,9},{9,1},{17,25},{25,17},{2,10},{10... | collective-permute-start | bytes 1572872 | tf_op jit(solution)/shard_map/ppermute | solution.py:23
  276.7 15.1 %collective-permute-start.33 = (bf16[64,2048]{0,1:T(8,128)(2,1)}, bf16[64,2048]{0,1:T(8,128)(2,1)}, u32[]{:S(2)}, u32[]{:S(2)}) collective-permute-start(bf16[64,2048]{0,1:T(8,128)(2,1)} %slice.128), channel_id=1, source_target_pairs={{0,8},{8,0},{16,24},{24,16},{1,9},{9,1},{17,25},{25,17},{2,10},{10... | collective-permute-start | bytes 786440 | tf_op jit(solution)/shard_map/ppermute | solution.py:23
  277.0 15.2 %collective-permute-start.32 = (bf16[64,2048]{0,1:T(8,128)(2,1)}, bf16[64,2048]{0,1:T(8,128)(2,1)}, u32[]{:S(2)}, u32[]{:S(2)}) collective-permute-start(bf16[64,2048]{0,1:T(8,128)(2,1)} %bitcast.204), channel_id=1, source_target_pairs={{0,16},{8,24},{16,0},{24,8},{1,17},{9,25},{17,1},{25,9},{2,18},{10... | collective-permute-start | bytes 786440 | tf_op jit(solution)/shard_map/ppermute | solution.py:23
  282.8 19.0 %collective-permute-start.38 = (bf16[128,2048]{1,0:T(8,128)(2,1)}, bf16[128,2048]{1,0:T(8,128)(2,1)S(1)}, u32[]{:S(2)}, u32[]{:S(2)}) collective-permute-start(bf16[128,2048]{1,0:T(8,128)(2,1)} %copy.47), channel_id=1, source_target_pairs={{0,8},{8,0},{16,24},{24,16},{1,9},{9,1},{17,25},{25,17},{2,10},{10... | collective-permute-start | bytes 1572872 | tf_op jit(solution)/shard_map/ppermute | solution.py:23
  284.2 18.0 %collective-permute-start.39 = (bf16[128,2048]{1,0:T(8,128)(2,1)}, bf16[128,2048]{1,0:T(8,128)(2,1)}, u32[]{:S(2)}, u32[]{:S(2)}) collective-permute-start(bf16[128,2048]{1,0:T(8,128)(2,1)} %copy.47), channel_id=1, source_target_pairs={{0,16},{8,24},{16,0},{24,8},{1,17},{9,25},{17,1},{25,9},{2,18},{10... | collective-permute-start | bytes 1572872 | tf_op jit(solution)/shard_map/ppermute | solution.py:23
  294.3 15.9 %copy-start.8 = (bf16[4,128,2048]{2,1,0:T(8,128)(2,1)S(1)}, bf16[4,128,2048]{2,1,0:T(8,128)(2,1)}, u32[]{:S(2)}) copy-start(bf16[4,128,2048]{2,1,0:T(8,128)(2,1)} %copy-done.7) | copy-start | bytes 6291460
  301.8 7.3 %collective-permute-start.40 = (bf16[64,2048]{1,0:T(8,128)(2,1)S(1)}, bf16[64,2048]{1,0:T(8,128)(2,1)S(1)}, u32[]{:S(2)}, u32[]{:S(2)}) collective-permute-start(bf16[64,2048]{1,0:T(8,128)(2,1)S(1)} %slice.132), channel_id=1, source_target_pairs={{0,16},{8,24},{16,0},{24,8},{1,17},{9,25},{17,1},{25,9},{2,18},{10... | collective-permute-start | bytes 786440 | tf_op jit(solution)/shard_map/ppermute | solution.py:23
  303.2 7.1 %collective-permute-start.41 = (bf16[64,2048]{1,0:T(8,128)(2,1)S(1)}, bf16[64,2048]{1,0:T(8,128)(2,1)S(1)}, u32[]{:S(2)}, u32[]{:S(2)}) collective-permute-start(bf16[64,2048]{1,0:T(8,128)(2,1)S(1)} %slice.133), channel_id=1, source_target_pairs={{0,8},{8,0},{16,24},{24,16},{1,9},{9,1},{17,25},{25,17},{2,10},{10... | collective-permute-start | bytes 786440 | tf_op jit(solution)/shard_map/ppermute | solution.py:23
  (10 other events, 47.8 us)
Sparse Core Ops, SparseCore 0:
  34.2 97.1 all-gather.4
  155.7 87.0 all-gather.2
